TPU v7x, 32 devices: a whole 2x2x4 slice. The times are simulated.
32 devices in a mesh: img: 4 (over y, core), term: 8 (over z, x).
Axes of the slice: x: 2, y: 2, z: 4, core: 2. Of those that a mesh axis runs over, the one named last changes fastest.
Arguments:
- patches: bfloat16 [16, 256, 1024], P('img', 'term'), may hold values from -6 to 6
- patch_mask: int32 [16, 256], P('img', 'term'), may hold values 0 or 1
- proj_weight: bfloat16 [1024, 30720], P('img', 'term'), may hold values from -0.1875 to 0.1875
- proj_bias: float32 [30720], P('term'), may hold values from -4 to 4
- slab: bfloat16 [2032, 30720], P('img', 'term'), may hold values from 0 to 2
- query_ids: int32 [1024, 32], replicated, may hold values from -1 to 30719, as said below
- term_weights: bfloat16 [1024, 32], replicated, may hold values from 0.25 to 4
Outputs:
- scores: float32 [1024, 2048], P('term', 'img')
Inputs may be any that keep to these rules, and one draw needn't show every extreme that they name: `query_ids`: within a query the non-negative ids are distinct and come before the padding slots; every query has at least 8 real terms and some query fills all 32 slots.
All inputs are finite; a program needn't handle non-finite values. No bound on the sum of `patch_mask` on one device may be relied on, other than what follows from the above.
Results may differ from a plain program's by a relative error of at most 0.0003.
Values may be sent and summed in bfloat16 or wider, within the bound.
No kernel may reach another device: no remote copies, remote signals or barrier semaphores. Data moves between devices by JAX's collectives and lax.ppermute only.
A program may use at most 64 MiB of HBM per device.

v0:
```python
import jax
import jax.numpy as jnp
from jax import lax
from jax.sharding import PartitionSpec as P


def shards(patches, patch_mask, proj_weight, proj_bias, slab, query_ids, term_weights):
    proj_full = lax.all_gather(proj_weight, "img", axis=0, tiled=True)
    block_width = proj_full.shape[1]
    start_max = jnp.zeros((patches.shape[0], block_width), jnp.float32)
    features = lax.all_gather(patches, "term", axis=1, tiled=True)
    keep_mask = lax.all_gather(patch_mask.astype(jnp.bfloat16), "term", axis=1, tiled=True)
    logits = (
        jnp.einsum("npd,dv->npv", features, proj_full, preferred_element_type=jnp.float32)
        + proj_bias
    )
    activity = jnp.log1p(jnp.maximum(logits, 0.0))
    activity = jnp.where(keep_mask[:, :, None] > 0, activity, 0.0)
    pooled = jnp.maximum(start_max, jnp.max(activity, axis=1))
    impacts = jnp.concatenate([slab, pooled.astype(jnp.bfloat16)], axis=0)
    zero_value = jnp.zeros((), jnp.bfloat16)
    weights = jnp.where(query_ids >= 0, term_weights, zero_value)
    regrouped = lax.all_to_all(impacts, "term", split_axis=0, concat_axis=1, tiled=True)
    safe_ids = jnp.maximum(query_ids, 0)
    picked = jnp.take(regrouped, safe_ids, axis=1).astype(jnp.float32)
    local_scores = jnp.sum(picked * weights.astype(jnp.float32)[None], axis=2)
    scores = lax.all_to_all(local_scores.T, "term", split_axis=0, concat_axis=1, tiled=True)
    return scores


def solution(mesh):
    placed = (
        P("img", "term", None),
        P("img", "term"),
        P("img", "term"),
        P("term"),
        P("img", "term"),
        P(),
        P(),
    )
    return jax.shard_map(
        shards, mesh=mesh, in_specs=placed, out_specs=P("term", "img"), check_vma=False
    )
```

profile of v0, /device:TPU:0, one launch (start us, length us, event | category | flops | bytes accessed | tf_op | source)
XLA Modules:
  0.0 383.6 jit_solution(2639687833125226804)
XLA Ops:
  6.5 0.0 all-gather.4.cloned.1.call-start
  6.5 0.7 all-gather.4.cloned.1.call-update
  7.3 0.0 all-gather.6.cloned.1.call-start
  7.3 0.7 all-gather.6.cloned.1.call-update
  8.0 0.7 convert_bitcast_fusion
  8.7 22.2 %all-gather = bf16[8,32,4]{1,2,0:T(4,128)(2,1)S(1)} all-gather(bf16[1,32,4]{1,2,0:T(4,128)(2,1)S(1)} %convert_bitcast_fusion), channel_id=1, replica_groups=mesh['img'=4,'term'=8] {'term'}, dimensions={0}, use_global_device_ids=true | all-gather | bytes 2304 | tf_op jit(solution)/shard_map/all_gather | solution.py:12
  31.0 0.1 reshape.28
  31.0 30.5 %all-gather.4.cloned.1.call-done = bf16[4,256,1024]{2,1,0:T(8,128)(2,1)} async-done(((bf16[4,32,1024]{2,1,0:T(8,128)(2,1)}), bf16[4,256,1024]{2,1,0:T(8,128)(2,1)}) %all-gather.4.cloned.1.call-update) | async-done | bytes 2097168 | tf_op jit(solution)/shard_map/all_gather | solution.py:11
  61.6 55.4 %all-gather.6.cloned.1.call-done = bf16[1024,3840]{1,0:T(8,128)(2,1)} async-done(((bf16[256,3840]{1,0:T(8,128)(2,1)}), bf16[1024,3840]{1,0:T(8,128)(2,1)}) %all-gather.6.cloned.1.call-update) | async-done | bytes 7864336 | tf_op jit(solution)/shard_map/all_gather | solution.py:8
  117.0 0.0 copy-start
  117.0 16.2 %select_reduce_fusion = bf16[4,3840]{1,0:T(4,128)(2,1)S(1)} fusion(f32[3840]{0:T(1024)} %param.10, pred[4,256]{1,0:T(4,128)(4,1)S(1)} %bitcast.26, bf16[4,256,1024]{2,1,0:T(8,128)(2,1)} %all-gather.4.cloned.1.call-done, bf16[1024,3840]{1,0:T(8,128)(2,1)} %all-gather.6.cloned.1.call-done), kind=kOutput, calls=%fused_computation.2 | convolution fusion | flops 8068776960 | bytes 10008576 | tf_op jit(solution)/shard_map/npd,dv->npv/dot_general | solution.py:14
  133.2 0.0 copy-done
  133.2 0.0 copy-start.1
  133.2 0.0 copy-start.2
  133.2 2.2 pad_maximum_fusion
  135.4 5.5 %all-to-all-start = ((bf16[8,64,3840]{2,1,0:T(8,128)(2,1)}), bf16[8,64,3840]{2,1,0:T(8,128)(2,1)}, u32[]{:S(2)}, u32[]{:S(2)}) async-start(bf16[8,64,3840]{2,1,0:T(8,128)(2,1)} %bitcast.23), calls=%async_computation | async-start | bytes 7864320 | tf_op jit(solution)/shard_map/all_to_all | solution.py:23
  140.9 0.0 copy-done.1
  140.9 0.2 copy.21
  141.1 0.2 reshape.17
  141.3 0.0 copy-done.2
  141.3 0.2 copy.22
  141.6 0.3 copy.18
  141.9 87.1 %all-to-all-done = bf16[8,64,3840]{2,1,0:T(8,128)(2,1)} async-done(((bf16[8,64,3840]{2,1,0:T(8,128)(2,1)}), bf16[8,64,3840]{2,1,0:T(8,128)(2,1)}, u32[]{:S(2)}, u32[]{:S(2)}) %all-to-all-start) | async-done | bytes 3932192 | tf_op jit(solution)/shard_map/all_to_all | solution.py:23
  229.0 8.3 %copy.20 = bf16[64,8,3840]{0,2,1:T(8,128)(2,1)} copy(bf16[64,8,3840]{2,0,1:T(8,128)(2,1)} %bitcast.5) | data formatting | bytes 7864320 | tf_op jit(solution)/shard_map/all_to_all | solution.py:23
  237.3 113.6 %gather_fusion = bf16[32768,64]{1,0:T(8,128)(2,1)} fusion(bf16[64,30720]{0,1:T(8,128)(2,1)} %bitcast.22, s32[32768]{0:T(1024)S(1)} %broadcast_clamp_fusion), kind=kCustom, calls=%fused_computation | custom fusion | bytes 8519680 | tf_op jit(solution)/shard_map/jit(_take)/gather | solution.py:25
  350.8 12.4 %multiply_reduce_fusion = f32[1024,64]{1,0:T(8,128)S(1)} fusion(f32[1024,32]{1,0:T(8,128)S(1)} %copy.22, pred[1024,32]{1,0:T(8,128)(4,1)S(1)} %copy.18, bf16[32768,64]{1,0:T(8,128)(2,1)} %gather_fusion), kind=kLoop, calls=%fused_computation.1 | loop fusion | flops 8323072 | bytes 4620288 | tf_op jit(solution)/shard_map/reduce_sum | solution.py:26
  363.3 0.2 copy.24
  363.4 12.5 %all_to_all.38 = f32[8,128,64]{1,2,0:T(8,128)S(1)} all-to-all(f32[8,128,64]{1,2,0:T(8,128)S(1)} %copy.24), channel_id=1, replica_groups=mesh['img'=4,'term'=8] {'term'}, dimensions={0} | all-to-all | bytes 524288 | tf_op jit(solution)/shard_map/all_to_all | solution.py:27
  376.0 0.8 copy.25
  (7 shorter events, 0.1 us)
Async XLA Ops:
  6.5 55.0 %all-gather.4.cloned.1.call-start = ((), (), s32[]{:S(2)}) async-start(), calls=%async_computation.2 | async-start | bytes 2359296 | tf_op jit(solution)/shard_map/all_gather | solution.py:11
  7.3 109.7 %all-gather.6.cloned.1.call-start = ((), (), s32[]{:S(2)}) async-start(), calls=%async_computation.3 | async-start | bytes 9830400 | tf_op jit(solution)/shard_map/all_gather | solution.py:8
  117.0 16.2 %copy-start = (bf16[508,3840]{1,0:T(8,128)(2,1)S(1)}, bf16[508,3840]{1,0:T(8,128)(2,1)}, u32[]{:S(2)}) copy-start(bf16[508,3840]{1,0:T(8,128)(2,1)} %param.11) | copy-start | bytes 11704324
  133.2 7.7 %copy-start.1 = (s32[1024,32]{0,1:T(8,128)S(1)}, s32[1024,32]{0,1:T(8,128)}, u32[]{:S(2)}) copy-start(s32[1024,32]{0,1:T(8,128)} %param.12) | copy-start | bytes 393220
  133.2 8.1 %copy-start.2 = (bf16[1024,32]{0,1:T(8,128)(2,1)S(1)}, bf16[1024,32]{0,1:T(8,128)(2,1)}, u32[]{:S(2)}) copy-start(bf16[1024,32]{0,1:T(8,128)(2,1)} %param.13) | copy-start | bytes 196612
  135.4 93.6 %all-to-all-start = ((bf16[8,64,3840]{2,1,0:T(8,128)(2,1)}), bf16[8,64,3840]{2,1,0:T(8,128)(2,1)}, u32[]{:S(2)}, u32[]{:S(2)}) async-start(bf16[8,64,3840]{2,1,0:T(8,128)(2,1)} %bitcast.23), calls=%async_computation | async-start | bytes 7864320 | tf_op jit(solution)/shard_map/all_to_all | solution.py:23
Sparse Core Ops, SparseCore 0:
  9.5 51.9 all-gather.3
  63.1 53.7 all-gather.5
where the time goes:
time: 384 us
  waiting for transfers between devices  174 us (45%)
  local copies, waits for them, and re-layouts  124 us (32%)
  blocking collectives  34.8 us (9%)
  matrix products  16.2 us (4%)
  other arithmetic  15.4 us (4%)
  between operations  13.5 us (4%)
  starting transfers between devices  5.55 us (1%)
    gather x1, local copies, waits for them, and re-layouts, shards(): picked = jnp.take(regrouped, safe_ids, axis=1).astype(jnp.float32)  114 us
    all_to_all x1, waiting for transfers between devices, shards(): lax.all_to_all(impacts, 'term', split_axis=0, concat_axis=1, tiled=True)  87.1 us
    all_gather x1, waiting for transfers between devices, shards(): proj_full = lax.all_gather(proj_weight, 'img', axis=0, tiled=True)  55.4 us
    all_gather x1, waiting for transfers between devices, shards(): features = lax.all_gather(patches, 'term', axis=1, tiled=True)  30.5 us
    all_gather x1, blocking collectives, shards(): lax.all_gather(patch_mask.astype(jnp.bfloat16), 'term', axis=1, tiled=True)  22.2 us
    dot_general x1, matrix products, shards(): jnp.einsum('npd,dv->npv', features, proj_full, preferred_element_type=jnp...  16.2 us
    all_to_all x1, blocking collectives, shards(): lax.all_to_all(local_scores.T, 'term', split_axis=0, concat_axis=1, tiled...  12.5 us
    reduce_sum x1, other arithmetic, shards(): local_scores = jnp.sum(picked * weights.astype(jnp.float32)[None], axis=2)  12.4 us
  transfers between devices with their start and end apart: 3, of which 3 were waited for; matrix products, arithmetic and copies ran while one was open for 0% of the time, Pallas kernels for 0%

commit v1 on v0

v1 whole, which is shorter than its diff:
```python
import functools

import jax
import jax.numpy as jnp
from jax import lax
from jax.experimental import pallas as pl
from jax.experimental.pallas import tpu as pltpu
from jax.sharding import Mesh, PartitionSpec as P

BF16 = jnp.bfloat16
F32 = jnp.float32
LANES = 128
WIDE = 256
GROUP = 8
ROWS_BY_ROWS = (((1,), (1,)), ((), ()))
VMEM_BYTES = 48 << 20


def whole(array):
    return pl.BlockSpec(array.shape, lambda i, *_: (0,) * array.ndim)


def expand_terms(slots, blocks, width, base, ids, weights, out, row):
    query = lax.broadcasted_iota(jnp.int32, (1, GROUP * slots), 1) // slots
    parts = []
    for g in range(2):
        local = ids[pl.ds(2 * row + g, 1), :] - base
        inside = (local >= 0) & (local < width)
        key = jnp.where(inside, (local // WIDE) * GROUP + query, -1)
        rows = lax.broadcasted_iota(jnp.int32, (blocks * GROUP, GROUP * slots), 0)
        coarse = jnp.where(rows == key, weights[pl.ds(2 * row + g, 1), :], 0.0).astype(BF16)
        place = lax.broadcasted_iota(jnp.int32, (WIDE, GROUP * slots), 0)
        fine = jnp.where(place == (local & (WIDE - 1)), 1.0, 0.0).astype(BF16)
        parts.append(
            lax.dot_general(coarse, fine, ROWS_BY_ROWS, preferred_element_type=F32)
        )
    start = pl.multiple_of(row * 2 * GROUP, 2 * GROUP)
    for b in range(blocks):
        pair = [part[b * GROUP : (b + 1) * GROUP] for part in parts]
        out[pl.ds(start, 2 * GROUP), b * WIDE : (b + 1) * WIDE] = jnp.concatenate(
            pair, axis=0
        ).astype(BF16)


def score_kernel(slots, place, ids, weights, slab, dense, *rest):
    *outs, scores = rest
    images, width = slab.shape
    base, z = place[0], place[1]
    blocks = dense.shape[1] // WIDE
    steps = ids.shape[0] // 2

    def step(row, carry):
        expand_terms(slots, blocks, width, base, ids, weights, dense, row)
        return carry

    lax.fori_loop(0, steps, step, 0, unroll=8 if steps % 8 == 0 else 1)
    found = lax.dot_general(
        dense[:, :width], slab[...], ROWS_BY_ROWS, preferred_element_type=F32
    )
    scores[...] = found.reshape(scores.shape)
    for k, out in enumerate(outs):
        out[:, :images] = scores[jnp.bitwise_xor(z, k)]
        out[:, images:] = jnp.zeros((out.shape[0], out.shape[1] - images), F32)


def score_slab(place, ids, weights, slab, slots, depth, images):
    groups = ids.shape[0]
    queries = groups * GROUP
    held, width = slab.shape
    padded = -(-width // WIDE) * WIDE
    rows = queries // depth
    dense = jax.ShapeDtypeStruct((queries, padded), BF16)
    part = jax.ShapeDtypeStruct((rows, images), F32)
    return pl.pallas_call(
        functools.partial(score_kernel, slots),
        grid_spec=pltpu.PrefetchScalarGridSpec(
            num_scalar_prefetch=1,
            grid=(1,),
            in_specs=[whole(ids), whole(weights), whole(slab)],
            out_specs=[whole(dense)] + [whole(part)] * depth,
            scratch_shapes=[pltpu.VMEM((depth, rows, held), F32)],
        ),
        out_shape=[dense] + [part] * depth,
        compiler_params=pltpu.CompilerParams(vmem_limit_bytes=VMEM_BYTES),
        cost_estimate=pl.CostEstimate(
            flops=2 * queries * width * images * 3, bytes_accessed=12 << 20, transcendentals=0
        ),
        name="score_slab",
    )(place, ids, weights, slab)


def project_kernel(pieces, parts, aligned, images, patches, place, *refs):
    own, peer = refs[0], refs[1]
    weights = refs[2 : 2 + pieces]
    bias = refs[2 + pieces]
    dense = refs[3 + pieces : 3 + pieces + parts]
    running, out, gathered, best, wide, arrived = refs[3 + pieces + parts :]
    i = pl.program_id(0)
    steps = pl.num_programs(0) // 2
    depth, columns = weights[0].shape
    index, core, x, offset = place[0], place[1], place[2], place[3]

    def fetch(k):
        source = dense[k]
        if aligned:
            source = source.at[:, pl.ds(pl.multiple_of(offset, LANES), columns)]
        return pltpu.make_async_copy(source, wide.at[k], arrived.at[k])

    @pl.when(i == 0)
    def _():
        for k in range(parts):
            fetch(k).start()
        for k, piece in enumerate(weights):
            at = jnp.bitwise_xor(index, k) * depth
            gathered[pl.ds(pl.multiple_of(at, depth), depth), :] = piece[...]
        best[...] = jnp.full(best.shape, -jnp.inf, F32)

    def pool(block, side):
        logits = jnp.dot(block[...], gathered[...], preferred_element_type=F32)
        real = block[:, 0:1].astype(F32) < jnp.inf
        logits = jnp.where(real, logits, -jnp.inf)
        logits = logits.reshape(-1, images, patches, columns)
        best[side] = jnp.maximum(best[side], jnp.max(jnp.max(logits, axis=2), axis=0))

    @pl.when(i < steps)
    def _():
        pool(own, 0)

    @pl.when(i >= steps)
    def _():
        pool(peer, 1)

    @pl.when(i == 2 * steps - 1)
    def _():
        active = jnp.log1p(jnp.maximum(best[...] + bias[...], 0.0))
        pooled = jnp.concatenate([active[0], active[1]], axis=0).astype(BF16)
        out[...] = running[...]
        depth_z, queries = out.shape[1], out.shape[4]
        for k in range(parts):
            fetch(k).wait()
            found = lax.dot_general(pooled, wide[k], ROWS_BY_ROWS, preferred_element_type=F32)
            at = jnp.bitwise_xor(x, k)
            for z in range(depth_z):
                mine = found[:, z * queries : (z + 1) * queries]
                for side in range(2):
                    spot = (jnp.bitwise_xor(core, side), z, at, slice(0, images))
                    out[spot] = out[spot] + mine[side * images : (side + 1) * images]


def project(place, own, peer, weights, bias, dense, running, aligned, images, patches):
    rows, features = own.shape
    block = 512 if rows % 512 == 0 else rows
    steps = rows // block
    depth, columns = weights[0].shape
    queries = dense[0].shape[0]
    return pl.pallas_call(
        functools.partial(
            project_kernel, len(weights), len(dense), aligned, images, patches
        ),
        grid_spec=pltpu.PrefetchScalarGridSpec(
            num_scalar_prefetch=1,
            grid=(2 * steps,),
            in_specs=[
                pl.BlockSpec((block, features), lambda i, s: (jnp.minimum(i, steps - 1), 0)),
                pl.BlockSpec((block, features), lambda i, s: (jnp.maximum(i - steps, 0), 0)),
            ]
            + [whole(w) for w in weights]
            + [whole(bias)]
            + [pl.BlockSpec(memory_space=pl.ANY)] * len(dense)
            + [whole(running)],
            out_specs=whole(running),
            scratch_shapes=[
                pltpu.VMEM((features, columns), BF16),
                pltpu.VMEM((2, images, columns), F32),
                pltpu.VMEM((len(dense), queries, columns), BF16),
                pltpu.SemaphoreType.DMA((len(dense),)),
            ],
        ),
        out_shape=jax.ShapeDtypeStruct(running.shape, F32),
        compiler_params=pltpu.CompilerParams(vmem_limit_bytes=VMEM_BYTES),
        cost_estimate=pl.CostEstimate(
            flops=4 * rows * features * columns, bytes_accessed=8 << 20, transcendentals=0
        ),
        name="project",
    )(place, own, peer, *weights, bias, *dense, running)


def column_blocks(width):
    if width % LANES or width < 4 * LANES:
        return [(0, width)]
    tiles = width // LANES
    sizes, left = [], tiles
    for share in (3, 2, 2):
        take = max(1, left // share) if left > 1 else left
        if take:
            sizes.append(take)
            left -= take
    if left:
        sizes.append(left)
    sizes.sort(reverse=True)
    blocks, start = [], 0
    for size in sizes:
        blocks.append((start * LANES, size * LANES))
        start += size
    return blocks


def shards(rows, terms, patches, patch_mask, proj_weight, proj_bias, slab, query_ids, term_weights):
    along_x = 1
    while along_x * along_x * 4 <= terms:
        along_x *= 2
    along_z = terms // along_x
    row, core, term = lax.axis_index("row"), lax.axis_index("core"), lax.axis_index("term")
    x, z = term % along_x, term // along_x
    images, patch_rows, features = patches.shape
    depth, width = proj_weight.shape
    held = slab.shape[0]
    slots = query_ids.shape[1]
    block_queries = query_ids.shape[0] // terms

    def to_term(value, k):
        return lax.ppermute(value, "term", [(i, i ^ k) for i in range(terms)])

    def to_row(value, k, flip):
        return lax.ppermute(
            value, ("row", "core"), [(i, i ^ (2 * k + flip)) for i in range(2 * rows)]
        )

    half = width // 2
    blocks = column_blocks(half)
    pieces = []
    for start, size in blocks:
        mine = lax.dynamic_slice(proj_weight, (0, core * half + start), (depth, size))
        other = lax.dynamic_slice(proj_weight, (0, (1 - core) * half + start), (depth, size))
        got = [mine]
        for k in range(1, 2 * rows):
            got.append(to_row(other if k % 2 else mine, k // 2, k % 2))
        pieces.append(got)

    marked = jnp.where(patch_mask[:, :, None] > 0, patches, jnp.array(jnp.inf, BF16))
    columns_z = [marked] + [to_term(marked, k * along_x) for k in range(1, along_z)]
    everything = list(columns_z)
    for k in range(1, along_x):
        everything += [to_term(block, k) for block in columns_z]
    own = jnp.stack(everything).reshape(terms * images * patch_rows, features)
    peer = to_row(own, 0, 1)

    ids = query_ids.reshape(along_z, along_x, block_queries, slots)
    weights = jnp.where(query_ids >= 0, term_weights, jnp.zeros((), BF16)).astype(F32)
    weights = weights.reshape(ids.shape)
    place = jnp.stack([term * width, z]).astype(jnp.int32)
    dense, summed = [], None
    for k in [*range(1, along_x), 0]:
        picked = [
            lax.dynamic_index_in_dim(a, x ^ k, 1, keepdims=False).reshape(-1, GROUP * slots)
            for a in (ids, weights)
        ]
        full, *parts = score_slab(
            place, *picked, slab, slots, along_z, held + images
        )
        dense.append((k, full))
        if k:
            parts = [to_term(part, k) for part in parts]
        summed = parts if summed is None else [a + b for a, b in zip(summed, parts)]
    dense = [full for _, full in sorted(dense, key=lambda pair: pair[0])]
    stored = summed[0]
    for k in range(1, along_z):
        stored = stored + to_term(summed[k], k * along_x)

    running = jnp.zeros((2, along_z, along_x, 8, block_queries), F32)
    bias = proj_bias.reshape(1, width)
    aligned = half % LANES == 0
    for (start, size), got in zip(blocks, pieces):
        offset = core * half + start
        place = jnp.stack([2 * row + core, core, x, offset]).astype(jnp.int32)
        spans = dense
        if not aligned:
            spans = [lax.dynamic_slice(d, (0, offset), (d.shape[0], size)) for d in dense]
        running = project(
            place, own, peer, got, lax.dynamic_slice(bias, (0, offset), (1, size)),
            spans, running, aligned, images, patch_rows,
        )
    sent = running.reshape(2 * terms, 8, block_queries)
    fresh = lax.all_to_all(sent, ("core", "term"), split_axis=0, concat_axis=0, tiled=True)
    fresh = jnp.sum(fresh, axis=0)[:images].T
    return jnp.concatenate([stored[:, :held], fresh], axis=1)


def solution(mesh):
    groups, terms = mesh.shape["img"], mesh.shape["term"]
    rows = groups // 2
    cores = Mesh(mesh.devices.reshape(rows, 2, terms), ("row", "core", "term"))
    img = ("row", "core")
    placed = (
        P(img, "term", None),
        P(img, "term"),
        P(img, "term"),
        P("term"),
        P(img, "term"),
        P(),
        P(),
    )
    return jax.shard_map(
        functools.partial(shards, rows, terms),
        mesh=cores,
        in_specs=placed,
        out_specs=P("term", img),
        check_vma=False,
    )
```

time: 384 us -> 146 us (0.38)
  waiting for transfers between devices: 174 us -> 40.7 us
  local copies, waits for them, and re-layouts: 124 us -> 17.1 us
  Pallas kernels: 0 us -> 42.8 us
  blocking collectives: 34.8 us -> 0 us
  starting transfers between devices: 5.55 us -> 31.6 us
  matrix products: 16.2 us -> 0 us
  between operations: 13.5 us -> 0.4 us
    gather x1 -> x0, local copies, waits for them, and re-layouts: 114 us -> none  [shards(): picked = jnp.take(regrouped, safe_ids, axis=1).astype(jnp.float32)]
    all_gather x2 -> x0, waiting for transfers between devices: 85.9 us -> none  [the longest x1 55.4 us: shards(): proj_full = lax.all_gather(proj_weight, 'img', axis=0, tiled=True)]
    all_to_all x1, waiting for transfers between devices: 87.1 us -> 5.64 us  [shards(): lax.all_to_all(sent, ('core', 'term'), split_axis=0, concat_axis=0, tiled...]
    pallas_call x0 -> x6, Pallas kernels: none -> 42.8 us  [the longest x4 25 us: project(): pl.pallas_call(functools.partial(project_kernel, len(weights), len(dense)...]
    ppermute x0 -> x27, waiting for transfers between devices: none -> 35.1 us  [the longest x14 22 us: to_term(): return lax.ppermute(value, 'term', [(i, i ^ k) for i in range(terms)])]
    ppermute x0 -> x27, starting transfers between devices: none -> 26.8 us  [the longest x14 20.1 us: to_term(): return lax.ppermute(value, 'term', [(i, i ^ k) for i in range(terms)])]
    all_gather x1 -> x0, blocking collectives: 22.2 us -> none  [shards(): lax.all_gather(patch_mask.astype(jnp.bfloat16), 'term', axis=1, tiled=True)]
    dot_general x1 -> x0, matrix products: 16.2 us -> none  [shards(): jnp.einsum('npd,dv->npv', features, proj_full, preferred_element_type=jnp...]
  transfers between devices with their start and end apart: 3 -> 28, of which waited for: 3 -> 8; matrix products, arithmetic and copies ran while one was open for 0% -> 12% of each run, Pallas kernels for 0% -> 30%
where the time goes in v1:
time: 146 us; the launch traced here: 145 us
  Pallas kernels  42.8 us (29%)
  waiting for transfers between devices  40.7 us (28%)
  starting transfers between devices  31.6 us (22%)
  local copies, waits for them, and re-layouts  17.1 us (12%)
  other arithmetic  12 us (8%)
    pallas_call x4, Pallas kernels, project(): pl.pallas_call(functools.partial(project_kernel, len(weights), len(dense)...  25 us
    ppermute x14, waiting for transfers between devices, to_term(): return lax.ppermute(value, 'term', [(i, i ^ k) for i in range(terms)])  22 us
    ppermute x14, starting transfers between devices, to_term(): return lax.ppermute(value, 'term', [(i, i ^ k) for i in range(terms)])  20.1 us
    pallas_call x2, Pallas kernels, score_slab(): pl.pallas_call(functools.partial(score_kernel, slots), grid_spec=pltpu.Pr...  17.8 us
    ppermute x13, waiting for transfers between devices, to_row(): lax.ppermute(value, ('row', 'core'), [(i, i ^ 2 * k + flip) for i in rang...  13 us
    unnamed x38, local copies, waits for them, and re-layouts  8.53 us
    ppermute x13, starting transfers between devices, to_row(): lax.ppermute(value, ('row', 'core'), [(i, i ^ 2 * k + flip) for i in rang...  6.62 us
    all_to_all x1, waiting for transfers between devices, shards(): lax.all_to_all(sent, ('core', 'term'), split_axis=0, concat_axis=0, tiled...  5.64 us
  transfers between devices with their start and end apart: 28, of which 8 were waited for; matrix products, arithmetic and copies ran while one was open for 12% of the time, Pallas kernels for 30%

profile of v1, /device:TPU:0, one launch (start us, length us, event | category | flops | bytes accessed | tf_op | source)
XLA Modules:
  0.0 144.7 jit_solution(7497542723223272977)
XLA Ops:
  0.7 1.8 %bitcast_dynamic-update-slice_fusion.7 = (bf16[8,4,32,1024]{3,2,1,0:T(8,128)(2,1)S(1)}, bf16[4,32,1024]{2,1,0:T(8,128)(2,1)}) fusion(bf16[4,32,1024]{2,1,0:T(8,128)(2,1)} %param.7, pred[4,32]{1,0:T(4,128)(4,1)S(1)} %broadcast_compare_fusion), kind=kLoop, calls=%fused_computation.12 | loop fusion | flops 131071 | bytes 786560
  2.5 3.0 %collective-permute-start.7 = (bf16[4,32,1024]{2,1,0:T(8,128)(2,1)}, bf16[4,32,1024]{2,1,0:T(8,128)(2,1)S(1)}, u32[]{:S(2)}, u32[]{:S(2)}) collective-permute-start(bf16[4,32,1024]{2,1,0:T(8,128)(2,1)} %get-tuple-element.28), channel_id=1, source_target_pairs={{0,2},{1,3},{2,0},{3,1},{4,6},{5,7},{6,4},{7,5},{8,10},{9,11},{10,... | collective-permute-start | bytes 786440 | tf_op jit(solution)/shard_map/ppermute | solution.py:222
  5.5 2.6 %collective-permute-start.8 = (bf16[4,32,1024]{2,1,0:T(8,128)(2,1)}, bf16[4,32,1024]{2,1,0:T(8,128)(2,1)S(1)}, u32[]{:S(2)}, u32[]{:S(2)}) collective-permute-start(bf16[4,32,1024]{2,1,0:T(8,128)(2,1)} %get-tuple-element.28), channel_id=1, source_target_pairs={{0,4},{1,5},{2,6},{3,7},{4,0},{5,1},{6,2},{7,3},{8,12},{9,13},{10,... | collective-permute-start | bytes 786440 | tf_op jit(solution)/shard_map/ppermute | solution.py:222
  8.1 1.7 %collective-permute-start.10 = (bf16[4,32,1024]{2,1,0:T(8,128)(2,1)}, bf16[4,32,1024]{2,1,0:T(8,128)(2,1)S(1)}, u32[]{:S(2)}, u32[]{:S(2)}) collective-permute-start(bf16[4,32,1024]{2,1,0:T(8,128)(2,1)} %get-tuple-element.28), channel_id=1, source_target_pairs={{0,1},{1,0},{2,3},{3,2},{4,5},{5,4},{6,7},{7,6},{8,9},{9,8},{10,11... | collective-permute-start | bytes 786440 | tf_op jit(solution)/shard_map/ppermute | solution.py:222
  9.8 1.0 fusion
  11.0 1.0 reshape.38
  12.0 4.8 %collective-permute-done.7 = bf16[4,32,1024]{2,1,0:T(8,128)(2,1)S(1)} collective-permute-done((bf16[4,32,1024]{2,1,0:T(8,128)(2,1)}, bf16[4,32,1024]{2,1,0:T(8,128)(2,1)S(1)}, u32[]{:S(2)}, u32[]{:S(2)}) %collective-permute-start.7) | collective-permute-done | bytes 262176 | tf_op jit(solution)/shard_map/ppermute | solution.py:222
  16.8 1.7 %collective-permute-start.11 = (bf16[4,32,1024]{2,1,0:T(8,128)(2,1)S(1)}, bf16[4,32,1024]{2,1,0:T(8,128)(2,1)S(1)}, u32[]{:S(2)}, u32[]{:S(2)}) collective-permute-start(bf16[4,32,1024]{2,1,0:T(8,128)(2,1)S(1)} %collective-permute-done.7), channel_id=1, source_target_pairs={{0,1},{1,0},{2,3},{3,2},{4,5},{5,4},{6,7},{7,6},{8,9},{9,8},{10,11... | collective-permute-start | bytes 786440 | tf_op jit(solution)/shard_map/ppermute | solution.py:222
  18.5 8.5 %collective-permute-done.8 = bf16[4,32,1024]{2,1,0:T(8,128)(2,1)S(1)} collective-permute-done((bf16[4,32,1024]{2,1,0:T(8,128)(2,1)}, bf16[4,32,1024]{2,1,0:T(8,128)(2,1)S(1)}, u32[]{:S(2)}, u32[]{:S(2)}) %collective-permute-start.8) | collective-permute-done | bytes 262176 | tf_op jit(solution)/shard_map/ppermute | solution.py:222
  27.1 1.5 %collective-permute-start.12 = (bf16[4,32,1024]{2,1,0:T(8,128)(2,1)S(1)}, bf16[4,32,1024]{2,1,0:T(8,128)(2,1)S(1)}, u32[]{:S(2)}, u32[]{:S(2)}) collective-permute-start(bf16[4,32,1024]{2,1,0:T(8,128)(2,1)S(1)} %collective-permute-done.8), channel_id=1, source_target_pairs={{0,1},{1,0},{2,3},{3,2},{4,5},{5,4},{6,7},{7,6},{8,9},{9,8},{10,11... | collective-permute-start | bytes 786440 | tf_op jit(solution)/shard_map/ppermute | solution.py:222
  29.3 4.2 %collective-permute-done.12 = bf16[4,32,1024]{2,1,0:T(8,128)(2,1)S(1)} collective-permute-done((bf16[4,32,1024]{2,1,0:T(8,128)(2,1)S(1)}, bf16[4,32,1024]{2,1,0:T(8,128)(2,1)S(1)}, u32[]{:S(2)}, u32[]{:S(2)}) %collective-permute-start.12) | collective-permute-done | bytes 262176 | tf_op jit(solution)/shard_map/ppermute | solution.py:222
  33.4 2.8 %collective-permute-done.13 = bf16[4,32,1024]{2,1,0:T(8,128)(2,1)S(1)} collective-permute-done((bf16[4,32,1024]{2,1,0:T(8,128)(2,1)S(1)}, bf16[4,32,1024]{2,1,0:T(8,128)(2,1)S(1)}, u32[]{:S(2)}, u32[]{:S(2)}) %collective-permute-start.13) | collective-permute-done | bytes 262176 | tf_op jit(solution)/shard_map/ppermute | solution.py:222
  37.1 9.3 %score_slab.2 = (bf16[512,3840]{1,0:T(8,128)(2,1)S(1)}, f32[128,512]{1,0:T(8,128)}, f32[128,512]{1,0:T(8,128)S(1)}, f32[128,512]{1,0:T(8,128)}, f32[128,512]{1,0:T(8,128)}) custom-call(s32[2]{0:T(128)S(1)} %pad_add_fusion.place, s32[64,256]{1,0:T(8,128)S(1)} %reshape.39.ids, f32[64,256]{1,0:T(8,128)S(1)} %reshape.42.weights, bf16[508,3840]{1,0:T(8,128)(2,1)} %slab.3), custom_call_target="tpu_custom_call" | custom-call | flops 6039797760 | bytes 12582912 | tf_op jit(solution)/shard_map/score_slab/pallas_call | solution.py:74
  46.4 1.9 %copy-done = bf16[512,3840]{1,0:T(8,128)(2,1)} copy-done((bf16[512,3840]{1,0:T(8,128)(2,1)}, bf16[512,3840]{1,0:T(8,128)(2,1)S(1)}, u32[]{:S(2)}) %copy-start) | copy-done | bytes 3932184
  48.3 1.5 %collective-permute-start.1 = (f32[128,512]{1,0:T(8,128)S(1)}, f32[128,512]{1,0:T(8,128)}, u32[]{:S(2)}, u32[]{:S(2)}) collective-permute-start(f32[128,512]{1,0:T(8,128)S(1)} %get-tuple-element.17), channel_id=1, source_target_pairs={{0,1},{1,0},{2,3},{3,2},{4,5},{5,4},{6,7},{7,6},{8,9},{9,8},{10,11... | collective-permute-start | bytes 786440 | tf_op jit(solution)/shard_map/ppermute | solution.py:222
  50.3 1.6 %constant_dynamic-slice_fusion.6 = (bf16[256,256]{1,0:T(8,128)(2,1)}, bf16[256,256]{1,0:T(8,128)(2,1)S(1)}) fusion(bf16[256,3840]{1,0:T(8,128)(2,1)} %param.9, s32[]{:T(128)S(6)} %select_n.64, s32[]{:T(128)S(6)} %select_n.63), kind=kLoop, calls=%fused_computation.22 | loop fusion | bytes 524296 | tf_op jit(solution)/shard_map/dynamic_slice | solution.py:234
  52.0 1.5 %collective-permute-start.16 = (bf16[256,256]{1,0:T(8,128)(2,1)S(1)}, bf16[256,256]{1,0:T(8,128)(2,1)S(1)}, u32[]{:S(2)}, u32[]{:S(2)}) collective-permute-start(bf16[256,256]{1,0:T(8,128)(2,1)S(1)} %get-tuple-element.36.refs_2_), channel_id=1, source_target_pairs={{0,16},{8,24},{16,0},{24,8},{1,17},{9,25},{17,1},{25,9},{2,18},{10... | collective-permute-start | bytes 393224 | tf_op jit(solution)/shard_map/ppermute | solution.py:225
  54.1 8.5 %score_slab.3 = (bf16[512,3840]{1,0:T(8,128)(2,1)S(1)}, f32[128,512]{1,0:T(8,128)S(1)}, f32[128,512]{1,0:T(8,128)S(1)}, f32[128,512]{1,0:T(8,128)S(1)}, f32[128,512]{1,0:T(8,128)S(1)}) custom-call(s32[2]{0:T(128)S(1)} %pad_add_fusion.place, s32[64,256]{1,0:T(8,128)S(1)} %reshape.43.ids, f32[64,256]{1,0:T(8,128)S(1)} %reshape.44.weights, bf16[508,3840]{1,0:T(8,128)(2,1)} %slab.3), custom_call_target="tpu_custom_call" | custom-call | flops 6039797760 | bytes 12582912 | tf_op jit(solution)/shard_map/score_slab/pallas_call | solution.py:74
  62.6 1.9 %copy-done.1 = bf16[512,3840]{1,0:T(8,128)(2,1)} copy-done((bf16[512,3840]{1,0:T(8,128)(2,1)}, bf16[512,3840]{1,0:T(8,128)(2,1)S(1)}, u32[]{:S(2)}) %copy-start.1) | copy-done | bytes 3932184
  64.5 0.7 copy-done.2
  65.2 0.7 copy-done.4
  65.9 0.7 copy-done.5
  66.6 0.7 copy-done.6
  67.4 2.2 %constant_dynamic-slice_fusion = (bf16[256,640]{1,0:T(8,128)(2,1)}, bf16[256,640]{1,0:T(8,128)(2,1)}, bf16[256,640]{1,0:T(8,128)(2,1)S(1)}, bf16[256,640]{1,0:T(8,128)(2,1)S(1)}) fusion(bf16[256,3840]{1,0:T(8,128)(2,1)} %param.9, s32[]{:T(128)S(6)} %select_n.70, s32[]{:T(128)S(6)} %select_n.68, s32[]{:T(128)S(6)} %select_n.67, s32[]{:T(128)S(6)} %select_n.69), kind=kLoop, calls=%fused_computation.16 | loop fusion | bytes 2621456 | tf_op jit(solution)/shard_map/dynamic_slice | solution.py:234
  70.3 1.5 %collective-permute-start.5 = (f32[128,512]{1,0:T(8,128)}, f32[128,512]{1,0:T(8,128)}, u32[]{:S(2)}, u32[]{:S(2)}) collective-permute-start(f32[128,512]{1,0:T(8,128)} %get-tuple-element.21), channel_id=1, source_target_pairs={{0,1},{1,0},{2,3},{3,2},{4,5},{5,4},{6,7},{7,6},{8,9},{9,8},{10,11... | collective-permute-start | bytes 786440 | tf_op jit(solution)/shard_map/ppermute | solution.py:222
  73.6 0.8 dynamic-slice.12
  74.4 0.8 dynamic-slice.13
  75.1 1.4 collective-permute-start.26
  76.5 0.8 pad_add_fusion.4
  77.3 1.7 %collective-permute-done.5 = f32[128,512]{1,0:T(8,128)} collective-permute-done((f32[128,512]{1,0:T(8,128)}, f32[128,512]{1,0:T(8,128)}, u32[]{:S(2)}, u32[]{:S(2)}) %collective-permute-start.5) | collective-permute-done | bytes 262176 | tf_op jit(solution)/shard_map/ppermute | solution.py:222
  79.6 3.3 %collective-permute-done.25.refs_4_ = bf16[256,640]{1,0:T(8,128)(2,1)S(1)} collective-permute-done((bf16[256,640]{1,0:T(8,128)(2,1)S(1)}, bf16[256,640]{1,0:T(8,128)(2,1)S(1)}, u32[]{:S(2)}, u32[]{:S(2)}) %collective-permute-start.25) | collective-permute-done | bytes 327712 | tf_op jit(solution)/shard_map/ppermute | solution.py:225
  83.4 1.1 constant_dynamic-slice_fusion.4
  84.5 1.8 %add.107 = f32[128,512]{1,0:T(8,128)} add(f32[128,512]{1,0:T(8,128)} %collective-permute-done.1, f32[128,512]{1,0:T(8,128)} %copy-done.5) | non-fusion elementwise | flops 65536 | bytes 786432 | tf_op jit(solution)/shard_map/add | solution.py:264
  86.3 1.8 %add.109 = f32[128,512]{1,0:T(8,128)} add(f32[128,512]{1,0:T(8,128)} %collective-permute-done.3, f32[128,512]{1,0:T(8,128)} %copy-done.4) | non-fusion elementwise | flops 65536 | bytes 786432 | tf_op jit(solution)/shard_map/add | solution.py:264
  88.0 1.7 %add.111 = f32[128,512]{1,0:T(8,128)} add(f32[128,512]{1,0:T(8,128)} %collective-permute-done.5, f32[128,512]{1,0:T(8,128)S(1)} %copy-done.3) | non-fusion elementwise | flops 65536 | bytes 786432 | tf_op jit(solution)/shard_map/add | solution.py:264
  90.1 1.2 collective-permute-start.19
  91.3 6.8 %project.4.refs_9_ = f32[2,4,2,8,128]{4,3,2,1,0:T(8,128)S(1)} custom-call(s32[4]{0:T(128)S(1)} %copy-done.12, bf16[1024,1024]{1,0:T(8,128)(2,1)S(1)} %bitcast.50, bf16[1024,1024]{1,0:T(8,128)(2,1)} %collective-permute-done.14.refs_1_, bf16[256,640]{1,0:T(8,128)(2,1)S(1)} %get-tuple-element.32.refs_2_, bf16[256,640]{1,0:T(8,128)(2,1)S(1)} %collective-permute-done.24.refs_3_, ...), custom_call_target="tpu_custom_call" | custom-call | flops 2684354560 | bytes 8388608 | tf_op jit(solution)/shard_map/project/pallas_call | solution.py:156
  98.5 9.7 %collective-permute-done.19.refs_4_ = bf16[256,384]{1,0:T(8,128)(2,1)S(1)} collective-permute-done((bf16[256,384]{1,0:T(8,128)(2,1)S(1)}, bf16[256,384]{1,0:T(8,128)(2,1)S(1)}, u32[]{:S(2)}, u32[]{:S(2)}) %collective-permute-start.19) | collective-permute-done | bytes 196640 | tf_op jit(solution)/shard_map/ppermute | solution.py:225
  108.7 2.6 %collective-permute-start.2 = (f32[128,512]{1,0:T(8,128)}, f32[128,512]{1,0:T(8,128)S(1)}, u32[]{:S(2)}, u32[]{:S(2)}) collective-permute-start(f32[128,512]{1,0:T(8,128)} %add.107), channel_id=1, source_target_pairs={{0,2},{1,3},{2,0},{3,1},{4,6},{5,7},{6,4},{7,5},{8,10},{9,11},{10,... | collective-permute-start | bytes 786440 | tf_op jit(solution)/shard_map/ppermute | solution.py:222
  111.3 1.0 collective-permute-start.4
  112.3 1.5 %collective-permute-start.6 = (f32[128,512]{1,0:T(8,128)}, f32[128,512]{1,0:T(8,128)}, u32[]{:S(2)}, u32[]{:S(2)}) collective-permute-start(f32[128,512]{1,0:T(8,128)} %add.111), channel_id=1, source_target_pairs={{0,6},{1,7},{2,4},{3,5},{4,2},{5,3},{6,0},{7,1},{8,14},{9,15},{10,... | collective-permute-start | bytes 786440 | tf_op jit(solution)/shard_map/ppermute | solution.py:222
  113.8 6.8 %project.5.refs_9_ = f32[2,4,2,8,128]{4,3,2,1,0:T(8,128)S(1)} custom-call(s32[4]{0:T(128)S(1)} %get-tuple-element.43.place, bf16[1024,1024]{1,0:T(8,128)(2,1)S(1)} %bitcast.51, bf16[1024,1024]{1,0:T(8,128)(2,1)} %collective-permute-done.14.refs_1_, bf16[256,640]{1,0:T(8,128)(2,1)S(1)} %get-tuple-element.31.refs_2_, ...), custom_call_target="tpu_custom_call" | custom-call | flops 2684354560 | bytes 8388608 | tf_op jit(solution)/shard_map/project/pallas_call | solution.py:156
  120.7 5.8 %project.6.refs_9_ = f32[2,4,2,8,128]{4,3,2,1,0:T(8,128)S(1)} custom-call(s32[4]{0:T(128)S(1)} %get-tuple-element.44.place, bf16[1024,1024]{1,0:T(8,128)(2,1)S(1)} %bitcast.52, bf16[1024,1024]{1,0:T(8,128)(2,1)} %collective-permute-done.14.refs_1_, bf16[256,384]{1,0:T(8,128)(2,1)S(1)} %get-tuple-element.34.refs_2_, ...), custom_call_target="tpu_custom_call" | custom-call | flops 1610612736 | bytes 8388608 | tf_op jit(solution)/shard_map/project/pallas_call | solution.py:156
  126.5 5.5 %project.7 = f32[2,4,2,8,128]{4,3,2,1,0:T(8,128)} custom-call(s32[4]{0:T(128)S(1)} %get-tuple-element.45.place, bf16[1024,1024]{1,0:T(8,128)(2,1)S(1)} %bitcast.53, bf16[1024,1024]{1,0:T(8,128)(2,1)} %collective-permute-done.14.refs_1_, bf16[256,256]{1,0:T(8,128)(2,1)S(1)} %get-tuple-element.36.refs_2_, bf16[256,256]{1,0:T(8,128)(2,1)S(1)} %copy-done.9, ...), custom_call_target="tpu_custom_call" | custom-call | flops 1073741824 | bytes 8388608 | tf_op jit(solution)/shard_map/project/pallas_call | solution.py:156
  132.1 4.9 %all-to-all-start = ((f32[16,8,128]{2,1,0:T(8,128)}), f32[16,8,128]{2,1,0:T(8,128)S(1)}, u32[]{:S(2)}, u32[]{:S(2)}) async-start(f32[16,8,128]{2,1,0:T(8,128)} %bitcast.19), calls=%async_computation | async-start | bytes 131072 | tf_op jit(solution)/shard_map/all_to_all | solution.py:284
  137.0 1.1 slice_add_fusion
  138.1 5.6 %all-to-all-done = f32[16,8,128]{2,1,0:T(8,128)S(1)} async-done(((f32[16,8,128]{2,1,0:T(8,128)}), f32[16,8,128]{2,1,0:T(8,128)S(1)}, u32[]{:S(2)}, u32[]{:S(2)}) %all-to-all-start) | async-done | bytes 65568 | tf_op jit(solution)/shard_map/all_to_all | solution.py:284
  143.9 0.8 pad_maximum_fusion
  (85 shorter events, 8.7 us)
Async XLA Ops:
  2.5 14.4 %collective-permute-start.7 = (bf16[4,32,1024]{2,1,0:T(8,128)(2,1)}, bf16[4,32,1024]{2,1,0:T(8,128)(2,1)S(1)}, u32[]{:S(2)}, u32[]{:S(2)}) collective-permute-start(bf16[4,32,1024]{2,1,0:T(8,128)(2,1)} %get-tuple-element.28), channel_id=1, source_target_pairs={{0,2},{1,3},{2,0},{3,1},{4,6},{5,7},{6,4},{7,5},{8,10},{9,11},{10,... | collective-permute-start | bytes 786440 | tf_op jit(solution)/shard_map/ppermute | solution.py:222
  5.5 21.6 %collective-permute-start.8 = (bf16[4,32,1024]{2,1,0:T(8,128)(2,1)}, bf16[4,32,1024]{2,1,0:T(8,128)(2,1)S(1)}, u32[]{:S(2)}, u32[]{:S(2)}) collective-permute-start(bf16[4,32,1024]{2,1,0:T(8,128)(2,1)} %get-tuple-element.28), channel_id=1, source_target_pairs={{0,4},{1,5},{2,6},{3,7},{4,0},{5,1},{6,2},{7,3},{8,12},{9,13},{10,... | collective-permute-start | bytes 786440 | tf_op jit(solution)/shard_map/ppermute | solution.py:222
  8.1 20.5 %collective-permute-start.9 = (bf16[4,32,1024]{2,1,0:T(8,128)(2,1)}, bf16[4,32,1024]{2,1,0:T(8,128)(2,1)S(1)}, u32[]{:S(2)}, u32[]{:S(2)}) collective-permute-start(bf16[4,32,1024]{2,1,0:T(8,128)(2,1)} %get-tuple-element.28), channel_id=1, source_target_pairs={{0,6},{1,7},{2,4},{3,5},{4,2},{5,3},{6,0},{7,1},{8,14},{9,15},{10,... | collective-permute-start | bytes 786440 | tf_op jit(solution)/shard_map/ppermute | solution.py:222
  8.1 21.1 %collective-permute-start.10 = (bf16[4,32,1024]{2,1,0:T(8,128)(2,1)}, bf16[4,32,1024]{2,1,0:T(8,128)(2,1)S(1)}, u32[]{:S(2)}, u32[]{:S(2)}) collective-permute-start(bf16[4,32,1024]{2,1,0:T(8,128)(2,1)} %get-tuple-element.28), channel_id=1, source_target_pairs={{0,1},{1,0},{2,3},{3,2},{4,5},{5,4},{6,7},{7,6},{8,9},{9,8},{10,11... | collective-permute-start | bytes 786440 | tf_op jit(solution)/shard_map/ppermute | solution.py:222
  16.8 12.4 %collective-permute-start.11 = (bf16[4,32,1024]{2,1,0:T(8,128)(2,1)S(1)}, bf16[4,32,1024]{2,1,0:T(8,128)(2,1)S(1)}, u32[]{:S(2)}, u32[]{:S(2)}) collective-permute-start(bf16[4,32,1024]{2,1,0:T(8,128)(2,1)S(1)} %collective-permute-done.7), channel_id=1, source_target_pairs={{0,1},{1,0},{2,3},{3,2},{4,5},{5,4},{6,7},{7,6},{8,9},{9,8},{10,11... | collective-permute-start | bytes 786440 | tf_op jit(solution)/shard_map/ppermute | solution.py:222
  27.1 6.4 %collective-permute-start.12 = (bf16[4,32,1024]{2,1,0:T(8,128)(2,1)S(1)}, bf16[4,32,1024]{2,1,0:T(8,128)(2,1)S(1)}, u32[]{:S(2)}, u32[]{:S(2)}) collective-permute-start(bf16[4,32,1024]{2,1,0:T(8,128)(2,1)S(1)} %collective-permute-done.8), channel_id=1, source_target_pairs={{0,1},{1,0},{2,3},{3,2},{4,5},{5,4},{6,7},{7,6},{8,9},{9,8},{10,11... | collective-permute-start | bytes 786440 | tf_op jit(solution)/shard_map/ppermute | solution.py:222
  28.6 7.7 %collective-permute-start.13 = (bf16[4,32,1024]{2,1,0:T(8,128)(2,1)S(1)}, bf16[4,32,1024]{2,1,0:T(8,128)(2,1)S(1)}, u32[]{:S(2)}, u32[]{:S(2)}) collective-permute-start(bf16[4,32,1024]{2,1,0:T(8,128)(2,1)S(1)} %collective-permute-done.9), channel_id=1, source_target_pairs={{0,1},{1,0},{2,3},{3,2},{4,5},{5,4},{6,7},{7,6},{8,9},{9,8},{10,11... | collective-permute-start | bytes 786440 | tf_op jit(solution)/shard_map/ppermute | solution.py:222
  36.3 53.8 %collective-permute-start.14 = (bf16[1024,1024]{1,0:T(8,128)(2,1)S(1)}, bf16[1024,1024]{1,0:T(8,128)(2,1)}, u32[]{:S(2)}, u32[]{:S(2)}) collective-permute-start(bf16[1024,1024]{1,0:T(8,128)(2,1)S(1)} %bitcast.49), channel_id=1, source_target_pairs={{0,8},{8,0},{16,24},{24,16},{1,9},{9,1},{17,25},{25,17},{2,10},{10... | collective-permute-start | bytes 6291464 | tf_op jit(solution)/shard_map/ppermute | solution.py:225
  46.4 1.9 %copy-start = (bf16[512,3840]{1,0:T(8,128)(2,1)}, bf16[512,3840]{1,0:T(8,128)(2,1)S(1)}, u32[]{:S(2)}) copy-start(bf16[512,3840]{1,0:T(8,128)(2,1)S(1)} %get-tuple-element.24.refs_8_) | copy-start | bytes 11796484
  48.3 24.1 %collective-permute-start.1 = (f32[128,512]{1,0:T(8,128)S(1)}, f32[128,512]{1,0:T(8,128)}, u32[]{:S(2)}, u32[]{:S(2)}) collective-permute-start(f32[128,512]{1,0:T(8,128)S(1)} %get-tuple-element.17), channel_id=1, source_target_pairs={{0,1},{1,0},{2,3},{3,2},{4,5},{5,4},{6,7},{7,6},{8,9},{9,8},{10,11... | collective-permute-start | bytes 786440 | tf_op jit(solution)/shard_map/ppermute | solution.py:222
  49.8 25.3 %collective-permute-start.3 = (f32[128,512]{1,0:T(8,128)}, f32[128,512]{1,0:T(8,128)}, u32[]{:S(2)}, u32[]{:S(2)}) collective-permute-start(f32[128,512]{1,0:T(8,128)} %get-tuple-element.19), channel_id=1, source_target_pairs={{0,1},{1,0},{2,3},{3,2},{4,5},{5,4},{6,7},{7,6},{8,9},{9,8},{10,11... | collective-permute-start | bytes 786440 | tf_op jit(solution)/shard_map/ppermute | solution.py:222
  52.0 17.6 %collective-permute-start.15 = (bf16[256,256]{1,0:T(8,128)(2,1)}, bf16[256,256]{1,0:T(8,128)(2,1)S(1)}, u32[]{:S(2)}, u32[]{:S(2)}) collective-permute-start(bf16[256,256]{1,0:T(8,128)(2,1)} %get-tuple-element.35), channel_id=1, source_target_pairs={{0,8},{8,0},{16,24},{24,16},{1,9},{9,1},{17,25},{25,17},{2,10},{10... | collective-permute-start | bytes 393224 | tf_op jit(solution)/shard_map/ppermute | solution.py:225
  52.0 19.8 %collective-permute-start.16 = (bf16[256,256]{1,0:T(8,128)(2,1)S(1)}, bf16[256,256]{1,0:T(8,128)(2,1)S(1)}, u32[]{:S(2)}, u32[]{:S(2)}) collective-permute-start(bf16[256,256]{1,0:T(8,128)(2,1)S(1)} %get-tuple-element.36.refs_2_), channel_id=1, source_target_pairs={{0,16},{8,24},{16,0},{24,8},{1,17},{9,25},{17,1},{25,9},{2,18},{10... | collective-permute-start | bytes 393224 | tf_op jit(solution)/shard_map/ppermute | solution.py:225
  54.0 13.3 %copy-start.13 = (f32[3840]{0:T(1024)S(1)}, f32[3840]{0:T(1024)}, u32[]{:S(2)}) copy-start(f32[3840]{0:T(1024)} %param.10) | copy-start | bytes 46084
  62.6 1.9 %copy-start.1 = (bf16[512,3840]{1,0:T(8,128)(2,1)}, bf16[512,3840]{1,0:T(8,128)(2,1)S(1)}, u32[]{:S(2)}) copy-start(bf16[512,3840]{1,0:T(8,128)(2,1)S(1)} %get-tuple-element.23.refs_7_) | copy-start | bytes 11796484
  64.5 0.7 copy-start.2
  65.2 0.7 copy-start.4
  65.9 0.7 copy-start.5
  66.6 0.7 copy-start.6
  69.6 0.6 copy-start.8
  70.3 8.8 %collective-permute-start.5 = (f32[128,512]{1,0:T(8,128)}, f32[128,512]{1,0:T(8,128)}, u32[]{:S(2)}, u32[]{:S(2)}) collective-permute-start(f32[128,512]{1,0:T(8,128)} %get-tuple-element.21), channel_id=1, source_target_pairs={{0,1},{1,0},{2,3},{3,2},{4,5},{5,4},{6,7},{7,6},{8,9},{9,8},{10,11... | collective-permute-start | bytes 786440 | tf_op jit(solution)/shard_map/ppermute | solution.py:222
  71.8 0.6 copy-start.10
  72.4 6.6 %collective-permute-start.24 = (bf16[256,640]{1,0:T(8,128)(2,1)}, bf16[256,640]{1,0:T(8,128)(2,1)S(1)}, u32[]{:S(2)}, u32[]{:S(2)}) collective-permute-start(bf16[256,640]{1,0:T(8,128)(2,1)} %get-tuple-element.29), channel_id=1, source_target_pairs={{0,8},{8,0},{16,24},{24,16},{1,9},{9,1},{17,25},{25,17},{2,10},{10... | collective-permute-start | bytes 983048 | tf_op jit(solution)/shard_map/ppermute | solution.py:225
  72.4 10.5 %collective-permute-start.25 = (bf16[256,640]{1,0:T(8,128)(2,1)S(1)}, bf16[256,640]{1,0:T(8,128)(2,1)S(1)}, u32[]{:S(2)}, u32[]{:S(2)}) collective-permute-start(bf16[256,640]{1,0:T(8,128)(2,1)S(1)} %get-tuple-element.32.refs_2_), channel_id=1, source_target_pairs={{0,16},{8,24},{16,0},{24,8},{1,17},{9,25},{17,1},{25,9},{2,18},{10... | collective-permute-start | bytes 983048 | tf_op jit(solution)/shard_map/ppermute | solution.py:225
  75.1 12.9 %copy-start.3 = (f32[128,512]{1,0:T(8,128)S(1)}, f32[128,512]{1,0:T(8,128)}, u32[]{:S(2)}) copy-start(f32[128,512]{1,0:T(8,128)} %copy-done.2) | copy-start | bytes 786436
  75.1 16.2 %copy-start.12 = (s32[4]{0:T(128)S(1)}, s32[4]{0:T(128)}, u32[]{:S(2)}) copy-start(s32[4]{0:T(128)} %get-tuple-element.25.place) | copy-start | bytes 52
  75.1 14.6 %collective-permute-start.26 = (bf16[256,640]{1,0:T(8,128)(2,1)}, bf16[256,640]{1,0:T(8,128)(2,1)S(1)}, u32[]{:S(2)}, u32[]{:S(2)}) collective-permute-start(bf16[256,640]{1,0:T(8,128)(2,1)} %get-tuple-element.29), channel_id=1, source_target_pairs={{0,24},{8,16},{16,8},{24,0},{1,25},{9,17},{17,9},{25,1},{2,26},{10... | collective-permute-start | bytes 983048 | tf_op jit(solution)/shard_map/ppermute | solution.py:225
  79.0 29.7 %collective-permute-start.21 = (bf16[256,640]{1,0:T(8,128)(2,1)}, bf16[256,640]{1,0:T(8,128)(2,1)S(1)}, u32[]{:S(2)}, u32[]{:S(2)}) collective-permute-start(bf16[256,640]{1,0:T(8,128)(2,1)} %get-tuple-element.30), channel_id=1, source_target_pairs={{0,8},{8,0},{16,24},{24,16},{1,9},{9,1},{17,25},{25,17},{2,10},{10... | collective-permute-start | bytes 983048 | tf_op jit(solution)/shard_map/ppermute | solution.py:225
  79.0 33.3 %collective-permute-start.23 = (bf16[256,640]{1,0:T(8,128)(2,1)}, bf16[256,640]{1,0:T(8,128)(2,1)S(1)}, u32[]{:S(2)}, u32[]{:S(2)}) collective-permute-start(bf16[256,640]{1,0:T(8,128)(2,1)} %get-tuple-element.30), channel_id=1, source_target_pairs={{0,24},{8,16},{16,8},{24,0},{1,25},{9,17},{17,9},{25,1},{2,26},{10... | collective-permute-start | bytes 983048 | tf_op jit(solution)/shard_map/ppermute | solution.py:225
  82.9 28.4 %collective-permute-start.22 = (bf16[256,640]{1,0:T(8,128)(2,1)S(1)}, bf16[256,640]{1,0:T(8,128)(2,1)S(1)}, u32[]{:S(2)}, u32[]{:S(2)}) collective-permute-start(bf16[256,640]{1,0:T(8,128)(2,1)S(1)} %get-tuple-element.31.refs_2_), channel_id=1, source_target_pairs={{0,16},{8,24},{16,0},{24,8},{1,17},{9,25},{17,1},{25,9},{2,18},{10... | collective-permute-start | bytes 983048 | tf_op jit(solution)/shard_map/ppermute | solution.py:225
  89.7 8.4 %collective-permute-start.18 = (bf16[256,384]{1,0:T(8,128)(2,1)S(1)}, bf16[256,384]{1,0:T(8,128)(2,1)S(1)}, u32[]{:S(2)}, u32[]{:S(2)}) collective-permute-start(bf16[256,384]{1,0:T(8,128)(2,1)S(1)} %get-tuple-element.33), channel_id=1, source_target_pairs={{0,8},{8,0},{16,24},{24,16},{1,9},{9,1},{17,25},{25,17},{2,10},{10... | collective-permute-start | bytes 589832 | tf_op jit(solution)/shard_map/ppermute | solution.py:225
  90.1 18.1 %collective-permute-start.19 = (bf16[256,384]{1,0:T(8,128)(2,1)S(1)}, bf16[256,384]{1,0:T(8,128)(2,1)S(1)}, u32[]{:S(2)}, u32[]{:S(2)}) collective-permute-start(bf16[256,384]{1,0:T(8,128)(2,1)S(1)} %get-tuple-element.34.refs_2_), channel_id=1, source_target_pairs={{0,16},{8,24},{16,0},{24,8},{1,17},{9,25},{17,1},{25,9},{2,18},{10... | collective-permute-start | bytes 589832 | tf_op jit(solution)/shard_map/ppermute | solution.py:225
  98.1 22.4 %collective-permute-start.20 = (bf16[256,384]{1,0:T(8,128)(2,1)S(1)}, bf16[256,384]{1,0:T(8,128)(2,1)S(1)}, u32[]{:S(2)}, u32[]{:S(2)}) collective-permute-start(bf16[256,384]{1,0:T(8,128)(2,1)S(1)} %get-tuple-element.33), channel_id=1, source_target_pairs={{0,24},{8,16},{16,8},{24,0},{1,25},{9,17},{17,9},{25,1},{2,26},{10... | collective-permute-start | bytes 589832 | tf_op jit(solution)/shard_map/ppermute | solution.py:225
  108.2 28.8 %collective-permute-start = (f32[128,512]{1,0:T(8,128)}, f32[128,512]{1,0:T(8,128)S(1)}, u32[]{:S(2)}, u32[]{:S(2)}) collective-permute-start(f32[128,512]{1,0:T(8,128)} %get-tuple-element.15), channel_id=1, source_target_pairs={{0,1},{1,0},{2,3},{3,2},{4,5},{5,4},{6,7},{7,6},{8,9},{9,8},{10,11... | collective-permute-start | bytes 786440 | tf_op jit(solution)/shard_map/ppermute | solution.py:222
  108.7 28.2 %collective-permute-start.2 = (f32[128,512]{1,0:T(8,128)}, f32[128,512]{1,0:T(8,128)S(1)}, u32[]{:S(2)}, u32[]{:S(2)}) collective-permute-start(f32[128,512]{1,0:T(8,128)} %add.107), channel_id=1, source_target_pairs={{0,2},{1,3},{2,0},{3,1},{4,6},{5,7},{6,4},{7,5},{8,10},{9,11},{10,... | collective-permute-start | bytes 786440 | tf_op jit(solution)/shard_map/ppermute | solution.py:222
  111.3 25.7 %collective-permute-start.4 = (f32[128,512]{1,0:T(8,128)}, f32[128,512]{1,0:T(8,128)S(1)}, u32[]{:S(2)}, u32[]{:S(2)}) collective-permute-start(f32[128,512]{1,0:T(8,128)} %add.109), channel_id=1, source_target_pairs={{0,4},{1,5},{2,6},{3,7},{4,0},{5,1},{6,2},{7,3},{8,12},{9,13},{10,... | collective-permute-start | bytes 786440 | tf_op jit(solution)/shard_map/ppermute | solution.py:222
  112.3 24.7 %collective-permute-start.6 = (f32[128,512]{1,0:T(8,128)}, f32[128,512]{1,0:T(8,128)}, u32[]{:S(2)}, u32[]{:S(2)}) collective-permute-start(f32[128,512]{1,0:T(8,128)} %add.111), channel_id=1, source_target_pairs={{0,6},{1,7},{2,4},{3,5},{4,2},{5,3},{6,0},{7,1},{8,14},{9,15},{10,... | collective-permute-start | bytes 786440 | tf_op jit(solution)/shard_map/ppermute | solution.py:222
  120.6 5.9 %collective-permute-start.17 = (bf16[256,256]{1,0:T(8,128)(2,1)}, bf16[256,256]{1,0:T(8,128)(2,1)S(1)}, u32[]{:S(2)}, u32[]{:S(2)}) collective-permute-start(bf16[256,256]{1,0:T(8,128)(2,1)} %get-tuple-element.35), channel_id=1, source_target_pairs={{0,24},{8,16},{16,8},{24,0},{1,25},{9,17},{17,9},{25,1},{2,26},{10... | collective-permute-start | bytes 393224 | tf_op jit(solution)/shard_map/ppermute | solution.py:225
  120.7 5.9 %copy-start.9 = (bf16[256,256]{1,0:T(8,128)(2,1)S(1)}, bf16[256,256]{1,0:T(8,128)(2,1)}, u32[]{:S(2)}) copy-start(bf16[256,256]{1,0:T(8,128)(2,1)} %copy-done.8) | copy-start | bytes 393220
  120.7 5.9 %copy-start.11 = (bf16[256,256]{1,0:T(8,128)(2,1)S(1)}, bf16[256,256]{1,0:T(8,128)(2,1)}, u32[]{:S(2)}) copy-start(bf16[256,256]{1,0:T(8,128)(2,1)} %copy-done.10) | copy-start | bytes 393220
  126.5 10.5 %copy-start.7 = (f32[128,512]{1,0:T(8,128)S(1)}, f32[128,512]{1,0:T(8,128)}, u32[]{:S(2)}) copy-start(f32[128,512]{1,0:T(8,128)} %copy-done.6) | copy-start | bytes 786436
  132.1 11.6 %all-to-all-start = ((f32[16,8,128]{2,1,0:T(8,128)}), f32[16,8,128]{2,1,0:T(8,128)S(1)}, u32[]{:S(2)}, u32[]{:S(2)}) async-start(f32[16,8,128]{2,1,0:T(8,128)} %bitcast.19), calls=%async_computation | async-start | bytes 131072 | tf_op jit(solution)/shard_map/all_to_all | solution.py:284

commit v2 on v0

v2 whole, which is shorter than its diff:
```python
import functools

import jax
import jax.numpy as jnp
from jax import lax
from jax.experimental import pallas as pl
from jax.experimental.pallas import tpu as pltpu
from jax.sharding import Mesh, PartitionSpec as P

BF16 = jnp.bfloat16
F32 = jnp.float32
LANES = 128
WIDE = 256
GROUP = 8
ROWS_BY_ROWS = (((1,), (1,)), ((), ()))
VMEM_BYTES = 61 << 20
LEVELS, OFFSET, TINY = 65535.0, 32768, 1e-30
PARTS = 2
K1COST = 9 << 30
TILE = 768
BRIEF = pl.CostEstimate(flops=1024, bytes_accessed=1024, transcendentals=0)


def whole(array):
    return pl.BlockSpec(array.shape, lambda i, *_: (0,) * array.ndim)


def expand_terms(slots, blocks, width, base, ids, weights, out, row):
    query = lax.broadcasted_iota(jnp.int32, (1, GROUP * slots), 1) // slots
    parts = []
    for g in range(2):
        local = ids[pl.ds(2 * row + g, 1), :] - base
        inside = (local >= 0) & (local < width)
        key = jnp.where(inside, (local // WIDE) * GROUP + query, -1)
        rows = lax.broadcasted_iota(jnp.int32, (blocks * GROUP, GROUP * slots), 0)
        coarse = jnp.where(rows == key, weights[pl.ds(2 * row + g, 1), :], 0.0).astype(BF16)
        place = lax.broadcasted_iota(jnp.int32, (WIDE, GROUP * slots), 0)
        fine = jnp.where(place == (local & (WIDE - 1)), 1.0, 0.0).astype(BF16)
        parts.append(
            lax.dot_general(coarse, fine, ROWS_BY_ROWS, preferred_element_type=F32)
        )
    start = pl.multiple_of(row * 2 * GROUP, 2 * GROUP)
    for b in range(blocks):
        pair = [part[b * GROUP : (b + 1) * GROUP] for part in parts]
        out[pl.ds(start, 2 * GROUP), b * WIDE : (b + 1) * WIDE] = jnp.concatenate(
            pair, axis=0
        ).astype(BF16)


def score_kernel(place, query_ids, term_weights, slab, *refs):
    dense, coded, scales, whole_row, stored, weighed, ids, weights, came = refs[-9:]
    slots = query_ids.shape[1]
    images, width = slab.shape
    terms, queries, _ = coded.shape
    blocks = dense.shape[1] // WIDE
    steps = ids.shape[0] // 2
    fetch = pltpu.make_async_copy(slab, stored, came)
    fetch.start()
    weighed[...] = jnp.where(query_ids[...] >= 0, term_weights[...].astype(F32), 0.0)
    for q in range(GROUP):
        rows = pl.ds(q, ids.shape[0], stride=GROUP)
        ids[:, q * slots : (q + 1) * slots] = query_ids[rows, :]
        weights[:, q * slots : (q + 1) * slots] = weighed[rows, :]

    def step(row, carry):
        expand_terms(slots, blocks, width, place[0], ids, weights, dense, row)
        return carry

    lax.fori_loop(0, steps, step, 0, unroll=8 if steps % 8 == 0 else 1)
    fetch.wait()
    found = lax.dot_general(
        dense[:, :width], stored[...], ROWS_BY_ROWS, preferred_element_type=F32
    )
    lane = lax.broadcasted_iota(jnp.int32, (queries, LANES), 1)
    tops = jnp.zeros((queries, LANES), F32)
    whole_row[...] = jnp.zeros(whole_row.shape, F32)
    for t in range(terms):
        part = found[t * queries : (t + 1) * queries]
        top = jnp.maximum(jnp.max(part, axis=1, keepdims=True), TINY)
        whole_row[:, :images] = part * (LEVELS / top) + 0.5
        coded[t] = (whole_row[...].astype(jnp.int32) - OFFSET).astype(jnp.int16)
        tops = jnp.where(lane == t, top * (1.0 / LEVELS), tops)
    scales[...] = jnp.swapaxes(tops, 0, 1)[: scales.shape[0]]


def score_slab(place, ids, weights, slab, terms, images, part, parts, coded):
    queries, slots = ids.shape[0] // parts, ids.shape[1]
    groups = queries // GROUP
    share = pl.BlockSpec((queries, slots), lambda i, s: (part, 0))
    held, width = slab.shape
    padded = -(-width // WIDE) * WIDE
    rows = queries * parts // terms
    given = [] if coded is None else [coded]
    span = (terms // parts, rows, images)
    kept = -(-(terms // parts) // 8) * 8
    return pl.pallas_call(
        score_kernel,
        grid_spec=pltpu.PrefetchScalarGridSpec(
            num_scalar_prefetch=1,
            grid=(1,),
            in_specs=[share, share, pl.BlockSpec(memory_space=pltpu.HBM)]
            + [pl.BlockSpec(memory_space=pl.ANY)] * len(given),
            out_specs=[
                pl.BlockSpec((queries, padded), lambda i, s: (0, 0)),
                pl.BlockSpec(span, lambda i, s: (part, 0, 0)),
                pl.BlockSpec((kept, rows), lambda i, s: (0, 0)),
            ],
            scratch_shapes=[
                pltpu.VMEM((rows, images), F32),
                pltpu.VMEM(slab.shape, BF16),
                pltpu.VMEM((queries, slots), F32),
                pltpu.VMEM((groups, GROUP * slots), jnp.int32),
                pltpu.VMEM((groups, GROUP * slots), F32),
                pltpu.SemaphoreType.DMA,
            ],
        ),
        out_shape=[
            pltpu.HBM((queries, padded), BF16),
            pltpu.HBM((terms, rows, images), jnp.int16),
            jax.ShapeDtypeStruct((kept, rows), F32),
        ],
        input_output_aliases={} if coded is None else {4: 1},
        compiler_params=pltpu.CompilerParams(vmem_limit_bytes=VMEM_BYTES),
        cost_estimate=pl.CostEstimate(flops=K1COST, bytes_accessed=1024, transcendentals=0),
        name="score_slab",
    )(place, ids, weights, slab, *given)


def project_kernel(counts, block, images, patches, spans, place, *refs):
    groups = []
    for count in counts:
        groups.append(refs[:count])
        refs = refs[count:]
    features, weights, dense = groups
    bias, running, out, rows, gathered, wide, came_f, came_w, came_d = refs
    depth, columns = weights[0].shape[0], gathered.shape[1]
    index = place[0]

    rows_in = []
    for k, (source, start) in enumerate(zip(weights, spans)):
        at = pl.multiple_of(jnp.bitwise_xor(index, k) * depth, depth)
        rows_in.append(
            pltpu.make_async_copy(
                source.at[:, start : start + columns], gathered.at[pl.ds(at, depth), :], came_w.at[k]
            )
        )
    features_in, at = [], 0
    for k, source in enumerate(features):
        size = source.shape[0]
        copy = pltpu.make_async_copy(source, rows.at[at : at + size], came_f.at[k])
        features_in.append((at, copy))
        at += size
    start, size = spans[0], wide.shape[2]
    dense_in = [
        pltpu.make_async_copy(source.at[:, start : start + size], wide.at[k], came_d.at[k])
        for k, source in enumerate(dense)
    ]
    for copy in rows_in + [copy for _, copy in features_in] + dense_in:
        copy.start()
    for copy in rows_in:
        copy.wait()
    best = None
    for first in range(0, rows.shape[0], block):
        for at, copy in features_in:
            if first <= at < first + block:
                copy.wait()
        held = rows[first : first + block]
        real = held[:, 0:1].astype(F32) < jnp.inf
        tops = []
        for left in range(0, columns, TILE):
            right = min(left + TILE, columns)
            logits = jnp.dot(held, gathered[:, left:right], preferred_element_type=F32)
            logits = jnp.where(real, logits, -jnp.inf)
            logits = logits.reshape(-1, images, patches, right - left)
            tops.append(jnp.max(jnp.max(logits, axis=0), axis=1))
        tops = tops[0] if len(tops) == 1 else jnp.concatenate(tops, axis=1)
        best = tops if best is None else jnp.maximum(best, tops)
    active = jnp.log1p(jnp.maximum(best + bias[...], 0.0))
    pooled = jnp.concatenate([active, jnp.zeros_like(active)], axis=0).astype(BF16)
    queries, lines = out.shape[2], out.shape[1]
    t = 0
    for k, copy in enumerate(dense_in):
        copy.wait()
        found = lax.dot_general(
            pooled, wide[k, :, :columns], ROWS_BY_ROWS, preferred_element_type=F32
        )
        for left in range(0, found.shape[1], queries):
            out[t] = running[t] + found[:lines, left : left + queries]
            t += 1


def project(index, features, weights, spans, bias, dense, running, images, patches):
    width = features[0].shape[1]
    columns = bias.shape[1]
    total = sum(f.shape[0] for f in features)
    block = 512 if total % 512 == 0 else total
    queries, padded = dense[0].shape
    tail = spans[0] + columns >= padded - WIDE + 1 and columns % LANES
    kept = padded - spans[0] if tail else columns
    inputs = [*features, *weights, *dense]
    local = pl.BlockSpec(memory_space=pltpu.VMEM)
    return pl.pallas_call(
        functools.partial(
            project_kernel,
            (len(features), len(weights), len(dense)),
            block,
            images,
            patches,
            spans,
        ),
        in_specs=[pl.BlockSpec(memory_space=pltpu.SMEM)]
        + [pl.BlockSpec(memory_space=pl.ANY)] * len(inputs)
        + [local, local],
        out_specs=local,
        scratch_shapes=[
            pltpu.VMEM((total, width), BF16),
            pltpu.VMEM((width, columns), BF16),
            pltpu.VMEM((len(dense), queries, kept), BF16),
            pltpu.SemaphoreType.DMA((len(features),)),
            pltpu.SemaphoreType.DMA((len(weights),)),
            pltpu.SemaphoreType.DMA((len(dense),)),
        ],
        out_shape=jax.ShapeDtypeStruct(running.shape, F32),
        compiler_params=pltpu.CompilerParams(vmem_limit_bytes=40 << 20),
        cost_estimate=BRIEF,
        name="project",
    )(jnp.stack([index]).astype(jnp.int32), *inputs, bias, running)


def finish_kernel(images, coded, fresh, out, table):
    terms, queries, _ = coded.shape
    total = None
    for t in range(fresh.shape[0]):
        part = fresh[t]
        total = part if total is None else total + part
    table[...] = jnp.zeros(table.shape, F32)
    table[LANES - images :, :queries] = total[:images]
    for t in range(terms):
        table[t : t + 1, :queries] = fresh[t][images : images + 1]
    columns = jnp.swapaxes(table[...], 0, 1)[:queries]
    stored = None
    for t in range(terms):
        part = (coded[t].astype(jnp.int32) + OFFSET).astype(F32) * columns[:, t : t + 1]
        stored = part if stored is None else stored + part
    out[...] = stored
    tail = out.shape[1] - LANES
    lane = lax.broadcasted_iota(jnp.int32, (queries, LANES), 1)
    out[:, tail:] = jnp.where(lane < LANES - images, stored[:, tail:], columns)


def finish(coded, fresh, images):
    _, queries, total = coded.shape
    local = pl.BlockSpec(memory_space=pltpu.VMEM)
    return pl.pallas_call(
        functools.partial(finish_kernel, images),
        in_specs=[local, local],
        out_specs=local,
        scratch_shapes=[pltpu.VMEM((LANES, LANES), F32)],
        out_shape=jax.ShapeDtypeStruct((queries, total), F32),
        compiler_params=pltpu.CompilerParams(vmem_limit_bytes=16 << 20),
        cost_estimate=BRIEF,
        name="finish",
    )(coded, fresh)


def column_blocks(width):
    if width % LANES or width < 8 * LANES:
        return [(0, width)]
    tiles = width // LANES
    small = max(1, tiles * 2 // 15)
    sizes = [tiles * 6 // 30, tiles - tiles * 6 // 30 - small, small]
    return [(sum(sizes[:i]) * LANES, size * LANES) for i, size in enumerate(sizes)]


def shards(rows, terms, patches, patch_mask, proj_weight, proj_bias, slab, query_ids, term_weights):
    along_x = 1
    while along_x * along_x * 4 <= terms:
        along_x *= 2
    along_z = terms // along_x
    row, core, term = lax.axis_index("row"), lax.axis_index("core"), lax.axis_index("term")
    images, patch_rows, features = patches.shape
    width = proj_weight.shape[1]
    held = slab.shape[0]
    block_queries = query_ids.shape[0] // terms

    def to_term(value, k):
        return lax.ppermute(value, "term", [(i, i ^ k) for i in range(terms)])

    def to_row(value, k):
        return lax.ppermute(value, "row", [(i, i ^ k) for i in range(rows)])

    def to_core(value):
        return lax.ppermute(value, "core", [(0, 1), (1, 0)])

    def after(value, *done):
        return lax.optimization_barrier((value, done))[0]

    blocks = column_blocks(width)
    crossed = []
    for b, (start, size) in enumerate(blocks):
        sent = proj_weight[:, start : start + size]
        crossed.append([to_row(sent, k) for k in range(1, rows)])
        if not b:
            patches = after(patches, sent)

    marked = jnp.where(patch_mask[:, :, None] > 0, patches, jnp.array(jnp.inf, BF16))
    marked = marked.reshape(images * patch_rows, features)
    first_x = [to_term(marked, k) for k in range(1, along_x)]
    by_z = [to_term(marked, k * along_x) for k in range(1, along_z)]
    second_x = [[to_term(block, k) for block in by_z] for k in range(1, along_x)]
    gathered = [marked, *by_z, *first_x]
    for blocks_x in second_x:
        gathered += blocks_x

    place = jnp.stack([term * width]).astype(jnp.int32)
    dense, scales, coded = [], [], None
    for part in range(PARTS):
        here = after(place, by_z, first_x, crossed[0]) if part else place
        full, coded, scale = score_slab(
            here, query_ids, term_weights, slab, terms, held + images, part, PARTS, coded
        )
        dense.append(full)
        scales.append(scale[: terms // PARTS])
    coded = after(coded, crossed[:-1], second_x)
    coded = lax.all_to_all(coded, "term", split_axis=0, concat_axis=0, tiled=True)

    scales = jnp.concatenate(scales).reshape(terms, 1, block_queries)
    running = jnp.concatenate(
        [jnp.zeros((terms, images, block_queries), F32), scales,
         jnp.zeros((terms, 7 - images, block_queries), F32)], axis=1)
    bias = proj_bias.reshape(1, width)
    beside = to_core(after(proj_weight, by_z))
    swapped = [[to_core(part) for part in came] for came in crossed]
    for b, (start, size) in enumerate(blocks):
        pieces = [proj_weight, beside]
        for mine, other in zip(crossed[b], swapped[b]):
            pieces += [mine, other]
        if 0 < b < len(blocks) - 1:
            running = after(running, crossed[-1])
        spans = [start, start] + [0] * (len(pieces) - 2)
        running = project(
            2 * row + core, gathered, pieces, spans, bias[:, start : start + size],
            dense, running, images, patch_rows,
        )
    running, coded = lax.optimization_barrier((running, coded))
    fresh = lax.all_to_all(running, "term", split_axis=0, concat_axis=0, tiled=True)
    return finish(coded, fresh, images)


def solution(mesh):
    groups, terms = mesh.shape["img"], mesh.shape["term"]
    rows = groups // 2
    cores = Mesh(mesh.devices.reshape(rows, 2, terms), ("row", "core", "term"))
    img = ("row", "core")
    placed = (
        P(img, "term", None),
        P(img, "term"),
        P(img, "term"),
        P("term"),
        P(img, "term"),
        P(),
        P(),
    )
    return jax.shard_map(
        functools.partial(shards, rows, terms),
        mesh=cores,
        in_specs=placed,
        out_specs=P("term", img),
        check_vma=False,
    )
```

time: 384 us -> 101 us (0.26)
  waiting for transfers between devices: 174 us -> 18 us
  local copies, waits for them, and re-layouts: 124 us -> 9.15 us
  Pallas kernels: 0 us -> 36 us
  blocking collectives: 34.8 us -> 12.5 us
  starting transfers between devices: 5.55 us -> 22.8 us
  matrix products: 16.2 us -> 0 us
  other arithmetic: 15.4 us -> 1.84 us
  between operations: 13.5 us -> 0.23 us
    gather x1 -> x0, local copies, waits for them, and re-layouts: 114 us -> none  [shards(): picked = jnp.take(regrouped, safe_ids, axis=1).astype(jnp.float32)]
    all_to_all x1, waiting for transfers between devices: 87.1 us -> 0.01 us  [shards(): lax.all_to_all(coded, 'term', split_axis=0, concat_axis=0, tiled=True)]
    all_gather x2 -> x0, waiting for transfers between devices: 85.9 us -> none  [the longest x1 55.4 us: shards(): proj_full = lax.all_gather(proj_weight, 'img', axis=0, tiled=True)]
    pallas_call x0 -> x6, Pallas kernels: none -> 36 us  [the longest x3 17.5 us: project(): pl.pallas_call(functools.partial(project_kernel, (len(features), len(weig...]
    all_gather x1 -> x0, blocking collectives: 22.2 us -> none  [shards(): lax.all_gather(patch_mask.astype(jnp.bfloat16), 'term', axis=1, tiled=True)]
    ppermute x0 -> x14, waiting for transfers between devices: none -> 18 us  [the longest x7 9.79 us: to_term(): return lax.ppermute(value, 'term', [(i, i ^ k) for i in range(terms)])]
    dot_general x1 -> x0, matrix products: 16.2 us -> none  [shards(): jnp.einsum('npd,dv->npv', features, proj_full, preferred_element_type=jnp...]
    ppermute x0 -> x14, starting transfers between devices: none -> 15.9 us  [the longest x7 11 us: to_term(): return lax.ppermute(value, 'term', [(i, i ^ k) for i in range(terms)])]
  transfers between devices with their start and end apart: 3 -> 15, of which waited for: 3 -> 6; matrix products, arithmetic and copies ran while one was open for 0% -> 5% of each run, Pallas kernels for 0% -> 33%
where the time goes in v2:
time: 101 us; the launch traced here: 100 us
  Pallas kernels  36 us (36%)
  starting transfers between devices  22.8 us (23%)
  waiting for transfers between devices  18 us (18%)
  blocking collectives  12.5 us (12%)
  local copies, waits for them, and re-layouts  9.15 us (9%)
  other arithmetic  1.84 us (2%)
    pallas_call x3, Pallas kernels, project(): pl.pallas_call(functools.partial(project_kernel, (len(features), len(weig...  17.5 us
    pallas_call x2, Pallas kernels, score_slab(): pl.pallas_call(score_kernel, grid_spec=pltpu.PrefetchScalarGridSpec(num_s...  16.1 us
    all_to_all x1, blocking collectives, shards(): lax.all_to_all(running, 'term', split_axis=0, concat_axis=0, tiled=True)  12.5 us
    ppermute x7, starting transfers between devices, to_term(): return lax.ppermute(value, 'term', [(i, i ^ k) for i in range(terms)])  11 us
    ppermute x7, waiting for transfers between devices, to_term(): return lax.ppermute(value, 'term', [(i, i ^ k) for i in range(terms)])  9.79 us
    ppermute x3, waiting for transfers between devices, to_row(): return lax.ppermute(value, 'row', [(i, i ^ k) for i in range(rows)])  8.19 us
    all_to_all x1, starting transfers between devices, shards(): lax.all_to_all(coded, 'term', split_axis=0, concat_axis=0, tiled=True)  6.91 us
    slice x3, local copies, waits for them, and re-layouts, shards(): sent = proj_weight[:, start:start + size]  5.02 us
  transfers between devices with their start and end apart: 15, of which 6 were waited for; matrix products, arithmetic and copies ran while one was open for 5% of the time, Pallas kernels for 33%

profile of v2, /device:TPU:0, one launch (start us, length us, event | category | flops | bytes accessed | tf_op | source)
XLA Modules:
  0.0 100.5 jit_solution(15098209194711270023)
XLA Ops:
  0.0 1.8 %slice.24 = bf16[256,768]{1,0:T(8,128)(2,1)} slice(bf16[256,3840]{1,0:T(8,128)(2,1)} %refs_8_.5), slice={[0:256], [0:768]} | slice | bytes 786432 | tf_op jit(solution)/shard_map/slice | solution.py:301
  1.8 0.7 broadcast_compare_fusion
  2.5 1.0 %broadcast_select_fusion = bf16[4,32,1024]{2,1,0:T(8,128)(2,1)S(1)} fusion(bf16[4,32,1024]{2,1,0:T(8,128)(2,1)} %param.7, pred[4,32]{1,0:T(4,128)(4,1)S(1)} %broadcast_compare_fusion), kind=kLoop, calls=%fused_computation | loop fusion | flops 131072 | bytes 524416 | tf_op jit(solution)/shard_map/jit(_where)/select_n | solution.py:306
  3.6 3.1 %collective-permute-start = (bf16[128,1024]{1,0:T(8,128)(2,1)S(1)}, bf16[128,1024]{1,0:T(8,128)(2,1)S(1)}, u32[]{:S(2)}, u32[]{:S(2)}) collective-permute-start(bf16[128,1024]{1,0:T(8,128)(2,1)S(1)} %bitcast.4), channel_id=1, source_target_pairs={{0,2},{1,3},{2,0},{3,1},{4,6},{5,7},{6,4},{7,5},{8,10},{9,11},{10,... | collective-permute-start | bytes 786440 | tf_op jit(solution)/shard_map/ppermute | solution.py:287
  6.7 2.6 %collective-permute-start.1 = (bf16[128,1024]{1,0:T(8,128)(2,1)S(1)}, bf16[128,1024]{1,0:T(8,128)(2,1)S(1)}, u32[]{:S(2)}, u32[]{:S(2)}) collective-permute-start(bf16[128,1024]{1,0:T(8,128)(2,1)S(1)} %bitcast.5), channel_id=1, source_target_pairs={{0,4},{1,5},{2,6},{3,7},{4,0},{5,1},{6,2},{7,3},{8,12},{9,13},{10,... | collective-permute-start | bytes 786440 | tf_op jit(solution)/shard_map/ppermute | solution.py:287
  9.3 0.0 collective-permute-start.2
  9.3 1.7 %collective-permute-start.3 = (bf16[128,1024]{1,0:T(8,128)(2,1)S(1)}, bf16[128,1024]{1,0:T(8,128)(2,1)}, u32[]{:S(2)}, u32[]{:S(2)}) collective-permute-start(bf16[128,1024]{1,0:T(8,128)(2,1)S(1)} %bitcast.7), channel_id=1, source_target_pairs={{0,1},{1,0},{2,3},{3,2},{4,5},{5,4},{6,7},{7,6},{8,9},{9,8},{10,11... | collective-permute-start | bytes 786440 | tf_op jit(solution)/shard_map/ppermute | solution.py:287
  11.0 1.5 %collective-permute-start.10 = (bf16[256,768]{1,0:T(8,128)(2,1)}, bf16[256,768]{1,0:T(8,128)(2,1)}, u32[]{:S(2)}, u32[]{:S(2)}) collective-permute-start(bf16[256,768]{1,0:T(8,128)(2,1)} %slice.24), channel_id=1, source_target_pairs={{0,16},{16,0},{1,17},{17,1},{2,18},{18,2},{3,19},{19,3},{4,20},{20... | collective-permute-start | bytes 1179656 | tf_op jit(solution)/shard_map/ppermute | solution.py:290
  12.5 2.5 %slice.27 = bf16[256,2560]{1,0:T(8,128)(2,1)} slice(bf16[256,3840]{1,0:T(8,128)(2,1)} %refs_8_.5), slice={[0:256], [768:3328]} | slice | bytes 2621440 | tf_op jit(solution)/shard_map/slice | solution.py:301
  15.0 1.0 %copy.9.query_ids = s32[1024,32]{1,0:T(8,128)} copy(s32[1024,32]{0,1:T(8,128)S(1)} %copy-done.3) | data formatting | bytes 262144 | tf_op args[5]
  16.0 0.8 copy.10.term_weights
  16.9 1.0 collective-permute-done.refs_1_
  17.8 1.7 %collective-permute-start.11 = (bf16[256,2560]{1,0:T(8,128)(2,1)}, bf16[256,2560]{1,0:T(8,128)(2,1)}, u32[]{:S(2)}, u32[]{:S(2)}) collective-permute-start(bf16[256,2560]{1,0:T(8,128)(2,1)} %slice.27), channel_id=1, source_target_pairs={{0,16},{16,0},{1,17},{17,1},{2,18},{18,2},{3,19},{19,3},{4,20},{20... | collective-permute-start | bytes 3932168 | tf_op jit(solution)/shard_map/ppermute | solution.py:290
  19.5 8.1 %score_slab.2 = (bf16[512,3840]{1,0:T(8,128)(2,1)}, s16[8,128,512]{2,1,0:T(8,128)(2,1)}, f32[8,128]{1,0:T(8,128)}) custom-call(s32[1]{0:T(128)} %bitcast.2.place, s32[1024,32]{1,0:T(8,128)} %copy.9.query_ids, bf16[1024,32]{1,0:T(8,128)(2,1)} %copy.10.term_weights, bf16[508,3840]{1,0:T(8,128)(2,1)} %slab.3), custom_call_target="tpu_custom_call" | custom-call | flops 9663676416 | bytes 1024 | tf_op jit(solution)/shard_map/score_slab/pallas_call | solution.py:96
  27.6 0.4 collective-permute-done.1.refs_2_
  28.0 0.0 collective-permute-done.2.refs_3_
  28.1 0.0 collective-permute-start.7
  28.1 1.6 %collective-permute-start.4 = (bf16[128,1024]{1,0:T(8,128)(2,1)S(1)}, bf16[128,1024]{1,0:T(8,128)(2,1)}, u32[]{:S(2)}, u32[]{:S(2)}) collective-permute-start(bf16[128,1024]{1,0:T(8,128)(2,1)S(1)} %collective-permute-done.refs_1_), channel_id=1, source_target_pairs={{0,1},{1,0},{2,3},{3,2},{4,5},{5,4},{6,7},{7,6},{8,9},{9,8},{10,11... | collective-permute-start | bytes 786440 | tf_op jit(solution)/shard_map/ppermute | solution.py:287
  29.6 0.0 collective-permute-done.3.refs_4_
  29.6 0.5 collective-permute-start.5
  30.2 0.0 collective-permute-done.10.refs_10_
  30.2 1.5 %collective-permute-start.6 = (bf16[128,1024]{1,0:T(8,128)(2,1)S(1)}, bf16[128,1024]{1,0:T(8,128)(2,1)}, u32[]{:S(2)}, u32[]{:S(2)}) collective-permute-start(bf16[128,1024]{1,0:T(8,128)(2,1)S(1)} %collective-permute-done.2.refs_3_), channel_id=1, source_target_pairs={{0,1},{1,0},{2,3},{3,2},{4,5},{5,4},{6,7},{7,6},{8,9},{9,8},{10,11... | collective-permute-start | bytes 786440 | tf_op jit(solution)/shard_map/ppermute | solution.py:287
  31.7 8.0 %score_slab.3 = (bf16[512,3840]{1,0:T(8,128)(2,1)}, s16[8,128,512]{2,1,0:T(8,128)(2,1)}, f32[8,128]{1,0:T(8,128)}) custom-call(s32[1]{0:T(128)} %bitcast.2.place, s32[1024,32]{1,0:T(8,128)} %copy.9.query_ids, bf16[1024,32]{1,0:T(8,128)(2,1)} %copy.10.term_weights, bf16[508,3840]{1,0:T(8,128)(2,1)} %slab.3, ...), custom_call_target="tpu_custom_call", output_to_operand_aliasing={{1}: (4, {})} | custom-call | flops 9663676416 | bytes 1024 | tf_op jit(solution)/shard_map/score_slab/pallas_call | solution.py:96
  39.6 0.0 copy-start.5
  39.7 0.0 collective-permute-done.4.refs_5_
  39.7 3.3 %collective-permute-done.5.refs_6_ = bf16[128,1024]{1,0:T(8,128)(2,1)} collective-permute-done((bf16[128,1024]{1,0:T(8,128)(2,1)S(1)}, bf16[128,1024]{1,0:T(8,128)(2,1)}, u32[]{:S(2)}, u32[]{:S(2)}) %collective-permute-start.5) | collective-permute-done | bytes 262176 | tf_op jit(solution)/shard_map/ppermute | solution.py:287
  43.0 5.2 %collective-permute-done.6.refs_7_ = bf16[128,1024]{1,0:T(8,128)(2,1)} collective-permute-done((bf16[128,1024]{1,0:T(8,128)(2,1)S(1)}, bf16[128,1024]{1,0:T(8,128)(2,1)}, u32[]{:S(2)}, u32[]{:S(2)}) %collective-permute-start.6) | collective-permute-done | bytes 262176 | tf_op jit(solution)/shard_map/ppermute | solution.py:287
  48.1 1.1 %collective-permute-done.11.refs_10_ = bf16[256,2560]{1,0:T(8,128)(2,1)} collective-permute-done((bf16[256,2560]{1,0:T(8,128)(2,1)}, bf16[256,2560]{1,0:T(8,128)(2,1)}, u32[]{:S(2)}, u32[]{:S(2)}) %collective-permute-start.11) | collective-permute-done | bytes 1310752 | tf_op jit(solution)/shard_map/ppermute | solution.py:290
  49.2 6.9 %all-to-all-start = ((s16[8,128,512]{2,1,0:T(8,128)(2,1)}), s16[8,128,512]{2,1,0:T(8,128)(2,1)}, u32[]{:S(2)}, u32[]{:S(2)}) async-start(s16[8,128,512]{2,1,0:T(8,128)(2,1)} %get-tuple-element.28), calls=%async_computation | async-start | bytes 2097152 | tf_op jit(solution)/shard_map/all_to_all | solution.py:325
  56.1 0.0 collective-permute-start.12
  56.1 0.7 slice.25
  56.8 1.5 %collective-permute-start.8 = (bf16[256,512]{1,0:T(8,128)(2,1)}, bf16[256,512]{1,0:T(8,128)(2,1)}, u32[]{:S(2)}, u32[]{:S(2)}) collective-permute-start(bf16[256,512]{1,0:T(8,128)(2,1)} %slice.25), channel_id=1, source_target_pairs={{0,16},{16,0},{1,17},{17,1},{2,18},{18,2},{3,19},{19,3},{4,20},{20... | collective-permute-start | bytes 786440 | tf_op jit(solution)/shard_map/ppermute | solution.py:290
  58.3 0.2 collective-permute-start.13
  58.6 0.1 pad.2.clone
  58.7 7.1 %collective-permute-done.8.refs_10_ = bf16[256,512]{1,0:T(8,128)(2,1)} collective-permute-done((bf16[256,512]{1,0:T(8,128)(2,1)}, bf16[256,512]{1,0:T(8,128)(2,1)}, u32[]{:S(2)}, u32[]{:S(2)}) %collective-permute-start.8) | collective-permute-done | bytes 262176 | tf_op jit(solution)/shard_map/ppermute | solution.py:290
  65.8 0.0 collective-permute-start.9
  65.9 0.1 maximum_maximum_fusion.refs_15_
  65.9 0.0 collective-permute-done.13.refs_11_
  66.0 0.0 collective-permute-done.7.refs_9_
  66.0 2.1 %copy-done = bf16[512,3840]{1,0:T(8,128)(2,1)S(1)} copy-done((bf16[512,3840]{1,0:T(8,128)(2,1)S(1)}, bf16[512,3840]{1,0:T(8,128)(2,1)}, u32[]{:S(2)}) %copy-start) | copy-done | bytes 3932184
  68.1 4.5 %project.3.refs_15_ = f32[8,8,128]{2,1,0:T(8,128)S(1)} custom-call(s32[1]{0:T(128)} %bitcast.place, bf16[128,1024]{1,0:T(8,128)(2,1)S(1)} %bitcast.8, bf16[128,1024]{1,0:T(8,128)(2,1)S(1)} %collective-permute-done.refs_1_, bf16[128,1024]{1,0:T(8,128)(2,1)S(1)} %collective-permute-done.1.refs_2_, bf16[128,1024]{1,0:T(8,128)(2,1)S(1)} %collective-permute-done.2.refs_3_, ...), custom_call_target="tpu_custom_call" | custom-call | flops 1024 | bytes 1024 | tf_op jit(solution)/shard_map/project/pallas_call | solution.py:202
  72.5 0.0 collective-permute-done.12.refs_11_
  72.6 9.9 %project.4.refs_15_ = f32[8,8,128]{2,1,0:T(8,128)S(1)} custom-call(s32[1]{0:T(128)} %bitcast.place, bf16[128,1024]{1,0:T(8,128)(2,1)S(1)} %bitcast.9, bf16[128,1024]{1,0:T(8,128)(2,1)S(1)} %collective-permute-done.refs_1_, bf16[128,1024]{1,0:T(8,128)(2,1)S(1)} %collective-permute-done.1.refs_2_, bf16[128,1024]{1,0:T(8,128)(2,1)S(1)} %collective-permute-done.2.refs_3_, ...), custom_call_target="tpu_custom_call" | custom-call | flops 1024 | bytes 1024 | tf_op jit(solution)/shard_map/project/pallas_call | solution.py:202
  82.4 0.0 collective-permute-done.9.refs_11_
  82.5 3.2 %project.5 = f32[8,8,128]{2,1,0:T(8,128)S(1)} custom-call(s32[1]{0:T(128)} %bitcast.place, bf16[128,1024]{1,0:T(8,128)(2,1)S(1)} %bitcast.10, bf16[128,1024]{1,0:T(8,128)(2,1)S(1)} %collective-permute-done.refs_1_, bf16[128,1024]{1,0:T(8,128)(2,1)S(1)} %collective-permute-done.1.refs_2_, bf16[128,1024]{1,0:T(8,128)(2,1)S(1)} %collective-permute-done.2.refs_3_, ...), custom_call_target="tpu_custom_call" | custom-call | flops 1024 | bytes 1024 | tf_op jit(solution)/shard_map/project/pallas_call | solution.py:202
  85.6 0.0 all-to-all-done.coded
  85.6 12.5 %all_to_all.10.fresh = f32[8,8,128]{2,1,0:T(8,128)S(1)} all-to-all(f32[8,8,128]{2,1,0:T(8,128)S(1)} %project.5), channel_id=1, replica_groups=mesh['row'=2,'core'=2,'term'=8] {'term'}, dimensions={0} | all-to-all | bytes 65536 | tf_op jit(solution)/shard_map/all_to_all | solution.py:346
  98.1 2.4 %finish.1 = f32[128,512]{1,0:T(8,128)} custom-call(s16[8,128,512]{2,1,0:T(8,128)(2,1)} %all-to-all-done.coded, f32[8,8,128]{2,1,0:T(8,128)S(1)} %all_to_all.10.fresh), custom_call_target="tpu_custom_call" | custom-call | flops 1024 | bytes 1024 | tf_op jit(solution)/shard_map/finish/pallas_call | solution.py:254
  (24 shorter events, 0.1 us)
Async XLA Ops:
  0.0 15.0 %copy-start.3 = (s32[1024,32]{0,1:T(8,128)S(1)}, s32[1024,32]{0,1:T(8,128)}, u32[]{:S(2)}) copy-start(s32[1024,32]{0,1:T(8,128)} %param.12) | copy-start | bytes 393220
  1.8 14.2 %copy-start.4 = (bf16[1024,32]{0,1:T(8,128)(2,1)S(1)}, bf16[1024,32]{0,1:T(8,128)(2,1)}, u32[]{:S(2)}) copy-start(bf16[1024,32]{0,1:T(8,128)(2,1)} %param.13) | copy-start | bytes 196612
  3.6 14.2 %collective-permute-start = (bf16[128,1024]{1,0:T(8,128)(2,1)S(1)}, bf16[128,1024]{1,0:T(8,128)(2,1)S(1)}, u32[]{:S(2)}, u32[]{:S(2)}) collective-permute-start(bf16[128,1024]{1,0:T(8,128)(2,1)S(1)} %bitcast.4), channel_id=1, source_target_pairs={{0,2},{1,3},{2,0},{3,1},{4,6},{5,7},{6,4},{7,5},{8,10},{9,11},{10,... | collective-permute-start | bytes 786440 | tf_op jit(solution)/shard_map/ppermute | solution.py:287
  6.7 21.4 %collective-permute-start.1 = (bf16[128,1024]{1,0:T(8,128)(2,1)S(1)}, bf16[128,1024]{1,0:T(8,128)(2,1)S(1)}, u32[]{:S(2)}, u32[]{:S(2)}) collective-permute-start(bf16[128,1024]{1,0:T(8,128)(2,1)S(1)} %bitcast.5), channel_id=1, source_target_pairs={{0,4},{1,5},{2,6},{3,7},{4,0},{5,1},{6,2},{7,3},{8,12},{9,13},{10,... | collective-permute-start | bytes 786440 | tf_op jit(solution)/shard_map/ppermute | solution.py:287
  9.3 18.8 %collective-permute-start.2 = (bf16[128,1024]{1,0:T(8,128)(2,1)S(1)}, bf16[128,1024]{1,0:T(8,128)(2,1)S(1)}, u32[]{:S(2)}, u32[]{:S(2)}) collective-permute-start(bf16[128,1024]{1,0:T(8,128)(2,1)S(1)} %bitcast.6), channel_id=1, source_target_pairs={{0,6},{1,7},{2,4},{3,5},{4,2},{5,3},{6,0},{7,1},{8,14},{9,15},{10,... | collective-permute-start | bytes 786440 | tf_op jit(solution)/shard_map/ppermute | solution.py:287
  9.3 20.4 %collective-permute-start.3 = (bf16[128,1024]{1,0:T(8,128)(2,1)S(1)}, bf16[128,1024]{1,0:T(8,128)(2,1)}, u32[]{:S(2)}, u32[]{:S(2)}) collective-permute-start(bf16[128,1024]{1,0:T(8,128)(2,1)S(1)} %bitcast.7), channel_id=1, source_target_pairs={{0,1},{1,0},{2,3},{3,2},{4,5},{5,4},{6,7},{7,6},{8,9},{9,8},{10,11... | collective-permute-start | bytes 786440 | tf_op jit(solution)/shard_map/ppermute | solution.py:287
  11.0 19.2 %collective-permute-start.10 = (bf16[256,768]{1,0:T(8,128)(2,1)}, bf16[256,768]{1,0:T(8,128)(2,1)}, u32[]{:S(2)}, u32[]{:S(2)}) collective-permute-start(bf16[256,768]{1,0:T(8,128)(2,1)} %slice.24), channel_id=1, source_target_pairs={{0,16},{16,0},{1,17},{17,1},{2,18},{18,2},{3,19},{19,3},{4,20},{20... | collective-permute-start | bytes 1179656 | tf_op jit(solution)/shard_map/ppermute | solution.py:290
  17.8 31.3 %collective-permute-start.11 = (bf16[256,2560]{1,0:T(8,128)(2,1)}, bf16[256,2560]{1,0:T(8,128)(2,1)}, u32[]{:S(2)}, u32[]{:S(2)}) collective-permute-start(bf16[256,2560]{1,0:T(8,128)(2,1)} %slice.27), channel_id=1, source_target_pairs={{0,16},{16,0},{1,17},{17,1},{2,18},{18,2},{3,19},{19,3},{4,20},{20... | collective-permute-start | bytes 3932168 | tf_op jit(solution)/shard_map/ppermute | solution.py:290
  19.5 8.5 %copy-start.2 = (bf16[256,3840]{1,0:T(8,128)(2,1)S(1)}, bf16[256,3840]{1,0:T(8,128)(2,1)}, u32[]{:S(2)}) copy-start(bf16[256,3840]{1,0:T(8,128)(2,1)} %refs_8_.5) | copy-start | bytes 5898244
  28.1 37.9 %collective-permute-start.7 = (bf16[256,3840]{1,0:T(8,128)(2,1)S(1)}, bf16[256,3840]{1,0:T(8,128)(2,1)}, u32[]{:S(2)}, u32[]{:S(2)}) collective-permute-start(bf16[256,3840]{1,0:T(8,128)(2,1)S(1)} %copy-done.2), channel_id=1, source_target_pairs={{0,8},{8,0},{1,9},{9,1},{2,10},{10,2},{3,11},{11,3},{4,12},{12,4},... | collective-permute-start | bytes 5898248 | tf_op jit(solution)/shard_map/ppermute | solution.py:293
  28.1 11.6 %collective-permute-start.4 = (bf16[128,1024]{1,0:T(8,128)(2,1)S(1)}, bf16[128,1024]{1,0:T(8,128)(2,1)}, u32[]{:S(2)}, u32[]{:S(2)}) collective-permute-start(bf16[128,1024]{1,0:T(8,128)(2,1)S(1)} %collective-permute-done.refs_1_), channel_id=1, source_target_pairs={{0,1},{1,0},{2,3},{3,2},{4,5},{5,4},{6,7},{7,6},{8,9},{9,8},{10,11... | collective-permute-start | bytes 786440 | tf_op jit(solution)/shard_map/ppermute | solution.py:287
  29.6 13.3 %collective-permute-start.5 = (bf16[128,1024]{1,0:T(8,128)(2,1)S(1)}, bf16[128,1024]{1,0:T(8,128)(2,1)}, u32[]{:S(2)}, u32[]{:S(2)}) collective-permute-start(bf16[128,1024]{1,0:T(8,128)(2,1)S(1)} %collective-permute-done.1.refs_2_), channel_id=1, source_target_pairs={{0,1},{1,0},{2,3},{3,2},{4,5},{5,4},{6,7},{7,6},{8,9},{9,8},{10,11... | collective-permute-start | bytes 786440 | tf_op jit(solution)/shard_map/ppermute | solution.py:287
  30.2 18.0 %collective-permute-start.6 = (bf16[128,1024]{1,0:T(8,128)(2,1)S(1)}, bf16[128,1024]{1,0:T(8,128)(2,1)}, u32[]{:S(2)}, u32[]{:S(2)}) collective-permute-start(bf16[128,1024]{1,0:T(8,128)(2,1)S(1)} %collective-permute-done.2.refs_3_), channel_id=1, source_target_pairs={{0,1},{1,0},{2,3},{3,2},{4,5},{5,4},{6,7},{7,6},{8,9},{9,8},{10,11... | collective-permute-start | bytes 786440 | tf_op jit(solution)/shard_map/ppermute | solution.py:287
  39.6 18.9 %copy-start.5 = (f32[3840]{0:T(1024)S(1)}, f32[3840]{0:T(1024)}, u32[]{:S(2)}) copy-start(f32[3840]{0:T(1024)} %param.10) | copy-start | bytes 46084
  39.7 19.0 %copy-start.7 = (f32[8,128]{1,0:T(8,128)S(1)}, f32[8,128]{1,0:T(8,128)}, u32[]{:S(2)}) copy-start(f32[8,128]{1,0:T(8,128)} %get-tuple-element.24) | copy-start | bytes 12292
  39.7 26.2 %copy-start.6 = (f32[8,128]{1,0:T(8,128)S(1)}, f32[8,128]{1,0:T(8,128)}, u32[]{:S(2)}) copy-start(f32[8,128]{1,0:T(8,128)} %get-tuple-element.25) | copy-start | bytes 12292
  49.2 36.5 %all-to-all-start = ((s16[8,128,512]{2,1,0:T(8,128)(2,1)}), s16[8,128,512]{2,1,0:T(8,128)(2,1)}, u32[]{:S(2)}, u32[]{:S(2)}) async-start(s16[8,128,512]{2,1,0:T(8,128)(2,1)} %get-tuple-element.28), calls=%async_computation | async-start | bytes 2097152 | tf_op jit(solution)/shard_map/all_to_all | solution.py:325
  56.1 16.4 %collective-permute-start.12 = (bf16[256,2560]{1,0:T(8,128)(2,1)}, bf16[256,2560]{1,0:T(8,128)(2,1)}, u32[]{:S(2)}, u32[]{:S(2)}) collective-permute-start(bf16[256,2560]{1,0:T(8,128)(2,1)} %collective-permute-done.11.refs_10_), channel_id=1, source_target_pairs={{0,8},{8,0},{1,9},{9,1},{2,10},{10,2},{3,11},{11,3},{4,12},{12,4},... | collective-permute-start | bytes 3932168 | tf_op jit(solution)/shard_map/ppermute | solution.py:293
  56.8 9.0 %collective-permute-start.8 = (bf16[256,512]{1,0:T(8,128)(2,1)}, bf16[256,512]{1,0:T(8,128)(2,1)}, u32[]{:S(2)}, u32[]{:S(2)}) collective-permute-start(bf16[256,512]{1,0:T(8,128)(2,1)} %slice.25), channel_id=1, source_target_pairs={{0,16},{16,0},{1,17},{17,1},{2,18},{18,2},{3,19},{19,3},{4,20},{20... | collective-permute-start | bytes 786440 | tf_op jit(solution)/shard_map/ppermute | solution.py:290
  58.3 7.6 %collective-permute-start.13 = (bf16[256,768]{1,0:T(8,128)(2,1)}, bf16[256,768]{1,0:T(8,128)(2,1)S(1)}, u32[]{:S(2)}, u32[]{:S(2)}) collective-permute-start(bf16[256,768]{1,0:T(8,128)(2,1)} %collective-permute-done.10.refs_10_), channel_id=1, source_target_pairs={{0,8},{8,0},{1,9},{9,1},{2,10},{10,2},{3,11},{11,3},{4,12},{12,4},... | collective-permute-start | bytes 1179656 | tf_op jit(solution)/shard_map/ppermute | solution.py:293
  65.8 16.6 %collective-permute-start.9 = (bf16[256,512]{1,0:T(8,128)(2,1)}, bf16[256,512]{1,0:T(8,128)(2,1)S(1)}, u32[]{:S(2)}, u32[]{:S(2)}) collective-permute-start(bf16[256,512]{1,0:T(8,128)(2,1)} %collective-permute-done.8.refs_10_), channel_id=1, source_target_pairs={{0,8},{8,0},{1,9},{9,1},{2,10},{10,2},{3,11},{11,3},{4,12},{12,4},... | collective-permute-start | bytes 786440 | tf_op jit(solution)/shard_map/ppermute | solution.py:293
  66.0 2.1 %copy-start = (bf16[512,3840]{1,0:T(8,128)(2,1)S(1)}, bf16[512,3840]{1,0:T(8,128)(2,1)}, u32[]{:S(2)}) copy-start(bf16[512,3840]{1,0:T(8,128)(2,1)} %get-tuple-element.20.refs_12_) | copy-start | bytes 11796484
  72.5 9.9 %copy-start.1 = (bf16[512,3840]{1,0:T(8,128)(2,1)S(1)}, bf16[512,3840]{1,0:T(8,128)(2,1)}, u32[]{:S(2)}) copy-start(bf16[512,3840]{1,0:T(8,128)(2,1)} %get-tuple-element.23.refs_13_) | copy-start | bytes 11796484

commit v3 on v2

--- a/solution.py
+++ b/solution.py
@@ -16,7 +16,7 @@
 VMEM_BYTES = 61 << 20
 LEVELS, OFFSET, TINY = 65535.0, 32768, 1e-30
 PARTS = 2
-K1COST = 9 << 30
+K1COST = 13 << 30
 TILE = 768
 BRIEF = pl.CostEstimate(flops=1024, bytes_accessed=1024, transcendentals=0)
 
@@ -48,25 +48,36 @@
 
 
 def score_kernel(place, query_ids, term_weights, slab, *refs):
-    dense, coded, scales, whole_row, stored, weighed, ids, weights, came = refs[-9:]
-    slots = query_ids.shape[1]
+    dense_out, coded, scales, dense, whole_row, stored, listed, weighed, ids, weights, came, sent = refs[-12:]
+    slots = query_ids.shape[0]
     images, width = slab.shape
     terms, queries, _ = coded.shape
     blocks = dense.shape[1] // WIDE
     steps = ids.shape[0] // 2
     fetch = pltpu.make_async_copy(slab, stored, came)
     fetch.start()
-    weighed[...] = jnp.where(query_ids[...] >= 0, term_weights[...].astype(F32), 0.0)
+    given = term_weights[...].astype(F32)
+    listed[...] = jnp.swapaxes(query_ids[...], 0, 1)
+    weighed[...] = jnp.swapaxes(jnp.where(query_ids[...] >= 0, given, 0.0), 0, 1)
     for q in range(GROUP):
         rows = pl.ds(q, ids.shape[0], stride=GROUP)
-        ids[:, q * slots : (q + 1) * slots] = query_ids[rows, :]
+        ids[:, q * slots : (q + 1) * slots] = listed[rows, :]
         weights[:, q * slots : (q + 1) * slots] = weighed[rows, :]
 
     def step(row, carry):
         expand_terms(slots, blocks, width, place[0], ids, weights, dense, row)
         return carry
 
-    lax.fori_loop(0, steps, step, 0, unroll=8 if steps % 8 == 0 else 1)
+    shares = 4 if steps % 4 == 0 else 1
+    count = steps // shares
+    leaving = []
+    for share in range(shares):
+        lax.fori_loop(
+            share * count, (share + 1) * count, step, 0, unroll=8 if count % 8 == 0 else 1
+        )
+        done = pl.ds(share * count * 2 * GROUP, count * 2 * GROUP)
+        leaving.append(pltpu.make_async_copy(dense.at[done], dense_out.at[done], sent.at[share]))
+        leaving[-1].start()
     fetch.wait()
     found = lax.dot_general(
         dense[:, :width], stored[...], ROWS_BY_ROWS, preferred_element_type=F32
@@ -81,12 +92,14 @@
         coded[t] = (whole_row[...].astype(jnp.int32) - OFFSET).astype(jnp.int16)
         tops = jnp.where(lane == t, top * (1.0 / LEVELS), tops)
     scales[...] = jnp.swapaxes(tops, 0, 1)[: scales.shape[0]]
+    for copy in leaving:
+        copy.wait()
 
 
 def score_slab(place, ids, weights, slab, terms, images, part, parts, coded):
-    queries, slots = ids.shape[0] // parts, ids.shape[1]
+    slots, queries = ids.shape[0], ids.shape[1] // parts
     groups = queries // GROUP
-    share = pl.BlockSpec((queries, slots), lambda i, s: (part, 0))
+    share = pl.BlockSpec((slots, queries), lambda i, s: (0, part))
     held, width = slab.shape
     padded = -(-width // WIDE) * WIDE
     rows = queries * parts // terms
@@ -101,17 +114,20 @@
             in_specs=[share, share, pl.BlockSpec(memory_space=pltpu.HBM)]
             + [pl.BlockSpec(memory_space=pl.ANY)] * len(given),
             out_specs=[
-                pl.BlockSpec((queries, padded), lambda i, s: (0, 0)),
+                pl.BlockSpec(memory_space=pl.ANY),
                 pl.BlockSpec(span, lambda i, s: (part, 0, 0)),
                 pl.BlockSpec((kept, rows), lambda i, s: (0, 0)),
             ],
             scratch_shapes=[
+                pltpu.VMEM((queries, padded), BF16),
                 pltpu.VMEM((rows, images), F32),
                 pltpu.VMEM(slab.shape, BF16),
+                pltpu.VMEM((queries, slots), jnp.int32),
                 pltpu.VMEM((queries, slots), F32),
                 pltpu.VMEM((groups, GROUP * slots), jnp.int32),
                 pltpu.VMEM((groups, GROUP * slots), F32),
                 pltpu.SemaphoreType.DMA,
+                pltpu.SemaphoreType.DMA((4,)),
             ],
         ),
         out_shape=[
@@ -120,13 +136,13 @@
             jax.ShapeDtypeStruct((kept, rows), F32),
         ],
         input_output_aliases={} if coded is None else {4: 1},
-        compiler_params=pltpu.CompilerParams(vmem_limit_bytes=VMEM_BYTES),
+        compiler_params=pltpu.CompilerParams(vmem_limit_bytes=44 << 20),
         cost_estimate=pl.CostEstimate(flops=K1COST, bytes_accessed=1024, transcendentals=0),
         name="score_slab",
-    )(place, ids, weights, slab, *given)
-
-
-def project_kernel(counts, block, images, patches, spans, place, *refs):
+    )(place, ids, weights, pltpu.with_memory_space_constraint(slab, pltpu.HBM), *given)
+
+
+def project_kernel(counts, block, images, patches, spans, offset, place, *refs):
     groups = []
     for count in counts:
         groups.append(refs[:count])
@@ -136,67 +152,84 @@
     depth, columns = weights[0].shape[0], gathered.shape[1]
     index = place[0]
 
-    rows_in = []
-    for k, (source, start) in enumerate(zip(weights, spans)):
+    tiles = [(left, min(left + TILE, columns)) for left in range(0, columns, TILE)]
+    if columns % LANES:
+        tiles = [(0, columns)]
+
+    def fetch_rows(j, k):
+        left, right = tiles[j]
         at = pl.multiple_of(jnp.bitwise_xor(index, k) * depth, depth)
-        rows_in.append(
-            pltpu.make_async_copy(
-                source.at[:, start : start + columns], gathered.at[pl.ds(at, depth), :], came_w.at[k]
-            )
-        )
+        return pltpu.make_async_copy(
+            weights[k].at[:, spans[k] + left : spans[k] + right],
+            gathered.at[pl.ds(at, depth), left:right],
+            came_w.at[j, k],
+        )
+
+    def fetch_dense(j, k):
+        left, right = tiles[j]
+        if columns % LANES:
+            return pltpu.make_async_copy(dense[k], wide.at[k], came_d.at[j, k])
+        return pltpu.make_async_copy(
+            dense[k].at[:, offset + left : offset + right],
+            wide.at[k, :, left:right],
+            came_d.at[j, k],
+        )
+
+    for k in range(len(weights)):
+        fetch_rows(0, k).start()
     features_in, at = [], 0
     for k, source in enumerate(features):
         size = source.shape[0]
         copy = pltpu.make_async_copy(source, rows.at[at : at + size], came_f.at[k])
+        copy.start()
         features_in.append((at, copy))
         at += size
-    start, size = spans[0], wide.shape[2]
-    dense_in = [
-        pltpu.make_async_copy(source.at[:, start : start + size], wide.at[k], came_d.at[k])
-        for k, source in enumerate(dense)
-    ]
-    for copy in rows_in + [copy for _, copy in features_in] + dense_in:
-        copy.start()
-    for copy in rows_in:
-        copy.wait()
-    best = None
-    for first in range(0, rows.shape[0], block):
-        for at, copy in features_in:
-            if first <= at < first + block:
-                copy.wait()
-        held = rows[first : first + block]
-        real = held[:, 0:1].astype(F32) < jnp.inf
-        tops = []
-        for left in range(0, columns, TILE):
-            right = min(left + TILE, columns)
+    for j in range(len(tiles)):
+        if j:
+            for k in range(len(weights)):
+                fetch_rows(j, k).start()
+        for k in range(len(dense)):
+            fetch_dense(j, k).start()
+    queries, lines = out.shape[2], out.shape[1]
+    sums = [None] * len(dense)
+    for j, (left, right) in enumerate(tiles):
+        for k in range(len(weights)):
+            fetch_rows(j, k).wait()
+        best = None
+        for first in range(0, rows.shape[0], block):
+            for at, copy in features_in:
+                if not j and first <= at < first + block:
+                    copy.wait()
+            held = rows[first : first + block]
+            real = held[:, 0:1].astype(F32) < jnp.inf
             logits = jnp.dot(held, gathered[:, left:right], preferred_element_type=F32)
             logits = jnp.where(real, logits, -jnp.inf)
             logits = logits.reshape(-1, images, patches, right - left)
-            tops.append(jnp.max(jnp.max(logits, axis=0), axis=1))
-        tops = tops[0] if len(tops) == 1 else jnp.concatenate(tops, axis=1)
-        best = tops if best is None else jnp.maximum(best, tops)
-    active = jnp.log1p(jnp.maximum(best + bias[...], 0.0))
-    pooled = jnp.concatenate([active, jnp.zeros_like(active)], axis=0).astype(BF16)
-    queries, lines = out.shape[2], out.shape[1]
+            tops = jnp.max(jnp.max(logits, axis=0), axis=1)
+            best = tops if best is None else jnp.maximum(best, tops)
+        active = jnp.log1p(jnp.maximum(best + bias[:, left:right], 0.0))
+        pooled = jnp.concatenate([active, jnp.zeros_like(active)], axis=0).astype(BF16)
+        for k in range(len(dense)):
+            fetch_dense(j, k).wait()
+            part = lax.dot_general(
+                pooled, wide[k, :, left:right], ROWS_BY_ROWS, preferred_element_type=F32
+            )
+            sums[k] = part if sums[k] is None else sums[k] + part
     t = 0
-    for k, copy in enumerate(dense_in):
-        copy.wait()
-        found = lax.dot_general(
-            pooled, wide[k, :, :columns], ROWS_BY_ROWS, preferred_element_type=F32
-        )
+    for found in sums:
         for left in range(0, found.shape[1], queries):
             out[t] = running[t] + found[:lines, left : left + queries]
             t += 1
 
 
-def project(index, features, weights, spans, bias, dense, running, images, patches):
+def project(index, features, weights, spans, offset, bias, dense, running, images, patches):
     width = features[0].shape[1]
     columns = bias.shape[1]
     total = sum(f.shape[0] for f in features)
     block = 512 if total % 512 == 0 else total
     queries, padded = dense[0].shape
-    tail = spans[0] + columns >= padded - WIDE + 1 and columns % LANES
-    kept = padded - spans[0] if tail else columns
+    tail = offset + columns >= padded - WIDE + 1 and columns % LANES
+    kept = padded - offset if tail else columns
     inputs = [*features, *weights, *dense]
     local = pl.BlockSpec(memory_space=pltpu.VMEM)
     return pl.pallas_call(
@@ -207,6 +240,7 @@
             images,
             patches,
             spans,
+            offset,
         ),
         in_specs=[pl.BlockSpec(memory_space=pltpu.SMEM)]
         + [pl.BlockSpec(memory_space=pl.ANY)] * len(inputs)
@@ -217,14 +251,21 @@
             pltpu.VMEM((width, columns), BF16),
             pltpu.VMEM((len(dense), queries, kept), BF16),
             pltpu.SemaphoreType.DMA((len(features),)),
-            pltpu.SemaphoreType.DMA((len(weights),)),
-            pltpu.SemaphoreType.DMA((len(dense),)),
+            pltpu.SemaphoreType.DMA((-(-columns // TILE), len(weights))),
+            pltpu.SemaphoreType.DMA((-(-columns // TILE), len(dense))),
         ],
         out_shape=jax.ShapeDtypeStruct(running.shape, F32),
         compiler_params=pltpu.CompilerParams(vmem_limit_bytes=40 << 20),
         cost_estimate=BRIEF,
         name="project",
-    )(jnp.stack([index]).astype(jnp.int32), *inputs, bias, running)
+    )(
+        jnp.stack([index]).astype(jnp.int32),
+        *[pltpu.with_memory_space_constraint(f, pltpu.HBM) for f in features],
+        *weights,
+        *dense,
+        bias,
+        running,
+    )
 
 
 def finish_kernel(images, coded, fresh, out, table):
@@ -268,7 +309,7 @@
         return [(0, width)]
     tiles = width // LANES
     small = max(1, tiles * 2 // 15)
-    sizes = [tiles * 6 // 30, tiles - tiles * 6 // 30 - small, small]
+    sizes = [tiles * 9 // 30, tiles - tiles * 9 // 30 - small, small]
     return [(sum(sizes[:i]) * LANES, size * LANES) for i, size in enumerate(sizes)]
 
 
@@ -296,9 +337,10 @@
         return lax.optimization_barrier((value, done))[0]
 
     blocks = column_blocks(width)
-    crossed = []
+    crossed, local = [], []
     for b, (start, size) in enumerate(blocks):
         sent = proj_weight[:, start : start + size]
+        local.append(sent)
         crossed.append([to_row(sent, k) for k in range(1, rows)])
         if not b:
             patches = after(patches, sent)
@@ -306,7 +348,10 @@
     marked = jnp.where(patch_mask[:, :, None] > 0, patches, jnp.array(jnp.inf, BF16))
     marked = marked.reshape(images * patch_rows, features)
     first_x = [to_term(marked, k) for k in range(1, along_x)]
-    by_z = [to_term(marked, k * along_x) for k in range(1, along_z)]
+    by_z = []
+    for k in range(1, along_z):
+        near = k & -k
+        by_z.append(to_term(by_z[k - near - 1] if k > near else marked, near * along_x))
     second_x = [[to_term(block, k) for block in by_z] for k in range(1, along_x)]
     gathered = [marked, *by_z, *first_x]
     for blocks_x in second_x:
@@ -315,13 +360,13 @@
     place = jnp.stack([term * width]).astype(jnp.int32)
     dense, scales, coded = [], [], None
     for part in range(PARTS):
-        here = after(place, by_z, first_x, crossed[0]) if part else place
+        here = after(place, by_z[:1], first_x, [v[:1] for v in second_x], local[-1]) if part else place
         full, coded, scale = score_slab(
-            here, query_ids, term_weights, slab, terms, held + images, part, PARTS, coded
-        )
-        dense.append(full)
+            here, query_ids.T, term_weights.T, slab, terms, held + images, part, PARTS, coded
+        )
+        dense.append(pltpu.with_memory_space_constraint(full, pltpu.HBM))
         scales.append(scale[: terms // PARTS])
-    coded = after(coded, crossed[:-1], second_x)
+    coded = after(coded, crossed[:1], second_x)
     coded = lax.all_to_all(coded, "term", split_axis=0, concat_axis=0, tiled=True)
 
     scales = jnp.concatenate(scales).reshape(terms, 1, block_queries)
@@ -330,18 +375,22 @@
          jnp.zeros((terms, 7 - images, block_queries), F32)], axis=1)
     bias = proj_bias.reshape(1, width)
     beside = to_core(after(proj_weight, by_z))
-    swapped = [[to_core(part) for part in came] for came in crossed]
     for b, (start, size) in enumerate(blocks):
-        pieces = [proj_weight, beside]
-        for mine, other in zip(crossed[b], swapped[b]):
+        if not b or b < len(blocks) - 1:
+            swapped = [to_core(part) for part in crossed[b]]
+        pieces = [local[b], beside]
+        for mine, other in zip(crossed[b], swapped):
             pieces += [mine, other]
-        if 0 < b < len(blocks) - 1:
+        spans = [0, start] + [0] * (len(pieces) - 2)
+        running = project(
+            2 * row + core, gathered, pieces, spans, start, bias[:, start : start + size],
+            dense, running, images, patch_rows,
+        )
+        if b == len(blocks) - 3:
+            swapped_last = [to_core(part) for part in after(crossed[-1], running)]
             running = after(running, crossed[-1])
-        spans = [start, start] + [0] * (len(pieces) - 2)
-        running = project(
-            2 * row + core, gathered, pieces, spans, bias[:, start : start + size],
-            dense, running, images, patch_rows,
-        )
+        if b == len(blocks) - 2:
+            swapped = swapped_last
     running, coded = lax.optimization_barrier((running, coded))
     fresh = lax.all_to_all(running, "term", split_axis=0, concat_axis=0, tiled=True)
     return finish(coded, fresh, images)

time: 101 us -> 87.2 us (0.86)
  waiting for transfers between devices: 18 us -> 12 us
  local copies, waits for them, and re-layouts: 9.15 us -> 5.85 us
  starting transfers between devices: 22.8 us -> 20.3 us
  blocking collectives: 12.5 us -> 10.4 us
    ppermute x3, waiting for transfers between devices: 8.19 us -> 2.03 us  [to_row(): return lax.ppermute(value, 'row', [(i, i ^ k) for i in range(rows)])]
    pallas_call x3, Pallas kernels: 17.5 us -> 20.5 us  [project(): pl.pallas_call(functools.partial(project_kernel, (len(features), len(weig...]
    pallas_call x2, Pallas kernels: 16.1 us -> 13.4 us  [score_slab(): pl.pallas_call(score_kernel, grid_spec=pltpu.PrefetchScalarGridSpec(num_s...]
    unnamed x18 -> x20, local copies, waits for them, and re-layouts: 4.02 us -> 1.44 us
    all_to_all x1, starting transfers between devices: 6.91 us -> 4.42 us  [shards(): lax.all_to_all(coded, 'term', split_axis=0, concat_axis=0, tiled=True)]
    all_to_all x1, blocking collectives: 12.5 us -> 10.4 us  [shards(): lax.all_to_all(running, 'term', split_axis=0, concat_axis=0, tiled=True)]
    ppermute x4, waiting for transfers between devices: 0.01 us -> 1.69 us  [to_core(): return lax.ppermute(value, 'core', [(0, 1), (1, 0)])]
    ppermute x7, waiting for transfers between devices: 9.79 us -> 8.3 us  [to_term(): return lax.ppermute(value, 'term', [(i, i ^ k) for i in range(terms)])]
  transfers between devices with their start and end apart: 15 -> 15, of which waited for: 6 -> 5; matrix products, arithmetic and copies ran while one was open for 5% -> 3% of each run, Pallas kernels for 33% -> 39%
where the time goes in v3:
time: 87.2 us; the launch traced here: 86.8 us
  Pallas kernels  36.3 us (42%)
  starting transfers between devices  20.3 us (23%)
  waiting for transfers between devices  12 us (14%)
  blocking collectives  10.4 us (12%)
  local copies, waits for them, and re-layouts  5.85 us (7%)
  other arithmetic  1.81 us (2%)
    pallas_call x3, Pallas kernels, project(): pl.pallas_call(functools.partial(project_kernel, (len(features), len(weig...  20.5 us
    pallas_call x2, Pallas kernels, score_slab(): pl.pallas_call(score_kernel, grid_spec=pltpu.PrefetchScalarGridSpec(num_s...  13.4 us
    ppermute x7, starting transfers between devices, to_term(): return lax.ppermute(value, 'term', [(i, i ^ k) for i in range(terms)])  11.5 us
    all_to_all x1, blocking collectives, shards(): lax.all_to_all(running, 'term', split_axis=0, concat_axis=0, tiled=True)  10.4 us
    ppermute x7, waiting for transfers between devices, to_term(): return lax.ppermute(value, 'term', [(i, i ^ k) for i in range(terms)])  8.3 us
    all_to_all x1, starting transfers between devices, shards(): lax.all_to_all(coded, 'term', split_axis=0, concat_axis=0, tiled=True)  4.42 us
    slice x3, local copies, waits for them, and re-layouts, shards(): sent = proj_weight[:, start:start + size]  4.3 us
    ppermute x3, starting transfers between devices, to_row(): return lax.ppermute(value, 'row', [(i, i ^ k) for i in range(rows)])  3.61 us
  transfers between devices with their start and end apart: 15, of which 5 were waited for; matrix products, arithmetic and copies ran while one was open for 3% of the time, Pallas kernels for 39%

profile of v3, /device:TPU:0, one launch (start us, length us, event | category | flops | bytes accessed | tf_op | source)
XLA Modules:
  0.0 86.8 jit_solution(5262243443446895008)
XLA Ops:
  0.0 2.0 %slice.24.refs_8_ = bf16[256,1152]{1,0:T(8,128)(2,1)} slice(bf16[256,3840]{1,0:T(8,128)(2,1)} %param.9), slice={[0:256], [0:1152]} | slice | bytes 1179648 | tf_op jit(solution)/shard_map/slice | solution.py:342
  2.0 0.7 broadcast_compare_fusion
  2.7 1.0 %broadcast_select_fusion = bf16[4,32,1024]{2,1,0:T(8,128)(2,1)S(1)} fusion(bf16[4,32,1024]{2,1,0:T(8,128)(2,1)} %param.7, pred[4,32]{1,0:T(4,128)(4,1)S(1)} %broadcast_compare_fusion), kind=kLoop, calls=%fused_computation | loop fusion | flops 131072 | bytes 524416 | tf_op jit(solution)/shard_map/jit(_where)/select_n | solution.py:348
  3.7 0.0 copy-start.2
  3.7 3.1 %collective-permute-start = (bf16[128,1024]{1,0:T(8,128)(2,1)S(1)}, bf16[128,1024]{1,0:T(8,128)(2,1)S(1)}, u32[]{:S(2)}, u32[]{:S(2)}) collective-permute-start(bf16[128,1024]{1,0:T(8,128)(2,1)S(1)} %bitcast.10), channel_id=1, source_target_pairs={{0,2},{1,3},{2,0},{3,1},{4,6},{5,7},{6,4},{7,5},{8,10},{9,11},{10,... | collective-permute-start | bytes 786440 | tf_op jit(solution)/shard_map/ppermute | solution.py:328
  6.8 2.6 %collective-permute-start.1 = (bf16[128,1024]{1,0:T(8,128)(2,1)S(1)}, bf16[128,1024]{1,0:T(8,128)(2,1)}, u32[]{:S(2)}, u32[]{:S(2)}) collective-permute-start(bf16[128,1024]{1,0:T(8,128)(2,1)S(1)} %bitcast.11), channel_id=1, source_target_pairs={{0,4},{1,5},{2,6},{3,7},{4,0},{5,1},{6,2},{7,3},{8,12},{9,13},{10,... | collective-permute-start | bytes 786440 | tf_op jit(solution)/shard_map/ppermute | solution.py:328
  9.4 1.5 %collective-permute-start.3 = (bf16[128,1024]{1,0:T(8,128)(2,1)S(1)}, bf16[128,1024]{1,0:T(8,128)(2,1)S(1)}, u32[]{:S(2)}, u32[]{:S(2)}) collective-permute-start(bf16[128,1024]{1,0:T(8,128)(2,1)S(1)} %bitcast.12), channel_id=1, source_target_pairs={{0,1},{1,0},{2,3},{3,2},{4,5},{5,4},{6,7},{7,6},{8,9},{9,8},{10,11... | collective-permute-start | bytes 786440 | tf_op jit(solution)/shard_map/ppermute | solution.py:328
  10.9 1.5 %collective-permute-start.9 = (bf16[256,1152]{1,0:T(8,128)(2,1)}, bf16[256,1152]{1,0:T(8,128)(2,1)}, u32[]{:S(2)}, u32[]{:S(2)}) collective-permute-start(bf16[256,1152]{1,0:T(8,128)(2,1)} %slice.24.refs_8_), channel_id=1, source_target_pairs={{0,16},{16,0},{1,17},{17,1},{2,18},{18,2},{3,19},{19,3},{4,20},{20... | collective-permute-start | bytes 1769480 | tf_op jit(solution)/shard_map/ppermute | solution.py:331
  12.4 1.3 %slice.30.refs_8_ = bf16[256,2176]{1,0:T(8,128)(2,1)S(1)} slice(bf16[256,3840]{1,0:T(8,128)(2,1)} %param.9), slice={[0:256], [1152:3328]} | slice | bytes 2228224 | tf_op jit(solution)/shard_map/slice | solution.py:342
  13.8 0.6 collective-permute-start.12
  14.3 4.3 %collective-permute-done.refs_1_ = bf16[128,1024]{1,0:T(8,128)(2,1)S(1)} collective-permute-done((bf16[128,1024]{1,0:T(8,128)(2,1)S(1)}, bf16[128,1024]{1,0:T(8,128)(2,1)S(1)}, u32[]{:S(2)}, u32[]{:S(2)}) %collective-permute-start) | collective-permute-done | bytes 262176 | tf_op jit(solution)/shard_map/ppermute | solution.py:328
  18.6 1.7 %collective-permute-start.4 = (bf16[128,1024]{1,0:T(8,128)(2,1)S(1)}, bf16[128,1024]{1,0:T(8,128)(2,1)S(1)}, u32[]{:S(2)}, u32[]{:S(2)}) collective-permute-start(bf16[128,1024]{1,0:T(8,128)(2,1)S(1)} %collective-permute-done.refs_1_), channel_id=1, source_target_pairs={{0,1},{1,0},{2,3},{3,2},{4,5},{5,4},{6,7},{7,6},{8,9},{9,8},{10,11... | collective-permute-start | bytes 786440 | tf_op jit(solution)/shard_map/ppermute | solution.py:328
  20.3 1.0 %collective-permute-done.1.refs_2_ = bf16[128,1024]{1,0:T(8,128)(2,1)} collective-permute-done((bf16[128,1024]{1,0:T(8,128)(2,1)S(1)}, bf16[128,1024]{1,0:T(8,128)(2,1)}, u32[]{:S(2)}, u32[]{:S(2)}) %collective-permute-start.1) | collective-permute-done | bytes 262176 | tf_op jit(solution)/shard_map/ppermute | solution.py:328
  21.3 0.4 collective-permute-start.2
  21.7 6.7 %score_slab.2 = (bf16[512,3840]{1,0:T(8,128)(2,1)}, s16[8,128,512]{2,1,0:T(8,128)(2,1)}, f32[8,128]{1,0:T(8,128)S(1)}) custom-call(s32[1]{0:T(128)} %bitcast.2.place, s32[32,1024]{1,0:T(8,128)S(1)} %bitcast.6, bf16[32,1024]{1,0:T(8,128)(2,1)S(1)} %bitcast.8, bf16[508,3840]{1,0:T(8,128)(2,1)} %slab.3), custom_call_target="tpu_custom_call" | custom-call | flops 13958643712 | bytes 1024 | tf_op jit(solution)/shard_map/score_slab/pallas_call | solution.py:109
  28.4 1.0 %slice.25.refs_8_ = bf16[256,512]{1,0:T(8,128)(2,1)S(1)} slice(bf16[256,3840]{1,0:T(8,128)(2,1)} %param.9), slice={[0:256], [3328:3840]} | slice | bytes 524288 | tf_op jit(solution)/shard_map/slice | solution.py:342
  29.4 0.0 collective-permute-done.3.refs_4_
  29.4 1.6 %collective-permute-start.5 = (bf16[128,1024]{1,0:T(8,128)(2,1)}, bf16[128,1024]{1,0:T(8,128)(2,1)S(1)}, u32[]{:S(2)}, u32[]{:S(2)}) collective-permute-start(bf16[128,1024]{1,0:T(8,128)(2,1)} %collective-permute-done.1.refs_2_), channel_id=1, source_target_pairs={{0,1},{1,0},{2,3},{3,2},{4,5},{5,4},{6,7},{7,6},{8,9},{9,8},{10,11... | collective-permute-start | bytes 786440 | tf_op jit(solution)/shard_map/ppermute | solution.py:328
  31.0 0.0 collective-permute-done.4.refs_5_
  31.0 0.7 copy-done.5
  31.7 0.0 collective-permute-done.2.refs_3_
  31.7 0.0 collective-permute-start.7
  31.7 0.7 collective-permute-start.6
  32.4 6.7 %score_slab.3 = (bf16[512,3840]{1,0:T(8,128)(2,1)}, s16[8,128,512]{2,1,0:T(8,128)(2,1)}, f32[8,128]{1,0:T(8,128)S(1)}) custom-call(s32[1]{0:T(128)} %bitcast.2.place, s32[32,1024]{1,0:T(8,128)S(1)} %bitcast.7, bf16[32,1024]{1,0:T(8,128)(2,1)S(1)} %bitcast.9, bf16[508,3840]{1,0:T(8,128)(2,1)} %slab.3, ...), custom_call_target="tpu_custom_call", output_to_operand_aliasing={{1}: (4, {})} | custom-call | flops 13958643712 | bytes 1024 | tf_op jit(solution)/shard_map/score_slab/pallas_call | solution.py:109
  39.1 0.0 copy-start.9
  39.1 0.0 collective-permute-done.5.refs_6_
  39.2 0.0 collective-permute-done.9.refs_10_
  39.2 3.0 %collective-permute-done.6.refs_7_ = bf16[128,1024]{1,0:T(8,128)(2,1)S(1)} collective-permute-done((bf16[128,1024]{1,0:T(8,128)(2,1)S(1)}, bf16[128,1024]{1,0:T(8,128)(2,1)S(1)}, u32[]{:S(2)}, u32[]{:S(2)}) %collective-permute-start.6) | collective-permute-done | bytes 262176 | tf_op jit(solution)/shard_map/ppermute | solution.py:328
  42.2 0.7 copy-done.8
  42.9 4.4 %all-to-all-start = ((s16[8,128,512]{2,1,0:T(8,128)(2,1)}), s16[8,128,512]{2,1,0:T(8,128)(2,1)}, u32[]{:S(2)}, u32[]{:S(2)}) async-start(s16[8,128,512]{2,1,0:T(8,128)(2,1)} %get-tuple-element.30), calls=%async_computation | async-start | bytes 2097152 | tf_op jit(solution)/shard_map/all_to_all | solution.py:370
  47.3 2.0 %collective-permute-done.12.refs_10_ = bf16[256,2176]{1,0:T(8,128)(2,1)} collective-permute-done((bf16[256,2176]{1,0:T(8,128)(2,1)S(1)}, bf16[256,2176]{1,0:T(8,128)(2,1)}, u32[]{:S(2)}, u32[]{:S(2)}) %collective-permute-start.12) | collective-permute-done | bytes 1114144 | tf_op jit(solution)/shard_map/ppermute | solution.py:331
  49.3 0.0 collective-permute-start.13
  49.3 0.5 collective-permute-start.10
  49.9 1.5 %collective-permute-start.8 = (bf16[256,512]{1,0:T(8,128)(2,1)S(1)}, bf16[256,512]{1,0:T(8,128)(2,1)}, u32[]{:S(2)}, u32[]{:S(2)}) collective-permute-start(bf16[256,512]{1,0:T(8,128)(2,1)S(1)} %slice.25.refs_8_), channel_id=1, source_target_pairs={{0,16},{16,0},{1,17},{17,1},{2,18},{18,2},{3,19},{19,3},{4,20},{20... | collective-permute-start | bytes 786440 | tf_op jit(solution)/shard_map/ppermute | solution.py:331
  51.4 0.1 pad.2.clone
  51.5 0.1 maximum_maximum_fusion.refs_15_
  51.6 1.7 %collective-permute-done.10.refs_11_ = bf16[256,1152]{1,0:T(8,128)(2,1)} collective-permute-done((bf16[256,1152]{1,0:T(8,128)(2,1)}, bf16[256,1152]{1,0:T(8,128)(2,1)}, u32[]{:S(2)}, u32[]{:S(2)}) %collective-permute-start.10) | collective-permute-done | bytes 589856 | tf_op jit(solution)/shard_map/ppermute | solution.py:334
  53.3 0.0 collective-permute-done.7.refs_9_
  53.3 6.7 %project.3.refs_15_ = f32[8,8,128]{2,1,0:T(8,128)S(1)} custom-call(s32[1]{0:T(128)} %bitcast.place, bf16[128,1024]{1,0:T(8,128)(2,1)} %bitcast.13, bf16[128,1024]{1,0:T(8,128)(2,1)} %copy-done.3, bf16[128,1024]{1,0:T(8,128)(2,1)} %collective-permute-done.1.refs_2_, bf16[128,1024]{1,0:T(8,128)(2,1)} %copy-done.6, bf16[128,1024]{1,0:T(8,128)(2,1)} %copy-done.4, ...), custom_call_target="tpu_custom_call" | custom-call | flops 1024 | bytes 1024 | tf_op jit(solution)/shard_map/project/pallas_call | solution.py:235
  60.0 0.0 collective-permute-done.8.refs_10_
  60.0 0.2 collective-permute-start.11
  60.2 0.0 collective-permute-done.13.refs_11_
  60.2 10.5 %project.4.refs_15_ = f32[8,8,128]{2,1,0:T(8,128)S(1)} custom-call(s32[1]{0:T(128)} %bitcast.place, bf16[128,1024]{1,0:T(8,128)(2,1)} %bitcast.14, bf16[128,1024]{1,0:T(8,128)(2,1)} %copy-done.3, bf16[128,1024]{1,0:T(8,128)(2,1)} %collective-permute-done.1.refs_2_, bf16[128,1024]{1,0:T(8,128)(2,1)} %copy-done.6, bf16[128,1024]{1,0:T(8,128)(2,1)} %copy-done.4, ...), custom_call_target="tpu_custom_call" | custom-call | flops 1024 | bytes 1024 | tf_op jit(solution)/shard_map/project/pallas_call | solution.py:235
  70.7 0.0 collective-permute-done.11.refs_11_
  70.7 3.4 %project.5 = f32[8,8,128]{2,1,0:T(8,128)S(1)} custom-call(s32[1]{0:T(128)} %bitcast.place, bf16[128,1024]{1,0:T(8,128)(2,1)} %bitcast.15, bf16[128,1024]{1,0:T(8,128)(2,1)} %copy-done.3, bf16[128,1024]{1,0:T(8,128)(2,1)} %collective-permute-done.1.refs_2_, bf16[128,1024]{1,0:T(8,128)(2,1)} %copy-done.6, bf16[128,1024]{1,0:T(8,128)(2,1)} %copy-done.4, ...), custom_call_target="tpu_custom_call" | custom-call | flops 1024 | bytes 1024 | tf_op jit(solution)/shard_map/project/pallas_call | solution.py:235
  74.1 0.0 all-to-all-done.coded
  74.1 10.4 %all_to_all.10.fresh = f32[8,8,128]{2,1,0:T(8,128)S(1)} all-to-all(f32[8,8,128]{2,1,0:T(8,128)S(1)} %project.5), channel_id=1, replica_groups=mesh['row'=2,'core'=2,'term'=8] {'term'}, dimensions={0} | all-to-all | bytes 65536 | tf_op jit(solution)/shard_map/all_to_all | solution.py:395
  84.5 2.4 %finish.1 = f32[128,512]{1,0:T(8,128)} custom-call(s16[8,128,512]{2,1,0:T(8,128)(2,1)} %all-to-all-done.coded, f32[8,8,128]{2,1,0:T(8,128)S(1)} %all_to_all.10.fresh), custom_call_target="tpu_custom_call" | custom-call | flops 1024 | bytes 1024 | tf_op jit(solution)/shard_map/finish/pallas_call | solution.py:295
  (26 shorter events, 0.1 us)
Async XLA Ops:
  0.0 21.7 %copy-start = (s32[1024,32]{0,1:T(8,128)S(1)}, s32[1024,32]{0,1:T(8,128)}, u32[]{:S(2)}) copy-start(s32[1024,32]{0,1:T(8,128)} %param.12) | copy-start | bytes 393220
  0.0 21.7 %copy-start.1 = (bf16[1024,32]{0,1:T(8,128)(2,1)S(1)}, bf16[1024,32]{0,1:T(8,128)(2,1)}, u32[]{:S(2)}) copy-start(bf16[1024,32]{0,1:T(8,128)(2,1)} %param.13) | copy-start | bytes 196612
  3.7 24.7 %copy-start.2 = (bf16[4,32,1024]{2,1,0:T(8,128)(2,1)}, bf16[4,32,1024]{2,1,0:T(8,128)(2,1)S(1)}, u32[]{:S(2)}) copy-start(bf16[4,32,1024]{2,1,0:T(8,128)(2,1)S(1)} %broadcast_select_fusion) | copy-start | bytes 786436
  3.7 14.9 %collective-permute-start = (bf16[128,1024]{1,0:T(8,128)(2,1)S(1)}, bf16[128,1024]{1,0:T(8,128)(2,1)S(1)}, u32[]{:S(2)}, u32[]{:S(2)}) collective-permute-start(bf16[128,1024]{1,0:T(8,128)(2,1)S(1)} %bitcast.10), channel_id=1, source_target_pairs={{0,2},{1,3},{2,0},{3,1},{4,6},{5,7},{6,4},{7,5},{8,10},{9,11},{10,... | collective-permute-start | bytes 786440 | tf_op jit(solution)/shard_map/ppermute | solution.py:328
  6.8 14.4 %collective-permute-start.1 = (bf16[128,1024]{1,0:T(8,128)(2,1)S(1)}, bf16[128,1024]{1,0:T(8,128)(2,1)}, u32[]{:S(2)}, u32[]{:S(2)}) collective-permute-start(bf16[128,1024]{1,0:T(8,128)(2,1)S(1)} %bitcast.11), channel_id=1, source_target_pairs={{0,4},{1,5},{2,6},{3,7},{4,0},{5,1},{6,2},{7,3},{8,12},{9,13},{10,... | collective-permute-start | bytes 786440 | tf_op jit(solution)/shard_map/ppermute | solution.py:328
  9.4 20.0 %collective-permute-start.3 = (bf16[128,1024]{1,0:T(8,128)(2,1)S(1)}, bf16[128,1024]{1,0:T(8,128)(2,1)S(1)}, u32[]{:S(2)}, u32[]{:S(2)}) collective-permute-start(bf16[128,1024]{1,0:T(8,128)(2,1)S(1)} %bitcast.12), channel_id=1, source_target_pairs={{0,1},{1,0},{2,3},{3,2},{4,5},{5,4},{6,7},{7,6},{8,9},{9,8},{10,11... | collective-permute-start | bytes 786440 | tf_op jit(solution)/shard_map/ppermute | solution.py:328
  10.9 28.2 %collective-permute-start.9 = (bf16[256,1152]{1,0:T(8,128)(2,1)}, bf16[256,1152]{1,0:T(8,128)(2,1)}, u32[]{:S(2)}, u32[]{:S(2)}) collective-permute-start(bf16[256,1152]{1,0:T(8,128)(2,1)} %slice.24.refs_8_), channel_id=1, source_target_pairs={{0,16},{16,0},{1,17},{17,1},{2,18},{18,2},{3,19},{19,3},{4,20},{20... | collective-permute-start | bytes 1769480 | tf_op jit(solution)/shard_map/ppermute | solution.py:331
  13.8 35.6 %collective-permute-start.12 = (bf16[256,2176]{1,0:T(8,128)(2,1)S(1)}, bf16[256,2176]{1,0:T(8,128)(2,1)}, u32[]{:S(2)}, u32[]{:S(2)}) collective-permute-start(bf16[256,2176]{1,0:T(8,128)(2,1)S(1)} %slice.30.refs_8_), channel_id=1, source_target_pairs={{0,16},{16,0},{1,17},{17,1},{2,18},{18,2},{3,19},{19,3},{4,20},{20... | collective-permute-start | bytes 3342344 | tf_op jit(solution)/shard_map/ppermute | solution.py:331
  18.6 9.8 %copy-start.3 = (bf16[128,1024]{1,0:T(8,128)(2,1)}, bf16[128,1024]{1,0:T(8,128)(2,1)S(1)}, u32[]{:S(2)}) copy-start(bf16[128,1024]{1,0:T(8,128)(2,1)S(1)} %collective-permute-done.refs_1_) | copy-start | bytes 786436
  18.6 12.4 %collective-permute-start.4 = (bf16[128,1024]{1,0:T(8,128)(2,1)S(1)}, bf16[128,1024]{1,0:T(8,128)(2,1)S(1)}, u32[]{:S(2)}, u32[]{:S(2)}) collective-permute-start(bf16[128,1024]{1,0:T(8,128)(2,1)S(1)} %collective-permute-done.refs_1_), channel_id=1, source_target_pairs={{0,1},{1,0},{2,3},{3,2},{4,5},{5,4},{6,7},{7,6},{8,9},{9,8},{10,11... | collective-permute-start | bytes 786440 | tf_op jit(solution)/shard_map/ppermute | solution.py:328
  21.3 10.4 %collective-permute-start.2 = (bf16[128,1024]{1,0:T(8,128)(2,1)}, bf16[128,1024]{1,0:T(8,128)(2,1)S(1)}, u32[]{:S(2)}, u32[]{:S(2)}) collective-permute-start(bf16[128,1024]{1,0:T(8,128)(2,1)} %collective-permute-done.1.refs_2_), channel_id=1, source_target_pairs={{0,2},{1,3},{2,0},{3,1},{4,6},{5,7},{6,4},{7,5},{8,10},{9,11},{10,... | collective-permute-start | bytes 786440 | tf_op jit(solution)/shard_map/ppermute | solution.py:328
  29.4 1.6 %copy-start.4 = (bf16[128,1024]{1,0:T(8,128)(2,1)}, bf16[128,1024]{1,0:T(8,128)(2,1)S(1)}, u32[]{:S(2)}) copy-start(bf16[128,1024]{1,0:T(8,128)(2,1)S(1)} %collective-permute-done.3.refs_4_) | copy-start | bytes 786436
  29.4 9.7 %collective-permute-start.5 = (bf16[128,1024]{1,0:T(8,128)(2,1)}, bf16[128,1024]{1,0:T(8,128)(2,1)S(1)}, u32[]{:S(2)}, u32[]{:S(2)}) collective-permute-start(bf16[128,1024]{1,0:T(8,128)(2,1)} %collective-permute-done.1.refs_2_), channel_id=1, source_target_pairs={{0,1},{1,0},{2,3},{3,2},{4,5},{5,4},{6,7},{7,6},{8,9},{9,8},{10,11... | collective-permute-start | bytes 786440 | tf_op jit(solution)/shard_map/ppermute | solution.py:328
  31.0 0.7 copy-start.5
  31.7 7.4 %copy-start.6 = (bf16[128,1024]{1,0:T(8,128)(2,1)}, bf16[128,1024]{1,0:T(8,128)(2,1)S(1)}, u32[]{:S(2)}) copy-start(bf16[128,1024]{1,0:T(8,128)(2,1)S(1)} %collective-permute-done.2.refs_3_) | copy-start | bytes 786436
  31.7 21.6 %collective-permute-start.7 = (bf16[256,3840]{1,0:T(8,128)(2,1)}, bf16[256,3840]{1,0:T(8,128)(2,1)S(1)}, u32[]{:S(2)}, u32[]{:S(2)}) collective-permute-start(bf16[256,3840]{1,0:T(8,128)(2,1)} %param.9), channel_id=1, source_target_pairs={{0,8},{8,0},{1,9},{9,1},{2,10},{10,2},{3,11},{11,3},{4,12},{12,4},... | collective-permute-start | bytes 5898248 | tf_op jit(solution)/shard_map/ppermute | solution.py:334
  31.7 10.5 %collective-permute-start.6 = (bf16[128,1024]{1,0:T(8,128)(2,1)S(1)}, bf16[128,1024]{1,0:T(8,128)(2,1)S(1)}, u32[]{:S(2)}, u32[]{:S(2)}) collective-permute-start(bf16[128,1024]{1,0:T(8,128)(2,1)S(1)} %collective-permute-done.2.refs_3_), channel_id=1, source_target_pairs={{0,1},{1,0},{2,3},{3,2},{4,5},{5,4},{6,7},{7,6},{8,9},{9,8},{10,11... | collective-permute-start | bytes 786440 | tf_op jit(solution)/shard_map/ppermute | solution.py:328
  39.1 12.3 %copy-start.9 = (f32[3840]{0:T(1024)S(1)}, f32[3840]{0:T(1024)}, u32[]{:S(2)}) copy-start(f32[3840]{0:T(1024)} %param.10) | copy-start | bytes 46084
  39.1 3.0 %copy-start.7 = (bf16[128,1024]{1,0:T(8,128)(2,1)}, bf16[128,1024]{1,0:T(8,128)(2,1)S(1)}, u32[]{:S(2)}) copy-start(bf16[128,1024]{1,0:T(8,128)(2,1)S(1)} %collective-permute-done.5.refs_6_) | copy-start | bytes 786436
  42.2 0.7 copy-start.8
  42.9 31.2 %all-to-all-start = ((s16[8,128,512]{2,1,0:T(8,128)(2,1)}), s16[8,128,512]{2,1,0:T(8,128)(2,1)}, u32[]{:S(2)}, u32[]{:S(2)}) async-start(s16[8,128,512]{2,1,0:T(8,128)(2,1)} %get-tuple-element.30), calls=%async_computation | async-start | bytes 2097152 | tf_op jit(solution)/shard_map/all_to_all | solution.py:370
  49.3 10.9 %collective-permute-start.13 = (bf16[256,2176]{1,0:T(8,128)(2,1)}, bf16[256,2176]{1,0:T(8,128)(2,1)}, u32[]{:S(2)}, u32[]{:S(2)}) collective-permute-start(bf16[256,2176]{1,0:T(8,128)(2,1)} %collective-permute-done.12.refs_10_), channel_id=1, source_target_pairs={{0,8},{8,0},{1,9},{9,1},{2,10},{10,2},{3,11},{11,3},{4,12},{12,4},... | collective-permute-start | bytes 3342344 | tf_op jit(solution)/shard_map/ppermute | solution.py:334
  49.3 3.9 %collective-permute-start.10 = (bf16[256,1152]{1,0:T(8,128)(2,1)}, bf16[256,1152]{1,0:T(8,128)(2,1)}, u32[]{:S(2)}, u32[]{:S(2)}) collective-permute-start(bf16[256,1152]{1,0:T(8,128)(2,1)} %collective-permute-done.9.refs_10_), channel_id=1, source_target_pairs={{0,8},{8,0},{1,9},{9,1},{2,10},{10,2},{3,11},{11,3},{4,12},{12,4},... | collective-permute-start | bytes 1769480 | tf_op jit(solution)/shard_map/ppermute | solution.py:334
  49.9 10.1 %collective-permute-start.8 = (bf16[256,512]{1,0:T(8,128)(2,1)S(1)}, bf16[256,512]{1,0:T(8,128)(2,1)}, u32[]{:S(2)}, u32[]{:S(2)}) collective-permute-start(bf16[256,512]{1,0:T(8,128)(2,1)S(1)} %slice.25.refs_8_), channel_id=1, source_target_pairs={{0,16},{16,0},{1,17},{17,1},{2,18},{18,2},{3,19},{19,3},{4,20},{20... | collective-permute-start | bytes 786440 | tf_op jit(solution)/shard_map/ppermute | solution.py:331
  60.0 10.7 %collective-permute-start.11 = (bf16[256,512]{1,0:T(8,128)(2,1)}, bf16[256,512]{1,0:T(8,128)(2,1)S(1)}, u32[]{:S(2)}, u32[]{:S(2)}) collective-permute-start(bf16[256,512]{1,0:T(8,128)(2,1)} %collective-permute-done.8.refs_10_), channel_id=1, source_target_pairs={{0,8},{8,0},{1,9},{9,1},{2,10},{10,2},{3,11},{11,3},{4,12},{12,4},... | collective-permute-start | bytes 786440 | tf_op jit(solution)/shard_map/ppermute | solution.py:334

commit v4 on v3

--- a/solution.py
+++ b/solution.py
@@ -17,7 +17,7 @@
 LEVELS, OFFSET, TINY = 65535.0, 32768, 1e-30
 PARTS = 2
 K1COST = 13 << 30
-TILE = 768
+TILE = 1152
 BRIEF = pl.CostEstimate(flops=1024, bytes_accessed=1024, transcendentals=0)
 
 
@@ -175,46 +175,68 @@
             came_d.at[j, k],
         )
 
-    for k in range(len(weights)):
-        fetch_rows(0, k).start()
+    def start_features(first):
+        for at, copy in features_in:
+            if first <= at < first + block:
+                copy.start()
+
     features_in, at = [], 0
     for k, source in enumerate(features):
         size = source.shape[0]
         copy = pltpu.make_async_copy(source, rows.at[at : at + size], came_f.at[k])
-        copy.start()
         features_in.append((at, copy))
         at += size
-    for j in range(len(tiles)):
-        if j:
-            for k in range(len(weights)):
-                fetch_rows(j, k).start()
-        for k in range(len(dense)):
-            fetch_dense(j, k).start()
+    for k in range(len(weights)):
+        fetch_rows(0, k).start()
+    start_features(0)
     queries, lines = out.shape[2], out.shape[1]
     sums = [None] * len(dense)
+
+    def score(j, pooled):
+        left, right = tiles[j]
+        for k in range(len(dense)):
+            part = lax.dot_general(
+                pooled, wide[k, :, left:right], ROWS_BY_ROWS, preferred_element_type=F32
+            )
+            sums[k] = part if sums[k] is None else sums[k] + part
+
+    pooled = None
     for j, (left, right) in enumerate(tiles):
         for k in range(len(weights)):
             fetch_rows(j, k).wait()
+        if j:
+            for k in range(len(dense)):
+                fetch_dense(j - 1, k).wait()
         best = None
         for first in range(0, rows.shape[0], block):
             for at, copy in features_in:
                 if not j and first <= at < first + block:
                     copy.wait()
+            if not first:
+                if not j:
+                    for later in range(block, rows.shape[0], block):
+                        start_features(later)
+                    for k in range(len(dense)):
+                        fetch_dense(0, k).start()
+                if j + 1 < len(tiles):
+                    for k in range(len(weights)):
+                        fetch_rows(j + 1, k).start()
+                    for k in range(len(dense)):
+                        fetch_dense(j + 1, k).start()
             held = rows[first : first + block]
             real = held[:, 0:1].astype(F32) < jnp.inf
             logits = jnp.dot(held, gathered[:, left:right], preferred_element_type=F32)
+            if j and not first:
+                score(j - 1, pooled)
             logits = jnp.where(real, logits, -jnp.inf)
             logits = logits.reshape(-1, images, patches, right - left)
             tops = jnp.max(jnp.max(logits, axis=0), axis=1)
             best = tops if best is None else jnp.maximum(best, tops)
         active = jnp.log1p(jnp.maximum(best + bias[:, left:right], 0.0))
         pooled = jnp.concatenate([active, jnp.zeros_like(active)], axis=0).astype(BF16)
-        for k in range(len(dense)):
-            fetch_dense(j, k).wait()
-            part = lax.dot_general(
-                pooled, wide[k, :, left:right], ROWS_BY_ROWS, preferred_element_type=F32
-            )
-            sums[k] = part if sums[k] is None else sums[k] + part
+    for k in range(len(dense)):
+        fetch_dense(len(tiles) - 1, k).wait()
+    score(len(tiles) - 1, pooled)
     t = 0
     for found in sums:
         for left in range(0, found.shape[1], queries):
@@ -268,8 +290,11 @@
     )
 
 
-def finish_kernel(images, coded, fresh, out, table):
+def finish_kernel(images, coded, fresh, out, table, held, came):
     terms, queries, _ = coded.shape
+    copies = [pltpu.make_async_copy(coded.at[t], held.at[t], came.at[t]) for t in range(terms)]
+    for copy in copies:
+        copy.start()
     total = None
     for t in range(fresh.shape[0]):
         part = fresh[t]
@@ -281,7 +306,8 @@
     columns = jnp.swapaxes(table[...], 0, 1)[:queries]
     stored = None
     for t in range(terms):
-        part = (coded[t].astype(jnp.int32) + OFFSET).astype(F32) * columns[:, t : t + 1]
+        copies[t].wait()
+        part = (held[t].astype(jnp.int32) + OFFSET).astype(F32) * columns[:, t : t + 1]
         stored = part if stored is None else stored + part
     out[...] = stored
     tail = out.shape[1] - LANES
@@ -290,13 +316,17 @@
 
 
 def finish(coded, fresh, images):
-    _, queries, total = coded.shape
+    terms, queries, total = coded.shape
     local = pl.BlockSpec(memory_space=pltpu.VMEM)
     return pl.pallas_call(
         functools.partial(finish_kernel, images),
-        in_specs=[local, local],
+        in_specs=[pl.BlockSpec(memory_space=pl.ANY), local],
         out_specs=local,
-        scratch_shapes=[pltpu.VMEM((LANES, LANES), F32)],
+        scratch_shapes=[
+            pltpu.VMEM((LANES, LANES), F32),
+            pltpu.VMEM(coded.shape, jnp.int16),
+            pltpu.SemaphoreType.DMA((terms,)),
+        ],
         out_shape=jax.ShapeDtypeStruct((queries, total), F32),
         compiler_params=pltpu.CompilerParams(vmem_limit_bytes=16 << 20),
         cost_estimate=BRIEF,

time: 87.2 us -> 86.3 us (0.990)
  Pallas kernels: 36.3 us -> 35.1 us
    pallas_call x3, Pallas kernels: 20.5 us -> 19.3 us  [project(): pl.pallas_call(functools.partial(project_kernel, (len(features), len(weig...]
  transfers between devices with their start and end apart: 15 -> 15, of which waited for: 5 -> 5; matrix products, arithmetic and copies ran while one was open for 3% -> 3% of each run, Pallas kernels for 39% -> 38%
where the time goes in v4:
time: 86.3 us; the launch traced here: 85.8 us
  Pallas kernels  35.1 us (41%)
  starting transfers between devices  20.3 us (24%)
  waiting for transfers between devices  12 us (14%)
  blocking collectives  10.4 us (12%)
  local copies, waits for them, and re-layouts  5.85 us (7%)
  other arithmetic  1.81 us (2%)
    pallas_call x3, Pallas kernels, project(): pl.pallas_call(functools.partial(project_kernel, (len(features), len(weig...  19.3 us
    pallas_call x2, Pallas kernels, score_slab(): pl.pallas_call(score_kernel, grid_spec=pltpu.PrefetchScalarGridSpec(num_s...  13.4 us
    ppermute x7, starting transfers between devices, to_term(): return lax.ppermute(value, 'term', [(i, i ^ k) for i in range(terms)])  11.5 us
    all_to_all x1, blocking collectives, shards(): lax.all_to_all(running, 'term', split_axis=0, concat_axis=0, tiled=True)  10.4 us
    ppermute x7, waiting for transfers between devices, to_term(): return lax.ppermute(value, 'term', [(i, i ^ k) for i in range(terms)])  8.3 us
    all_to_all x1, starting transfers between devices, shards(): lax.all_to_all(coded, 'term', split_axis=0, concat_axis=0, tiled=True)  4.42 us
    slice x3, local copies, waits for them, and re-layouts, shards(): sent = proj_weight[:, start:start + size]  4.3 us
    ppermute x3, starting transfers between devices, to_row(): return lax.ppermute(value, 'row', [(i, i ^ k) for i in range(rows)])  3.61 us
  transfers between devices with their start and end apart: 15, of which 5 were waited for; matrix products, arithmetic and copies ran while one was open for 3% of the time, Pallas kernels for 38%

profile of v4, /device:TPU:0, one launch (start us, length us, event | category | flops | bytes accessed | tf_op | source)
XLA Modules:
  0.0 85.8 jit_solution(953163340318507589)
XLA Ops:
  0.0 2.0 %slice.24.refs_8_ = bf16[256,1152]{1,0:T(8,128)(2,1)} slice(bf16[256,3840]{1,0:T(8,128)(2,1)} %param.9), slice={[0:256], [0:1152]} | slice | bytes 1179648 | tf_op jit(solution)/shard_map/slice | solution.py:372
  2.0 0.7 broadcast_compare_fusion
  2.7 1.0 %broadcast_select_fusion = bf16[4,32,1024]{2,1,0:T(8,128)(2,1)S(1)} fusion(bf16[4,32,1024]{2,1,0:T(8,128)(2,1)} %param.7, pred[4,32]{1,0:T(4,128)(4,1)S(1)} %broadcast_compare_fusion), kind=kLoop, calls=%fused_computation | loop fusion | flops 131072 | bytes 524416 | tf_op jit(solution)/shard_map/jit(_where)/select_n | solution.py:378
  3.7 0.0 copy-start.2
  3.7 3.1 %collective-permute-start = (bf16[128,1024]{1,0:T(8,128)(2,1)S(1)}, bf16[128,1024]{1,0:T(8,128)(2,1)S(1)}, u32[]{:S(2)}, u32[]{:S(2)}) collective-permute-start(bf16[128,1024]{1,0:T(8,128)(2,1)S(1)} %bitcast.10), channel_id=1, source_target_pairs={{0,2},{1,3},{2,0},{3,1},{4,6},{5,7},{6,4},{7,5},{8,10},{9,11},{10,... | collective-permute-start | bytes 786440 | tf_op jit(solution)/shard_map/ppermute | solution.py:358
  6.8 2.6 %collective-permute-start.1 = (bf16[128,1024]{1,0:T(8,128)(2,1)S(1)}, bf16[128,1024]{1,0:T(8,128)(2,1)}, u32[]{:S(2)}, u32[]{:S(2)}) collective-permute-start(bf16[128,1024]{1,0:T(8,128)(2,1)S(1)} %bitcast.11), channel_id=1, source_target_pairs={{0,4},{1,5},{2,6},{3,7},{4,0},{5,1},{6,2},{7,3},{8,12},{9,13},{10,... | collective-permute-start | bytes 786440 | tf_op jit(solution)/shard_map/ppermute | solution.py:358
  9.4 1.5 %collective-permute-start.3 = (bf16[128,1024]{1,0:T(8,128)(2,1)S(1)}, bf16[128,1024]{1,0:T(8,128)(2,1)S(1)}, u32[]{:S(2)}, u32[]{:S(2)}) collective-permute-start(bf16[128,1024]{1,0:T(8,128)(2,1)S(1)} %bitcast.12), channel_id=1, source_target_pairs={{0,1},{1,0},{2,3},{3,2},{4,5},{5,4},{6,7},{7,6},{8,9},{9,8},{10,11... | collective-permute-start | bytes 786440 | tf_op jit(solution)/shard_map/ppermute | solution.py:358
  10.9 1.5 %collective-permute-start.9 = (bf16[256,1152]{1,0:T(8,128)(2,1)}, bf16[256,1152]{1,0:T(8,128)(2,1)}, u32[]{:S(2)}, u32[]{:S(2)}) collective-permute-start(bf16[256,1152]{1,0:T(8,128)(2,1)} %slice.24.refs_8_), channel_id=1, source_target_pairs={{0,16},{16,0},{1,17},{17,1},{2,18},{18,2},{3,19},{19,3},{4,20},{20... | collective-permute-start | bytes 1769480 | tf_op jit(solution)/shard_map/ppermute | solution.py:361
  12.4 1.3 %slice.30.refs_8_ = bf16[256,2176]{1,0:T(8,128)(2,1)S(1)} slice(bf16[256,3840]{1,0:T(8,128)(2,1)} %param.9), slice={[0:256], [1152:3328]} | slice | bytes 2228224 | tf_op jit(solution)/shard_map/slice | solution.py:372
  13.8 0.6 collective-permute-start.12
  14.3 4.3 %collective-permute-done.refs_1_ = bf16[128,1024]{1,0:T(8,128)(2,1)S(1)} collective-permute-done((bf16[128,1024]{1,0:T(8,128)(2,1)S(1)}, bf16[128,1024]{1,0:T(8,128)(2,1)S(1)}, u32[]{:S(2)}, u32[]{:S(2)}) %collective-permute-start) | collective-permute-done | bytes 262176 | tf_op jit(solution)/shard_map/ppermute | solution.py:358
  18.6 1.7 %collective-permute-start.4 = (bf16[128,1024]{1,0:T(8,128)(2,1)S(1)}, bf16[128,1024]{1,0:T(8,128)(2,1)S(1)}, u32[]{:S(2)}, u32[]{:S(2)}) collective-permute-start(bf16[128,1024]{1,0:T(8,128)(2,1)S(1)} %collective-permute-done.refs_1_), channel_id=1, source_target_pairs={{0,1},{1,0},{2,3},{3,2},{4,5},{5,4},{6,7},{7,6},{8,9},{9,8},{10,11... | collective-permute-start | bytes 786440 | tf_op jit(solution)/shard_map/ppermute | solution.py:358
  20.3 1.0 %collective-permute-done.1.refs_2_ = bf16[128,1024]{1,0:T(8,128)(2,1)} collective-permute-done((bf16[128,1024]{1,0:T(8,128)(2,1)S(1)}, bf16[128,1024]{1,0:T(8,128)(2,1)}, u32[]{:S(2)}, u32[]{:S(2)}) %collective-permute-start.1) | collective-permute-done | bytes 262176 | tf_op jit(solution)/shard_map/ppermute | solution.py:358
  21.3 0.4 collective-permute-start.2
  21.7 6.7 %score_slab.2 = (bf16[512,3840]{1,0:T(8,128)(2,1)}, s16[8,128,512]{2,1,0:T(8,128)(2,1)}, f32[8,128]{1,0:T(8,128)S(1)}) custom-call(s32[1]{0:T(128)} %bitcast.2.place, s32[32,1024]{1,0:T(8,128)S(1)} %bitcast.6, bf16[32,1024]{1,0:T(8,128)(2,1)S(1)} %bitcast.8, bf16[508,3840]{1,0:T(8,128)(2,1)} %slab.3), custom_call_target="tpu_custom_call" | custom-call | flops 13958643712 | bytes 1024 | tf_op jit(solution)/shard_map/score_slab/pallas_call | solution.py:109
  28.4 1.0 %slice.25.refs_8_ = bf16[256,512]{1,0:T(8,128)(2,1)S(1)} slice(bf16[256,3840]{1,0:T(8,128)(2,1)} %param.9), slice={[0:256], [3328:3840]} | slice | bytes 524288 | tf_op jit(solution)/shard_map/slice | solution.py:372
  29.4 0.0 collective-permute-done.3.refs_4_
  29.4 1.6 %collective-permute-start.5 = (bf16[128,1024]{1,0:T(8,128)(2,1)}, bf16[128,1024]{1,0:T(8,128)(2,1)S(1)}, u32[]{:S(2)}, u32[]{:S(2)}) collective-permute-start(bf16[128,1024]{1,0:T(8,128)(2,1)} %collective-permute-done.1.refs_2_), channel_id=1, source_target_pairs={{0,1},{1,0},{2,3},{3,2},{4,5},{5,4},{6,7},{7,6},{8,9},{9,8},{10,11... | collective-permute-start | bytes 786440 | tf_op jit(solution)/shard_map/ppermute | solution.py:358
  31.0 0.0 collective-permute-done.4.refs_5_
  31.0 0.7 copy-done.5
  31.7 0.0 collective-permute-done.2.refs_3_
  31.7 0.0 collective-permute-start.7
  31.7 0.7 collective-permute-start.6
  32.4 6.7 %score_slab.3 = (bf16[512,3840]{1,0:T(8,128)(2,1)}, s16[8,128,512]{2,1,0:T(8,128)(2,1)}, f32[8,128]{1,0:T(8,128)S(1)}) custom-call(s32[1]{0:T(128)} %bitcast.2.place, s32[32,1024]{1,0:T(8,128)S(1)} %bitcast.7, bf16[32,1024]{1,0:T(8,128)(2,1)S(1)} %bitcast.9, bf16[508,3840]{1,0:T(8,128)(2,1)} %slab.3, ...), custom_call_target="tpu_custom_call", output_to_operand_aliasing={{1}: (4, {})} | custom-call | flops 13958643712 | bytes 1024 | tf_op jit(solution)/shard_map/score_slab/pallas_call | solution.py:109
  39.1 0.0 copy-start.9
  39.1 0.0 collective-permute-done.5.refs_6_
  39.2 0.0 collective-permute-done.9.refs_10_
  39.2 3.0 %collective-permute-done.6.refs_7_ = bf16[128,1024]{1,0:T(8,128)(2,1)S(1)} collective-permute-done((bf16[128,1024]{1,0:T(8,128)(2,1)S(1)}, bf16[128,1024]{1,0:T(8,128)(2,1)S(1)}, u32[]{:S(2)}, u32[]{:S(2)}) %collective-permute-start.6) | collective-permute-done | bytes 262176 | tf_op jit(solution)/shard_map/ppermute | solution.py:358
  42.2 0.7 copy-done.8
  42.9 4.4 %all-to-all-start = ((s16[8,128,512]{2,1,0:T(8,128)(2,1)}), s16[8,128,512]{2,1,0:T(8,128)(2,1)}, u32[]{:S(2)}, u32[]{:S(2)}) async-start(s16[8,128,512]{2,1,0:T(8,128)(2,1)} %get-tuple-element.30), calls=%async_computation | async-start | bytes 2097152 | tf_op jit(solution)/shard_map/all_to_all | solution.py:400
  47.3 2.0 %collective-permute-done.12.refs_10_ = bf16[256,2176]{1,0:T(8,128)(2,1)} collective-permute-done((bf16[256,2176]{1,0:T(8,128)(2,1)S(1)}, bf16[256,2176]{1,0:T(8,128)(2,1)}, u32[]{:S(2)}, u32[]{:S(2)}) %collective-permute-start.12) | collective-permute-done | bytes 1114144 | tf_op jit(solution)/shard_map/ppermute | solution.py:361
  49.3 0.0 collective-permute-start.13
  49.3 0.5 collective-permute-start.10
  49.9 1.5 %collective-permute-start.8 = (bf16[256,512]{1,0:T(8,128)(2,1)S(1)}, bf16[256,512]{1,0:T(8,128)(2,1)}, u32[]{:S(2)}, u32[]{:S(2)}) collective-permute-start(bf16[256,512]{1,0:T(8,128)(2,1)S(1)} %slice.25.refs_8_), channel_id=1, source_target_pairs={{0,16},{16,0},{1,17},{17,1},{2,18},{18,2},{3,19},{19,3},{4,20},{20... | collective-permute-start | bytes 786440 | tf_op jit(solution)/shard_map/ppermute | solution.py:361
  51.4 0.1 pad.2.clone
  51.5 0.1 maximum_maximum_fusion.refs_15_
  51.6 1.7 %collective-permute-done.10.refs_11_ = bf16[256,1152]{1,0:T(8,128)(2,1)} collective-permute-done((bf16[256,1152]{1,0:T(8,128)(2,1)}, bf16[256,1152]{1,0:T(8,128)(2,1)}, u32[]{:S(2)}, u32[]{:S(2)}) %collective-permute-start.10) | collective-permute-done | bytes 589856 | tf_op jit(solution)/shard_map/ppermute | solution.py:364
  53.3 0.0 collective-permute-done.7.refs_9_
  53.3 6.2 %project.3.refs_15_ = f32[8,8,128]{2,1,0:T(8,128)S(1)} custom-call(s32[1]{0:T(128)} %bitcast.place, bf16[128,1024]{1,0:T(8,128)(2,1)} %bitcast.13, bf16[128,1024]{1,0:T(8,128)(2,1)} %copy-done.3, bf16[128,1024]{1,0:T(8,128)(2,1)} %collective-permute-done.1.refs_2_, bf16[128,1024]{1,0:T(8,128)(2,1)} %copy-done.6, bf16[128,1024]{1,0:T(8,128)(2,1)} %copy-done.4, ...), custom_call_target="tpu_custom_call" | custom-call | flops 1024 | bytes 1024 | tf_op jit(solution)/shard_map/project/pallas_call | solution.py:257
  59.5 0.0 collective-permute-done.8.refs_10_
  59.5 0.2 collective-permute-start.11
  59.7 0.0 collective-permute-done.13.refs_11_
  59.7 9.4 %project.4.refs_15_ = f32[8,8,128]{2,1,0:T(8,128)S(1)} custom-call(s32[1]{0:T(128)} %bitcast.place, bf16[128,1024]{1,0:T(8,128)(2,1)} %bitcast.14, bf16[128,1024]{1,0:T(8,128)(2,1)} %copy-done.3, bf16[128,1024]{1,0:T(8,128)(2,1)} %collective-permute-done.1.refs_2_, bf16[128,1024]{1,0:T(8,128)(2,1)} %copy-done.6, bf16[128,1024]{1,0:T(8,128)(2,1)} %copy-done.4, ...), custom_call_target="tpu_custom_call" | custom-call | flops 1024 | bytes 1024 | tf_op jit(solution)/shard_map/project/pallas_call | solution.py:257
  69.1 0.0 collective-permute-done.11.refs_11_
  69.1 3.8 %project.5 = f32[8,8,128]{2,1,0:T(8,128)S(1)} custom-call(s32[1]{0:T(128)} %bitcast.place, bf16[128,1024]{1,0:T(8,128)(2,1)} %bitcast.15, bf16[128,1024]{1,0:T(8,128)(2,1)} %copy-done.3, bf16[128,1024]{1,0:T(8,128)(2,1)} %collective-permute-done.1.refs_2_, bf16[128,1024]{1,0:T(8,128)(2,1)} %copy-done.6, bf16[128,1024]{1,0:T(8,128)(2,1)} %copy-done.4, ...), custom_call_target="tpu_custom_call" | custom-call | flops 1024 | bytes 1024 | tf_op jit(solution)/shard_map/project/pallas_call | solution.py:257
  72.9 0.0 all-to-all-done.coded
  72.9 10.4 %all_to_all.10.fresh = f32[8,8,128]{2,1,0:T(8,128)S(1)} all-to-all(f32[8,8,128]{2,1,0:T(8,128)S(1)} %project.5), channel_id=1, replica_groups=mesh['row'=2,'core'=2,'term'=8] {'term'}, dimensions={0} | all-to-all | bytes 65536 | tf_op jit(solution)/shard_map/all_to_all | solution.py:425
  83.3 2.4 %finish.1 = f32[128,512]{1,0:T(8,128)} custom-call(s16[8,128,512]{2,1,0:T(8,128)(2,1)} %all-to-all-done.coded, f32[8,8,128]{2,1,0:T(8,128)S(1)} %all_to_all.10.fresh), custom_call_target="tpu_custom_call" | custom-call | flops 1024 | bytes 1024 | tf_op jit(solution)/shard_map/finish/pallas_call | solution.py:321
  (26 shorter events, 0.1 us)
Async XLA Ops:
  0.0 21.7 %copy-start = (s32[1024,32]{0,1:T(8,128)S(1)}, s32[1024,32]{0,1:T(8,128)}, u32[]{:S(2)}) copy-start(s32[1024,32]{0,1:T(8,128)} %param.12) | copy-start | bytes 393220
  0.0 21.7 %copy-start.1 = (bf16[1024,32]{0,1:T(8,128)(2,1)S(1)}, bf16[1024,32]{0,1:T(8,128)(2,1)}, u32[]{:S(2)}) copy-start(bf16[1024,32]{0,1:T(8,128)(2,1)} %param.13) | copy-start | bytes 196612
  3.7 24.7 %copy-start.2 = (bf16[4,32,1024]{2,1,0:T(8,128)(2,1)}, bf16[4,32,1024]{2,1,0:T(8,128)(2,1)S(1)}, u32[]{:S(2)}) copy-start(bf16[4,32,1024]{2,1,0:T(8,128)(2,1)S(1)} %broadcast_select_fusion) | copy-start | bytes 786436
  3.7 14.9 %collective-permute-start = (bf16[128,1024]{1,0:T(8,128)(2,1)S(1)}, bf16[128,1024]{1,0:T(8,128)(2,1)S(1)}, u32[]{:S(2)}, u32[]{:S(2)}) collective-permute-start(bf16[128,1024]{1,0:T(8,128)(2,1)S(1)} %bitcast.10), channel_id=1, source_target_pairs={{0,2},{1,3},{2,0},{3,1},{4,6},{5,7},{6,4},{7,5},{8,10},{9,11},{10,... | collective-permute-start | bytes 786440 | tf_op jit(solution)/shard_map/ppermute | solution.py:358
  6.8 14.4 %collective-permute-start.1 = (bf16[128,1024]{1,0:T(8,128)(2,1)S(1)}, bf16[128,1024]{1,0:T(8,128)(2,1)}, u32[]{:S(2)}, u32[]{:S(2)}) collective-permute-start(bf16[128,1024]{1,0:T(8,128)(2,1)S(1)} %bitcast.11), channel_id=1, source_target_pairs={{0,4},{1,5},{2,6},{3,7},{4,0},{5,1},{6,2},{7,3},{8,12},{9,13},{10,... | collective-permute-start | bytes 786440 | tf_op jit(solution)/shard_map/ppermute | solution.py:358
  9.4 20.0 %collective-permute-start.3 = (bf16[128,1024]{1,0:T(8,128)(2,1)S(1)}, bf16[128,1024]{1,0:T(8,128)(2,1)S(1)}, u32[]{:S(2)}, u32[]{:S(2)}) collective-permute-start(bf16[128,1024]{1,0:T(8,128)(2,1)S(1)} %bitcast.12), channel_id=1, source_target_pairs={{0,1},{1,0},{2,3},{3,2},{4,5},{5,4},{6,7},{7,6},{8,9},{9,8},{10,11... | collective-permute-start | bytes 786440 | tf_op jit(solution)/shard_map/ppermute | solution.py:358
  10.9 28.2 %collective-permute-start.9 = (bf16[256,1152]{1,0:T(8,128)(2,1)}, bf16[256,1152]{1,0:T(8,128)(2,1)}, u32[]{:S(2)}, u32[]{:S(2)}) collective-permute-start(bf16[256,1152]{1,0:T(8,128)(2,1)} %slice.24.refs_8_), channel_id=1, source_target_pairs={{0,16},{16,0},{1,17},{17,1},{2,18},{18,2},{3,19},{19,3},{4,20},{20... | collective-permute-start | bytes 1769480 | tf_op jit(solution)/shard_map/ppermute | solution.py:361
  13.8 35.6 %collective-permute-start.12 = (bf16[256,2176]{1,0:T(8,128)(2,1)S(1)}, bf16[256,2176]{1,0:T(8,128)(2,1)}, u32[]{:S(2)}, u32[]{:S(2)}) collective-permute-start(bf16[256,2176]{1,0:T(8,128)(2,1)S(1)} %slice.30.refs_8_), channel_id=1, source_target_pairs={{0,16},{16,0},{1,17},{17,1},{2,18},{18,2},{3,19},{19,3},{4,20},{20... | collective-permute-start | bytes 3342344 | tf_op jit(solution)/shard_map/ppermute | solution.py:361
  18.6 9.8 %copy-start.3 = (bf16[128,1024]{1,0:T(8,128)(2,1)}, bf16[128,1024]{1,0:T(8,128)(2,1)S(1)}, u32[]{:S(2)}) copy-start(bf16[128,1024]{1,0:T(8,128)(2,1)S(1)} %collective-permute-done.refs_1_) | copy-start | bytes 786436
  18.6 12.4 %collective-permute-start.4 = (bf16[128,1024]{1,0:T(8,128)(2,1)S(1)}, bf16[128,1024]{1,0:T(8,128)(2,1)S(1)}, u32[]{:S(2)}, u32[]{:S(2)}) collective-permute-start(bf16[128,1024]{1,0:T(8,128)(2,1)S(1)} %collective-permute-done.refs_1_), channel_id=1, source_target_pairs={{0,1},{1,0},{2,3},{3,2},{4,5},{5,4},{6,7},{7,6},{8,9},{9,8},{10,11... | collective-permute-start | bytes 786440 | tf_op jit(solution)/shard_map/ppermute | solution.py:358
  21.3 10.4 %collective-permute-start.2 = (bf16[128,1024]{1,0:T(8,128)(2,1)}, bf16[128,1024]{1,0:T(8,128)(2,1)S(1)}, u32[]{:S(2)}, u32[]{:S(2)}) collective-permute-start(bf16[128,1024]{1,0:T(8,128)(2,1)} %collective-permute-done.1.refs_2_), channel_id=1, source_target_pairs={{0,2},{1,3},{2,0},{3,1},{4,6},{5,7},{6,4},{7,5},{8,10},{9,11},{10,... | collective-permute-start | bytes 786440 | tf_op jit(solution)/shard_map/ppermute | solution.py:358
  29.4 1.6 %copy-start.4 = (bf16[128,1024]{1,0:T(8,128)(2,1)}, bf16[128,1024]{1,0:T(8,128)(2,1)S(1)}, u32[]{:S(2)}) copy-start(bf16[128,1024]{1,0:T(8,128)(2,1)S(1)} %collective-permute-done.3.refs_4_) | copy-start | bytes 786436
  29.4 9.7 %collective-permute-start.5 = (bf16[128,1024]{1,0:T(8,128)(2,1)}, bf16[128,1024]{1,0:T(8,128)(2,1)S(1)}, u32[]{:S(2)}, u32[]{:S(2)}) collective-permute-start(bf16[128,1024]{1,0:T(8,128)(2,1)} %collective-permute-done.1.refs_2_), channel_id=1, source_target_pairs={{0,1},{1,0},{2,3},{3,2},{4,5},{5,4},{6,7},{7,6},{8,9},{9,8},{10,11... | collective-permute-start | bytes 786440 | tf_op jit(solution)/shard_map/ppermute | solution.py:358
  31.0 0.7 copy-start.5
  31.7 7.4 %copy-start.6 = (bf16[128,1024]{1,0:T(8,128)(2,1)}, bf16[128,1024]{1,0:T(8,128)(2,1)S(1)}, u32[]{:S(2)}) copy-start(bf16[128,1024]{1,0:T(8,128)(2,1)S(1)} %collective-permute-done.2.refs_3_) | copy-start | bytes 786436
  31.7 21.6 %collective-permute-start.7 = (bf16[256,3840]{1,0:T(8,128)(2,1)}, bf16[256,3840]{1,0:T(8,128)(2,1)S(1)}, u32[]{:S(2)}, u32[]{:S(2)}) collective-permute-start(bf16[256,3840]{1,0:T(8,128)(2,1)} %param.9), channel_id=1, source_target_pairs={{0,8},{8,0},{1,9},{9,1},{2,10},{10,2},{3,11},{11,3},{4,12},{12,4},... | collective-permute-start | bytes 5898248 | tf_op jit(solution)/shard_map/ppermute | solution.py:364
  31.7 10.5 %collective-permute-start.6 = (bf16[128,1024]{1,0:T(8,128)(2,1)S(1)}, bf16[128,1024]{1,0:T(8,128)(2,1)S(1)}, u32[]{:S(2)}, u32[]{:S(2)}) collective-permute-start(bf16[128,1024]{1,0:T(8,128)(2,1)S(1)} %collective-permute-done.2.refs_3_), channel_id=1, source_target_pairs={{0,1},{1,0},{2,3},{3,2},{4,5},{5,4},{6,7},{7,6},{8,9},{9,8},{10,11... | collective-permute-start | bytes 786440 | tf_op jit(solution)/shard_map/ppermute | solution.py:358
  39.1 12.3 %copy-start.9 = (f32[3840]{0:T(1024)S(1)}, f32[3840]{0:T(1024)}, u32[]{:S(2)}) copy-start(f32[3840]{0:T(1024)} %param.10) | copy-start | bytes 46084
  39.1 3.0 %copy-start.7 = (bf16[128,1024]{1,0:T(8,128)(2,1)}, bf16[128,1024]{1,0:T(8,128)(2,1)S(1)}, u32[]{:S(2)}) copy-start(bf16[128,1024]{1,0:T(8,128)(2,1)S(1)} %collective-permute-done.5.refs_6_) | copy-start | bytes 786436
  42.2 0.7 copy-start.8
  42.9 30.0 %all-to-all-start = ((s16[8,128,512]{2,1,0:T(8,128)(2,1)}), s16[8,128,512]{2,1,0:T(8,128)(2,1)}, u32[]{:S(2)}, u32[]{:S(2)}) async-start(s16[8,128,512]{2,1,0:T(8,128)(2,1)} %get-tuple-element.30), calls=%async_computation | async-start | bytes 2097152 | tf_op jit(solution)/shard_map/all_to_all | solution.py:400
  49.3 10.4 %collective-permute-start.13 = (bf16[256,2176]{1,0:T(8,128)(2,1)}, bf16[256,2176]{1,0:T(8,128)(2,1)}, u32[]{:S(2)}, u32[]{:S(2)}) collective-permute-start(bf16[256,2176]{1,0:T(8,128)(2,1)} %collective-permute-done.12.refs_10_), channel_id=1, source_target_pairs={{0,8},{8,0},{1,9},{9,1},{2,10},{10,2},{3,11},{11,3},{4,12},{12,4},... | collective-permute-start | bytes 3342344 | tf_op jit(solution)/shard_map/ppermute | solution.py:364
  49.3 3.9 %collective-permute-start.10 = (bf16[256,1152]{1,0:T(8,128)(2,1)}, bf16[256,1152]{1,0:T(8,128)(2,1)}, u32[]{:S(2)}, u32[]{:S(2)}) collective-permute-start(bf16[256,1152]{1,0:T(8,128)(2,1)} %collective-permute-done.9.refs_10_), channel_id=1, source_target_pairs={{0,8},{8,0},{1,9},{9,1},{2,10},{10,2},{3,11},{11,3},{4,12},{12,4},... | collective-permute-start | bytes 1769480 | tf_op jit(solution)/shard_map/ppermute | solution.py:364
  49.9 9.6 %collective-permute-start.8 = (bf16[256,512]{1,0:T(8,128)(2,1)S(1)}, bf16[256,512]{1,0:T(8,128)(2,1)}, u32[]{:S(2)}, u32[]{:S(2)}) collective-permute-start(bf16[256,512]{1,0:T(8,128)(2,1)S(1)} %slice.25.refs_8_), channel_id=1, source_target_pairs={{0,16},{16,0},{1,17},{17,1},{2,18},{18,2},{3,19},{19,3},{4,20},{20... | collective-permute-start | bytes 786440 | tf_op jit(solution)/shard_map/ppermute | solution.py:361
  59.5 9.6 %collective-permute-start.11 = (bf16[256,512]{1,0:T(8,128)(2,1)}, bf16[256,512]{1,0:T(8,128)(2,1)S(1)}, u32[]{:S(2)}, u32[]{:S(2)}) collective-permute-start(bf16[256,512]{1,0:T(8,128)(2,1)} %collective-permute-done.8.refs_10_), channel_id=1, source_target_pairs={{0,8},{8,0},{1,9},{9,1},{2,10},{10,2},{3,11},{11,3},{4,12},{12,4},... | collective-permute-start | bytes 786440 | tf_op jit(solution)/shard_map/ppermute | solution.py:364

commit v5 on v4

--- a/solution.py
+++ b/solution.py
@@ -136,7 +136,7 @@
             jax.ShapeDtypeStruct((kept, rows), F32),
         ],
         input_output_aliases={} if coded is None else {4: 1},
-        compiler_params=pltpu.CompilerParams(vmem_limit_bytes=44 << 20),
+        compiler_params=pltpu.CompilerParams(vmem_limit_bytes=50 << 20),
         cost_estimate=pl.CostEstimate(flops=K1COST, bytes_accessed=1024, transcendentals=0),
         name="score_slab",
     )(place, ids, weights, pltpu.with_memory_space_constraint(slab, pltpu.HBM), *given)
@@ -339,7 +339,7 @@
         return [(0, width)]
     tiles = width // LANES
     small = max(1, tiles * 2 // 15)
-    sizes = [tiles * 9 // 30, tiles - tiles * 9 // 30 - small, small]
+    sizes = [tiles * 8 // 30, tiles - tiles * 8 // 30 - small, small]
     return [(sum(sizes[:i]) * LANES, size * LANES) for i, size in enumerate(sizes)]
 
 
@@ -396,7 +396,8 @@
         )
         dense.append(pltpu.with_memory_space_constraint(full, pltpu.HBM))
         scales.append(scale[: terms // PARTS])
-    coded = after(coded, crossed[:1], second_x)
+    swapped = [to_core(part) for part in after(crossed[0], by_z)]
+    coded = after(coded, swapped, second_x)
     coded = lax.all_to_all(coded, "term", split_axis=0, concat_axis=0, tiled=True)
 
     scales = jnp.concatenate(scales).reshape(terms, 1, block_queries)
@@ -406,7 +407,7 @@
     bias = proj_bias.reshape(1, width)
     beside = to_core(after(proj_weight, by_z))
     for b, (start, size) in enumerate(blocks):
-        if not b or b < len(blocks) - 1:
+        if 0 < b < len(blocks) - 1:
             swapped = [to_core(part) for part in crossed[b]]
         pieces = [local[b], beside]
         for mine, other in zip(crossed[b], swapped):

time: 86.3 us -> 85.8 us (level)
  waiting for transfers between devices: 12 us -> 9.81 us
  local copies, waits for them, and re-layouts: 5.85 us -> 7.83 us
    unnamed x20 -> x30, local copies, waits for them, and re-layouts: 1.44 us -> 4.29 us
    ppermute x4, waiting for transfers between devices: 1.69 us -> 0.01 us  [to_core(): return lax.ppermute(value, 'core', [(0, 1), (1, 0)])]
    ppermute x3, waiting for transfers between devices: 2.03 us -> 0.98 us  [to_row(): return lax.ppermute(value, 'row', [(i, i ^ k) for i in range(rows)])]
    all_to_all x1, waiting for transfers between devices: 0.01 us -> 0.9 us  [shards(): lax.all_to_all(coded, 'term', split_axis=0, concat_axis=0, tiled=True)]
    slice x3, local copies, waits for them, and re-layouts: 4.3 us -> 3.43 us  [shards(): sent = proj_weight[:, start:start + size]]
where the time goes in v5:
time: 85.8 us; the launch traced here: 85.2 us
  Pallas kernels  34.6 us (40%)
  starting transfers between devices  20.2 us (24%)
  blocking collectives  10.5 us (12%)
  waiting for transfers between devices  9.81 us (11%)
  local copies, waits for them, and re-layouts  7.83 us (9%)
  other arithmetic  1.83 us (2%)
    pallas_call x3, Pallas kernels, project(): pl.pallas_call(functools.partial(project_kernel, (len(features), len(weig...  18.7 us
    pallas_call x2, Pallas kernels, score_slab(): pl.pallas_call(score_kernel, grid_spec=pltpu.PrefetchScalarGridSpec(num_s...  13.4 us
    ppermute x7, starting transfers between devices, to_term(): return lax.ppermute(value, 'term', [(i, i ^ k) for i in range(terms)])  11.4 us
    all_to_all x1, blocking collectives, shards(): lax.all_to_all(running, 'term', split_axis=0, concat_axis=0, tiled=True)  10.5 us
    ppermute x7, waiting for transfers between devices, to_term(): return lax.ppermute(value, 'term', [(i, i ^ k) for i in range(terms)])  7.92 us
    all_to_all x1, starting transfers between devices, shards(): lax.all_to_all(coded, 'term', split_axis=0, concat_axis=0, tiled=True)  4.43 us
    unnamed x30, local copies, waits for them, and re-layouts  4.29 us
    ppermute x3, starting transfers between devices, to_row(): return lax.ppermute(value, 'row', [(i, i ^ k) for i in range(rows)])  3.61 us
  transfers between devices with their start and end apart: 15, of which 5 were waited for; matrix products, arithmetic and copies ran while one was open for 3% of the time, Pallas kernels for 38%

profile of v5, /device:TPU:0, one launch (start us, length us, event | category | flops | bytes accessed | tf_op | source)
XLA Modules:
  0.0 85.2 jit_solution(16903036212632044573)
XLA Ops:
  0.0 1.1 %slice.24.refs_8_ = bf16[256,1024]{1,0:T(8,128)(2,1)S(1)} slice(bf16[256,3840]{1,0:T(8,128)(2,1)} %param.9), slice={[0:256], [0:1024]} | slice | bytes 1048576 | tf_op jit(solution)/shard_map/slice | solution.py:372
  1.1 0.7 broadcast_compare_fusion
  1.8 1.0 %broadcast_select_fusion = bf16[4,32,1024]{2,1,0:T(8,128)(2,1)S(1)} fusion(bf16[4,32,1024]{2,1,0:T(8,128)(2,1)} %param.7, pred[4,32]{1,0:T(4,128)(4,1)S(1)} %broadcast_compare_fusion), kind=kLoop, calls=%fused_computation | loop fusion | flops 131072 | bytes 524416 | tf_op jit(solution)/shard_map/jit(_where)/select_n | solution.py:378
  2.9 0.0 copy-start.7
  2.9 3.1 %collective-permute-start = (bf16[128,1024]{1,0:T(8,128)(2,1)S(1)}, bf16[128,1024]{1,0:T(8,128)(2,1)S(1)}, u32[]{:S(2)}, u32[]{:S(2)}) collective-permute-start(bf16[128,1024]{1,0:T(8,128)(2,1)S(1)} %bitcast.10), channel_id=1, source_target_pairs={{0,2},{1,3},{2,0},{3,1},{4,6},{5,7},{6,4},{7,5},{8,10},{9,11},{10,... | collective-permute-start | bytes 786440 | tf_op jit(solution)/shard_map/ppermute | solution.py:358
  6.0 2.6 %collective-permute-start.1 = (bf16[128,1024]{1,0:T(8,128)(2,1)S(1)}, bf16[128,1024]{1,0:T(8,128)(2,1)}, u32[]{:S(2)}, u32[]{:S(2)}) collective-permute-start(bf16[128,1024]{1,0:T(8,128)(2,1)S(1)} %bitcast.11), channel_id=1, source_target_pairs={{0,4},{1,5},{2,6},{3,7},{4,0},{5,1},{6,2},{7,3},{8,12},{9,13},{10,... | collective-permute-start | bytes 786440 | tf_op jit(solution)/shard_map/ppermute | solution.py:358
  8.6 1.5 %collective-permute-start.3 = (bf16[128,1024]{1,0:T(8,128)(2,1)S(1)}, bf16[128,1024]{1,0:T(8,128)(2,1)S(1)}, u32[]{:S(2)}, u32[]{:S(2)}) collective-permute-start(bf16[128,1024]{1,0:T(8,128)(2,1)S(1)} %bitcast.12), channel_id=1, source_target_pairs={{0,1},{1,0},{2,3},{3,2},{4,5},{5,4},{6,7},{7,6},{8,9},{9,8},{10,11... | collective-permute-start | bytes 786440 | tf_op jit(solution)/shard_map/ppermute | solution.py:358
  10.1 1.5 %collective-permute-start.9 = (bf16[256,1024]{1,0:T(8,128)(2,1)S(1)}, bf16[256,1024]{1,0:T(8,128)(2,1)}, u32[]{:S(2)}, u32[]{:S(2)}) collective-permute-start(bf16[256,1024]{1,0:T(8,128)(2,1)S(1)} %slice.24.refs_8_), channel_id=1, source_target_pairs={{0,16},{16,0},{1,17},{17,1},{2,18},{18,2},{3,19},{19,3},{4,20},{20... | collective-permute-start | bytes 1572872 | tf_op jit(solution)/shard_map/ppermute | solution.py:361
  11.6 1.3 %slice.30.refs_8_ = bf16[256,2304]{1,0:T(8,128)(2,1)S(1)} slice(bf16[256,3840]{1,0:T(8,128)(2,1)} %param.9), slice={[0:256], [1024:3328]} | slice | bytes 2359296 | tf_op jit(solution)/shard_map/slice | solution.py:372
  12.9 0.6 collective-permute-start.12
  13.5 4.3 %collective-permute-done.refs_1_ = bf16[128,1024]{1,0:T(8,128)(2,1)S(1)} collective-permute-done((bf16[128,1024]{1,0:T(8,128)(2,1)S(1)}, bf16[128,1024]{1,0:T(8,128)(2,1)S(1)}, u32[]{:S(2)}, u32[]{:S(2)}) %collective-permute-start) | collective-permute-done | bytes 262176 | tf_op jit(solution)/shard_map/ppermute | solution.py:358
  17.8 1.7 %collective-permute-start.4 = (bf16[128,1024]{1,0:T(8,128)(2,1)S(1)}, bf16[128,1024]{1,0:T(8,128)(2,1)S(1)}, u32[]{:S(2)}, u32[]{:S(2)}) collective-permute-start(bf16[128,1024]{1,0:T(8,128)(2,1)S(1)} %collective-permute-done.refs_1_), channel_id=1, source_target_pairs={{0,1},{1,0},{2,3},{3,2},{4,5},{5,4},{6,7},{7,6},{8,9},{9,8},{10,11... | collective-permute-start | bytes 786440 | tf_op jit(solution)/shard_map/ppermute | solution.py:358
  19.5 1.0 %collective-permute-done.1.refs_2_ = bf16[128,1024]{1,0:T(8,128)(2,1)} collective-permute-done((bf16[128,1024]{1,0:T(8,128)(2,1)S(1)}, bf16[128,1024]{1,0:T(8,128)(2,1)}, u32[]{:S(2)}, u32[]{:S(2)}) %collective-permute-start.1) | collective-permute-done | bytes 262176 | tf_op jit(solution)/shard_map/ppermute | solution.py:358
  20.4 0.4 collective-permute-start.2
  20.9 6.7 %score_slab.2 = (bf16[512,3840]{1,0:T(8,128)(2,1)}, s16[8,128,512]{2,1,0:T(8,128)(2,1)}, f32[8,128]{1,0:T(8,128)S(1)}) custom-call(s32[1]{0:T(128)} %bitcast.2.place, s32[32,1024]{1,0:T(8,128)S(1)} %bitcast.6, bf16[32,1024]{1,0:T(8,128)(2,1)S(1)} %bitcast.8, bf16[508,3840]{1,0:T(8,128)(2,1)} %slab.3), custom_call_target="tpu_custom_call" | custom-call | flops 13958643712 | bytes 1024 | tf_op jit(solution)/shard_map/score_slab/pallas_call | solution.py:109
  27.6 1.0 %slice.25.refs_8_ = bf16[256,512]{1,0:T(8,128)(2,1)S(1)} slice(bf16[256,3840]{1,0:T(8,128)(2,1)} %param.9), slice={[0:256], [3328:3840]} | slice | bytes 524288 | tf_op jit(solution)/shard_map/slice | solution.py:372
  28.6 0.0 collective-permute-done.3.refs_4_
  28.6 1.6 %collective-permute-start.5 = (bf16[128,1024]{1,0:T(8,128)(2,1)}, bf16[128,1024]{1,0:T(8,128)(2,1)S(1)}, u32[]{:S(2)}, u32[]{:S(2)}) collective-permute-start(bf16[128,1024]{1,0:T(8,128)(2,1)} %collective-permute-done.1.refs_2_), channel_id=1, source_target_pairs={{0,1},{1,0},{2,3},{3,2},{4,5},{5,4},{6,7},{7,6},{8,9},{9,8},{10,11... | collective-permute-start | bytes 786440 | tf_op jit(solution)/shard_map/ppermute | solution.py:358
  30.2 0.0 collective-permute-done.4.refs_5_
  30.2 0.0 collective-permute-done.2.refs_3_
  30.2 0.0 collective-permute-done.9.refs_10_
  30.2 0.7 copy-done.10
  30.9 0.0 collective-permute-start.10
  30.9 0.5 collective-permute-start.7
  31.4 0.5 collective-permute-start.6
  32.0 6.7 %score_slab.3 = (bf16[512,3840]{1,0:T(8,128)(2,1)}, s16[8,128,512]{2,1,0:T(8,128)(2,1)}, f32[8,128]{1,0:T(8,128)S(1)}) custom-call(s32[1]{0:T(128)} %bitcast.2.place, s32[32,1024]{1,0:T(8,128)S(1)} %bitcast.7, bf16[32,1024]{1,0:T(8,128)(2,1)S(1)} %bitcast.9, bf16[508,3840]{1,0:T(8,128)(2,1)} %slab.3, ...), custom_call_target="tpu_custom_call", output_to_operand_aliasing={{1}: (4, {})} | custom-call | flops 13958643712 | bytes 1024 | tf_op jit(solution)/shard_map/score_slab/pallas_call | solution.py:109
  38.7 0.0 copy-start.14
  38.7 0.0 collective-permute-done.5.refs_6_
  38.7 2.7 %collective-permute-done.6.refs_7_ = bf16[128,1024]{1,0:T(8,128)(2,1)S(1)} collective-permute-done((bf16[128,1024]{1,0:T(8,128)(2,1)S(1)}, bf16[128,1024]{1,0:T(8,128)(2,1)S(1)}, u32[]{:S(2)}, u32[]{:S(2)}) %collective-permute-start.6) | collective-permute-done | bytes 262176 | tf_op jit(solution)/shard_map/ppermute | solution.py:358
  41.4 0.0 collective-permute-done.10.refs_11_
  41.4 0.7 copy-done.13
  42.1 0.8 copy-done.2
  42.9 4.4 %all-to-all-start = ((s16[8,128,512]{2,1,0:T(8,128)(2,1)}), s16[8,128,512]{2,1,0:T(8,128)(2,1)}, u32[]{:S(2)}, u32[]{:S(2)}) async-start(s16[8,128,512]{2,1,0:T(8,128)(2,1)} %get-tuple-element.32), calls=%async_computation | async-start | bytes 2097152 | tf_op jit(solution)/shard_map/all_to_all | solution.py:401
  47.3 1.0 %collective-permute-done.12.refs_10_ = bf16[256,2304]{1,0:T(8,128)(2,1)} collective-permute-done((bf16[256,2304]{1,0:T(8,128)(2,1)S(1)}, bf16[256,2304]{1,0:T(8,128)(2,1)}, u32[]{:S(2)}, u32[]{:S(2)}) %collective-permute-start.12) | collective-permute-done | bytes 1179680 | tf_op jit(solution)/shard_map/ppermute | solution.py:361
  48.3 1.5 %collective-permute-start.8 = (bf16[256,512]{1,0:T(8,128)(2,1)S(1)}, bf16[256,512]{1,0:T(8,128)(2,1)}, u32[]{:S(2)}, u32[]{:S(2)}) collective-permute-start(bf16[256,512]{1,0:T(8,128)(2,1)S(1)} %slice.25.refs_8_), channel_id=1, source_target_pairs={{0,16},{16,0},{1,17},{17,1},{2,18},{18,2},{3,19},{19,3},{4,20},{20... | collective-permute-start | bytes 786440 | tf_op jit(solution)/shard_map/ppermute | solution.py:361
  49.8 0.1 pad.2.clone
  50.0 0.1 maximum_maximum_fusion.refs_15_
  50.0 0.0 collective-permute-done.7.refs_9_
  50.0 1.0 %copy-done.1 = bf16[256,1024]{1,0:T(8,128)(2,1)S(1)} copy-done((bf16[256,1024]{1,0:T(8,128)(2,1)S(1)}, bf16[256,1024]{1,0:T(8,128)(2,1)}, u32[]{:S(2)}) %copy-start.1) | copy-done | bytes 524312
  51.1 1.0 %copy-done.3 = bf16[256,1024]{1,0:T(8,128)(2,1)S(1)} copy-done((bf16[256,1024]{1,0:T(8,128)(2,1)S(1)}, bf16[256,1024]{1,0:T(8,128)(2,1)}, u32[]{:S(2)}) %copy-start.3) | copy-done | bytes 524312
  52.1 5.0 %project.3.refs_15_ = f32[8,8,128]{2,1,0:T(8,128)S(1)} custom-call(s32[1]{0:T(128)} %bitcast.place, bf16[128,1024]{1,0:T(8,128)(2,1)} %bitcast.13, bf16[128,1024]{1,0:T(8,128)(2,1)} %copy-done.8, bf16[128,1024]{1,0:T(8,128)(2,1)} %collective-permute-done.1.refs_2_, bf16[128,1024]{1,0:T(8,128)(2,1)} %copy-done.11, bf16[128,1024]{1,0:T(8,128)(2,1)} %copy-done.9, ...), custom_call_target="tpu_custom_call" | custom-call | flops 1024 | bytes 1024 | tf_op jit(solution)/shard_map/project/pallas_call | solution.py:257
  57.1 0.0 collective-permute-done.8.refs_10_
  57.1 0.3 collective-permute-start.11
  57.4 10.0 %project.4.refs_15_ = f32[8,8,128]{2,1,0:T(8,128)S(1)} custom-call(s32[1]{0:T(128)} %bitcast.place, bf16[128,1024]{1,0:T(8,128)(2,1)} %bitcast.14, bf16[128,1024]{1,0:T(8,128)(2,1)} %copy-done.8, bf16[128,1024]{1,0:T(8,128)(2,1)} %collective-permute-done.1.refs_2_, bf16[128,1024]{1,0:T(8,128)(2,1)} %copy-done.11, bf16[128,1024]{1,0:T(8,128)(2,1)} %copy-done.9, ...), custom_call_target="tpu_custom_call" | custom-call | flops 1024 | bytes 1024 | tf_op jit(solution)/shard_map/project/pallas_call | solution.py:257
  67.4 3.8 %project.5 = f32[8,8,128]{2,1,0:T(8,128)S(1)} custom-call(s32[1]{0:T(128)} %bitcast.place, bf16[128,1024]{1,0:T(8,128)(2,1)} %bitcast.15, bf16[128,1024]{1,0:T(8,128)(2,1)} %copy-done.8, bf16[128,1024]{1,0:T(8,128)(2,1)} %collective-permute-done.1.refs_2_, bf16[128,1024]{1,0:T(8,128)(2,1)} %copy-done.11, bf16[128,1024]{1,0:T(8,128)(2,1)} %copy-done.9, ...), custom_call_target="tpu_custom_call" | custom-call | flops 1024 | bytes 1024 | tf_op jit(solution)/shard_map/project/pallas_call | solution.py:257
  71.2 0.9 %all-to-all-done.coded = s16[8,128,512]{2,1,0:T(8,128)(2,1)} async-done(((s16[8,128,512]{2,1,0:T(8,128)(2,1)}), s16[8,128,512]{2,1,0:T(8,128)(2,1)}, u32[]{:S(2)}, u32[]{:S(2)}) %all-to-all-start) | async-done | bytes 1048608 | tf_op jit(solution)/shard_map/all_to_all | solution.py:401
  72.1 10.5 %all_to_all.10.fresh = f32[8,8,128]{2,1,0:T(8,128)S(1)} all-to-all(f32[8,8,128]{2,1,0:T(8,128)S(1)} %project.5), channel_id=1, replica_groups=mesh['row'=2,'core'=2,'term'=8] {'term'}, dimensions={0} | all-to-all | bytes 65536 | tf_op jit(solution)/shard_map/all_to_all | solution.py:426
  82.6 2.4 %finish.1 = f32[128,512]{1,0:T(8,128)} custom-call(s16[8,128,512]{2,1,0:T(8,128)(2,1)} %all-to-all-done.coded, f32[8,8,128]{2,1,0:T(8,128)S(1)} %all_to_all.10.fresh), custom_call_target="tpu_custom_call" | custom-call | flops 1024 | bytes 1024 | tf_op jit(solution)/shard_map/finish/pallas_call | solution.py:321
  (36 shorter events, 0.1 us)
Async XLA Ops:
  0.0 20.9 %copy-start.4 = (s32[1024,32]{0,1:T(8,128)S(1)}, s32[1024,32]{0,1:T(8,128)}, u32[]{:S(2)}) copy-start(s32[1024,32]{0,1:T(8,128)} %param.12) | copy-start | bytes 393220
  0.0 20.9 %copy-start.5 = (bf16[1024,32]{0,1:T(8,128)(2,1)S(1)}, bf16[1024,32]{0,1:T(8,128)(2,1)}, u32[]{:S(2)}) copy-start(bf16[1024,32]{0,1:T(8,128)(2,1)} %param.13) | copy-start | bytes 196612
  1.1 26.5 %copy-start = (bf16[256,1024]{1,0:T(8,128)(2,1)}, bf16[256,1024]{1,0:T(8,128)(2,1)S(1)}, u32[]{:S(2)}) copy-start(bf16[256,1024]{1,0:T(8,128)(2,1)S(1)} %slice.24.refs_8_) | copy-start | bytes 1572868
  2.9 24.7 %copy-start.7 = (bf16[4,32,1024]{2,1,0:T(8,128)(2,1)}, bf16[4,32,1024]{2,1,0:T(8,128)(2,1)S(1)}, u32[]{:S(2)}) copy-start(bf16[4,32,1024]{2,1,0:T(8,128)(2,1)S(1)} %broadcast_select_fusion) | copy-start | bytes 786436
  2.9 14.9 %collective-permute-start = (bf16[128,1024]{1,0:T(8,128)(2,1)S(1)}, bf16[128,1024]{1,0:T(8,128)(2,1)S(1)}, u32[]{:S(2)}, u32[]{:S(2)}) collective-permute-start(bf16[128,1024]{1,0:T(8,128)(2,1)S(1)} %bitcast.10), channel_id=1, source_target_pairs={{0,2},{1,3},{2,0},{3,1},{4,6},{5,7},{6,4},{7,5},{8,10},{9,11},{10,... | collective-permute-start | bytes 786440 | tf_op jit(solution)/shard_map/ppermute | solution.py:358
  6.0 14.4 %collective-permute-start.1 = (bf16[128,1024]{1,0:T(8,128)(2,1)S(1)}, bf16[128,1024]{1,0:T(8,128)(2,1)}, u32[]{:S(2)}, u32[]{:S(2)}) collective-permute-start(bf16[128,1024]{1,0:T(8,128)(2,1)S(1)} %bitcast.11), channel_id=1, source_target_pairs={{0,4},{1,5},{2,6},{3,7},{4,0},{5,1},{6,2},{7,3},{8,12},{9,13},{10,... | collective-permute-start | bytes 786440 | tf_op jit(solution)/shard_map/ppermute | solution.py:358
  8.6 20.0 %collective-permute-start.3 = (bf16[128,1024]{1,0:T(8,128)(2,1)S(1)}, bf16[128,1024]{1,0:T(8,128)(2,1)S(1)}, u32[]{:S(2)}, u32[]{:S(2)}) collective-permute-start(bf16[128,1024]{1,0:T(8,128)(2,1)S(1)} %bitcast.12), channel_id=1, source_target_pairs={{0,1},{1,0},{2,3},{3,2},{4,5},{5,4},{6,7},{7,6},{8,9},{9,8},{10,11... | collective-permute-start | bytes 786440 | tf_op jit(solution)/shard_map/ppermute | solution.py:358
  10.1 20.1 %collective-permute-start.9 = (bf16[256,1024]{1,0:T(8,128)(2,1)S(1)}, bf16[256,1024]{1,0:T(8,128)(2,1)}, u32[]{:S(2)}, u32[]{:S(2)}) collective-permute-start(bf16[256,1024]{1,0:T(8,128)(2,1)S(1)} %slice.24.refs_8_), channel_id=1, source_target_pairs={{0,16},{16,0},{1,17},{17,1},{2,18},{18,2},{3,19},{19,3},{4,20},{20... | collective-permute-start | bytes 1572872 | tf_op jit(solution)/shard_map/ppermute | solution.py:361
  12.9 35.3 %collective-permute-start.12 = (bf16[256,2304]{1,0:T(8,128)(2,1)S(1)}, bf16[256,2304]{1,0:T(8,128)(2,1)}, u32[]{:S(2)}, u32[]{:S(2)}) collective-permute-start(bf16[256,2304]{1,0:T(8,128)(2,1)S(1)} %slice.30.refs_8_), channel_id=1, source_target_pairs={{0,16},{16,0},{1,17},{17,1},{2,18},{18,2},{3,19},{19,3},{4,20},{20... | collective-permute-start | bytes 3538952 | tf_op jit(solution)/shard_map/ppermute | solution.py:361
  17.8 9.8 %copy-start.8 = (bf16[128,1024]{1,0:T(8,128)(2,1)}, bf16[128,1024]{1,0:T(8,128)(2,1)S(1)}, u32[]{:S(2)}) copy-start(bf16[128,1024]{1,0:T(8,128)(2,1)S(1)} %collective-permute-done.refs_1_) | copy-start | bytes 786436
  17.8 12.4 %collective-permute-start.4 = (bf16[128,1024]{1,0:T(8,128)(2,1)S(1)}, bf16[128,1024]{1,0:T(8,128)(2,1)S(1)}, u32[]{:S(2)}, u32[]{:S(2)}) collective-permute-start(bf16[128,1024]{1,0:T(8,128)(2,1)S(1)} %collective-permute-done.refs_1_), channel_id=1, source_target_pairs={{0,1},{1,0},{2,3},{3,2},{4,5},{5,4},{6,7},{7,6},{8,9},{9,8},{10,11... | collective-permute-start | bytes 786440 | tf_op jit(solution)/shard_map/ppermute | solution.py:358
  20.4 9.8 %collective-permute-start.2 = (bf16[128,1024]{1,0:T(8,128)(2,1)}, bf16[128,1024]{1,0:T(8,128)(2,1)S(1)}, u32[]{:S(2)}, u32[]{:S(2)}) collective-permute-start(bf16[128,1024]{1,0:T(8,128)(2,1)} %collective-permute-done.1.refs_2_), channel_id=1, source_target_pairs={{0,2},{1,3},{2,0},{3,1},{4,6},{5,7},{6,4},{7,5},{8,10},{9,11},{10,... | collective-permute-start | bytes 786440 | tf_op jit(solution)/shard_map/ppermute | solution.py:358
  20.9 11.1 %copy-start.6 = (bf16[1024,32]{0,1:T(8,128)(2,1)S(1)}, bf16[1024,32]{0,1:T(8,128)(2,1)}, u32[]{:S(2)}) copy-start(bf16[1024,32]{0,1:T(8,128)(2,1)} %param.13) | copy-start | bytes 196612
  28.6 1.6 %copy-start.9 = (bf16[128,1024]{1,0:T(8,128)(2,1)}, bf16[128,1024]{1,0:T(8,128)(2,1)S(1)}, u32[]{:S(2)}) copy-start(bf16[128,1024]{1,0:T(8,128)(2,1)S(1)} %collective-permute-done.3.refs_4_) | copy-start | bytes 786436
  28.6 10.1 %collective-permute-start.5 = (bf16[128,1024]{1,0:T(8,128)(2,1)}, bf16[128,1024]{1,0:T(8,128)(2,1)S(1)}, u32[]{:S(2)}, u32[]{:S(2)}) collective-permute-start(bf16[128,1024]{1,0:T(8,128)(2,1)} %collective-permute-done.1.refs_2_), channel_id=1, source_target_pairs={{0,1},{1,0},{2,3},{3,2},{4,5},{5,4},{6,7},{7,6},{8,9},{9,8},{10,11... | collective-permute-start | bytes 786440 | tf_op jit(solution)/shard_map/ppermute | solution.py:358
  30.2 0.7 copy-start.10
  30.2 8.5 %copy-start.11 = (bf16[128,1024]{1,0:T(8,128)(2,1)}, bf16[128,1024]{1,0:T(8,128)(2,1)S(1)}, u32[]{:S(2)}) copy-start(bf16[128,1024]{1,0:T(8,128)(2,1)S(1)} %collective-permute-done.2.refs_3_) | copy-start | bytes 786436
  30.9 10.5 %collective-permute-start.10 = (bf16[256,1024]{1,0:T(8,128)(2,1)}, bf16[256,1024]{1,0:T(8,128)(2,1)S(1)}, u32[]{:S(2)}, u32[]{:S(2)}) collective-permute-start(bf16[256,1024]{1,0:T(8,128)(2,1)} %collective-permute-done.9.refs_10_), channel_id=1, source_target_pairs={{0,8},{8,0},{1,9},{9,1},{2,10},{10,2},{3,11},{11,3},{4,12},{12,4},... | collective-permute-start | bytes 1572872 | tf_op jit(solution)/shard_map/ppermute | solution.py:364
  30.9 19.1 %collective-permute-start.7 = (bf16[256,3840]{1,0:T(8,128)(2,1)}, bf16[256,3840]{1,0:T(8,128)(2,1)S(1)}, u32[]{:S(2)}, u32[]{:S(2)}) collective-permute-start(bf16[256,3840]{1,0:T(8,128)(2,1)} %param.9), channel_id=1, source_target_pairs={{0,8},{8,0},{1,9},{9,1},{2,10},{10,2},{3,11},{11,3},{4,12},{12,4},... | collective-permute-start | bytes 5898248 | tf_op jit(solution)/shard_map/ppermute | solution.py:364
  31.4 10.0 %collective-permute-start.6 = (bf16[128,1024]{1,0:T(8,128)(2,1)S(1)}, bf16[128,1024]{1,0:T(8,128)(2,1)S(1)}, u32[]{:S(2)}, u32[]{:S(2)}) collective-permute-start(bf16[128,1024]{1,0:T(8,128)(2,1)S(1)} %collective-permute-done.2.refs_3_), channel_id=1, source_target_pairs={{0,1},{1,0},{2,3},{3,2},{4,5},{5,4},{6,7},{7,6},{8,9},{9,8},{10,11... | collective-permute-start | bytes 786440 | tf_op jit(solution)/shard_map/ppermute | solution.py:358
  38.7 11.2 %copy-start.14 = (f32[3840]{0:T(1024)S(1)}, f32[3840]{0:T(1024)}, u32[]{:S(2)}) copy-start(f32[3840]{0:T(1024)} %param.10) | copy-start | bytes 46084
  38.7 2.7 %copy-start.12 = (bf16[128,1024]{1,0:T(8,128)(2,1)}, bf16[128,1024]{1,0:T(8,128)(2,1)S(1)}, u32[]{:S(2)}) copy-start(bf16[128,1024]{1,0:T(8,128)(2,1)S(1)} %collective-permute-done.5.refs_6_) | copy-start | bytes 786436
  41.4 0.7 copy-start.13
  42.1 0.8 copy-start.2
  42.9 29.2 %all-to-all-start = ((s16[8,128,512]{2,1,0:T(8,128)(2,1)}), s16[8,128,512]{2,1,0:T(8,128)(2,1)}, u32[]{:S(2)}, u32[]{:S(2)}) async-start(s16[8,128,512]{2,1,0:T(8,128)(2,1)} %get-tuple-element.32), calls=%async_computation | async-start | bytes 2097152 | tf_op jit(solution)/shard_map/all_to_all | solution.py:401
  48.3 9.2 %collective-permute-start.13 = (bf16[256,2304]{1,0:T(8,128)(2,1)}, bf16[256,2304]{1,0:T(8,128)(2,1)}, u32[]{:S(2)}, u32[]{:S(2)}) collective-permute-start(bf16[256,2304]{1,0:T(8,128)(2,1)} %collective-permute-done.12.refs_10_), channel_id=1, source_target_pairs={{0,8},{8,0},{1,9},{9,1},{2,10},{10,2},{3,11},{11,3},{4,12},{12,4},... | collective-permute-start | bytes 3538952 | tf_op jit(solution)/shard_map/ppermute | solution.py:364
  48.3 8.8 %collective-permute-start.8 = (bf16[256,512]{1,0:T(8,128)(2,1)S(1)}, bf16[256,512]{1,0:T(8,128)(2,1)}, u32[]{:S(2)}, u32[]{:S(2)}) collective-permute-start(bf16[256,512]{1,0:T(8,128)(2,1)S(1)} %slice.25.refs_8_), channel_id=1, source_target_pairs={{0,16},{16,0},{1,17},{17,1},{2,18},{18,2},{3,19},{19,3},{4,20},{20... | collective-permute-start | bytes 786440 | tf_op jit(solution)/shard_map/ppermute | solution.py:361
  50.0 1.0 %copy-start.1 = (bf16[256,1024]{1,0:T(8,128)(2,1)S(1)}, bf16[256,1024]{1,0:T(8,128)(2,1)}, u32[]{:S(2)}) copy-start(bf16[256,1024]{1,0:T(8,128)(2,1)} %copy-done) | copy-start | bytes 1572868
  51.1 1.0 %copy-start.3 = (bf16[256,1024]{1,0:T(8,128)(2,1)S(1)}, bf16[256,1024]{1,0:T(8,128)(2,1)}, u32[]{:S(2)}) copy-start(bf16[256,1024]{1,0:T(8,128)(2,1)} %copy-done.2) | copy-start | bytes 1572868
  57.1 10.3 %collective-permute-start.11 = (bf16[256,512]{1,0:T(8,128)(2,1)}, bf16[256,512]{1,0:T(8,128)(2,1)S(1)}, u32[]{:S(2)}, u32[]{:S(2)}) collective-permute-start(bf16[256,512]{1,0:T(8,128)(2,1)} %collective-permute-done.8.refs_10_), channel_id=1, source_target_pairs={{0,8},{8,0},{1,9},{9,1},{2,10},{10,2},{3,11},{11,3},{4,12},{12,4},... | collective-permute-start | bytes 786440 | tf_op jit(solution)/shard_map/ppermute | solution.py:364
